TPU v7x, 32 devices: a whole 2x2x4 slice. The times are simulated.
32 devices in a mesh: cube: 4 (over x, core), blk: 8 (over z, y).
Axes of the slice: x: 2, y: 2, z: 4, core: 2. Of those that a mesh axis runs over, the one named last changes fastest.
Arguments:
- right_side: float32 [3, 4, 8, 32, 64], P(None, 'cube', 'blk'), may hold values from -6 to 6
- diag_inverse: float32 [896, 2048], P('cube', 'blk'), as said below
- panels: float32 [2, 4, 8, 2, 16, 32], P(None, 'cube', 'blk'), may hold values from -1 to 1
- extend_map: int32 [2, 4, 8, 2, 16], P(None, 'cube', 'blk'), may hold values from 0 to 31
Outputs:
- solution: float32 [3, 4, 8, 32, 64], P(None, 'cube', 'blk')
Inputs may be any that keep to these rules, and one draw needn't show every extreme that they name: `extend_map`: each entry names one of the 32 parent rows held by the receiving device. `diag_inverse`: dense real entries.
All inputs are finite; a program needn't handle non-finite values.
Results may differ from a plain program's by a relative error of at most 0.0001.
Values sent between devices are 32-bit elements; how exact they have to be, the bound alone decides.
No kernel may reach another device: no remote copies, remote signals or barrier semaphores. Data moves between devices by JAX's collectives and lax.ppermute only.
A program may use at most 64 MiB of HBM per device.

v0:
```python
import jax
import jax.numpy as jnp
from jax import lax
from jax.sharding import PartitionSpec as P


def from_partner(block, axis, apart):
    count = lax.axis_size(axis)
    route = []
    for low in range(count):
        high = low | 1 << apart
        if high != low and high < count:
            route += [(low, high), (high, low)]
    return lax.ppermute(block, axis, route)


def collect_pairs(residual_rows, tree_level, cube_index):
    gathered = residual_rows
    for bit_index in range(tree_level):
        partner_rows = from_partner(gathered, "cube", bit_index)
        lower_side = cube_index // 2**bit_index % 2 == 0
        gathered = jnp.where(
            lower_side,
            jnp.concatenate([gathered, partner_rows], axis=0),
            jnp.concatenate([partner_rows, gathered], axis=0),
        )
    return gathered


def reduce_pairs(partial_value, tree_level, cube_index):
    for bit_index in reversed(range(tree_level)):
        half_rows = partial_value.shape[0] // 2
        lower_rows = partial_value[:half_rows]
        upper_rows = partial_value[half_rows:]
        lower_side = cube_index // 2**bit_index % 2 == 0
        kept_rows = jnp.where(lower_side, lower_rows, upper_rows)
        sent_rows = jnp.where(lower_side, upper_rows, lower_rows)
        partial_value = kept_rows + from_partner(sent_rows, "cube", bit_index)
    return partial_value


def body(right_side, diag_inverse, panels, extend_map):
    highest = lax.Precision.HIGHEST
    levels = right_side.shape[0]
    local_rows = right_side.shape[3]
    columns_k = right_side.shape[4]
    cube_index = lax.axis_index("cube")
    rhs_rows = right_side[:, 0, 0]
    panel_blocks = panels[:, 0, 0]
    row_maps = extend_map[:, 0, 0]
    row_ids = jnp.arange(local_rows, dtype=jnp.int32)
    update = jnp.zeros((local_rows, columns_k), jnp.float32)
    solved = []
    onehots = []
    diag_blocks = []
    for tree_level in range(levels):
        span_rows = 2**tree_level * local_rows
        offset = (2**tree_level - 1) * local_rows
        diag_block = diag_inverse[offset : offset + span_rows]
        diag_blocks.append(diag_block)
        residual_rows = rhs_rows[tree_level] - update
        column = collect_pairs(residual_rows, tree_level, cube_index)

        def term_rows(first_row, row_count, diag_block=diag_block, column=column):
            return jnp.einsum("ir,ik->rk", diag_block, column, precision=highest)

        solved_rows = lax.psum_scatter(
            term_rows(jnp.int32(0), lax.axis_size("blk") * local_rows),
            "blk",
            scatter_dimension=0,
            tiled=True,
        )
        solved.append(solved_rows)
        if tree_level + 1 < levels:
            onehot = (row_maps[tree_level][..., None] == row_ids).astype(jnp.float32)
            onehots.append(onehot)
            upd_rows = jnp.einsum(
                "hmr,rk->hmk", panel_blocks[tree_level], solved_rows, precision=highest
            )
            extended = jnp.einsum("hmt,hmk->htk", onehot, upd_rows, precision=highest)
            update = extended[0] + from_partner(extended[1], "cube", tree_level)
    results = [None] * levels
    parent = None
    for tree_level in reversed(range(levels)):
        span_rows = 2**tree_level * local_rows
        diag_block = diag_blocks[tree_level]
        work_rows = solved[tree_level]
        if parent is not None:
            partner_rows = from_partner(parent, "cube", tree_level)
            parent_pair = jnp.stack([parent, partner_rows], axis=0)
            fetched = jnp.einsum(
                "hmt,htk->hmk", onehots[tree_level], parent_pair, precision=highest
            )
            work_rows = work_rows - jnp.einsum(
                "hmr,hmk->rk", panel_blocks[tree_level], fetched, precision=highest
            )

        def accumulate(running, shard_rows, first_row, diag_block=diag_block):
            return jnp.einsum("ir,rk->ik", diag_block, shard_rows, precision=highest)

        initial = jnp.zeros((span_rows, columns_k), jnp.float32)
        partial_value = accumulate(
            initial, lax.all_gather(work_rows, "blk", axis=0, tiled=True), jnp.int32(0)
        )
        parent = reduce_pairs(partial_value, tree_level, cube_index)
        results[tree_level] = parent
    return jnp.stack(results)[:, None, None]


def solution(mesh):
    placed = (
        P(None, "cube", "blk", None, None),
        P("cube", "blk"),
        P(None, "cube", "blk", None, None, None),
        P(None, "cube", "blk", None, None),
    )
    return jax.shard_map(
        body,
        mesh=mesh,
        in_specs=placed,
        out_specs=P(None, "cube", "blk", None, None),
        check_vma=False,
    )
```

profile of v0, /device:TPU:0, one launch (start us, length us, event | category | flops | bytes accessed | tf_op | source)
XLA Modules:
  0.0 323.9 jit_solution(135299196685777458)
XLA Ops:
  6.5 1.8 fusion.26
  8.5 65.8 %reduce-scatter.8.cloned.1.call-done = f32[32,64]{1,0:T(8,128)} async-done(((f32[256,64]{1,0:T(8,128)}), f32[32,64]{1,0:T(8,128)}) %reduce-scatter.8.cloned.1.call-update) | async-done | bytes 8208 | tf_op jit(solution)/shard_map/reduce_scatter | solution.py:67
  74.2 0.8 convolution_bitcast_fusion.8
  75.5 1.2 collective-permute-done
  76.9 1.0 collective-permute-done.1
  78.2 0.8 copy.15
  79.0 60.0 %reduce-scatter.10.cloned.1.call-done = f32[32,64]{1,0:T(8,128)} async-done(((f32[256,64]{1,0:T(8,128)}), f32[32,64]{1,0:T(8,128)}) %reduce-scatter.10.cloned.1.call-update) | async-done | bytes 8208
  139.0 0.8 convolution_bitcast_fusion.7
  140.1 1.5 collective-permute-start.2
  141.7 2.3 collective-permute-done.2
  144.0 1.2 collective-permute-done.3
  145.1 1.5 collective-permute-start.4
  146.6 2.4 collective-permute-done.4
  150.1 60.0 %reduce-scatter.12.cloned.1.call-done = f32[32,64]{1,0:T(8,128)} async-done(((f32[256,64]{1,0:T(8,128)}), f32[32,64]{1,0:T(8,128)}) %reduce-scatter.12.cloned.1.call-update) | async-done | bytes 8208 | tf_op jit(solution)/shard_map/reduce_scatter | solution.py:67
  210.2 30.8 %all_gather.9 = f32[256,64]{1,0:T(8,128)S(1)} all-gather(f32[32,64]{1,0:T(8,128)} %reduce-scatter.12.cloned.1.call-done), channel_id=1, replica_groups=mesh['cube'=4,'blk'=8] {'blk'}, dimensions={0}, use_global_device_ids=true | all-gather | bytes 73728 | tf_op jit(solution)/shard_map/all_gather | solution.py:103
  241.4 1.5 collective-permute-start.5
  242.9 2.4 collective-permute-done.5
  245.5 1.2 collective-permute-done.6
  246.8 1.5 collective-permute-start.7
  248.4 2.3 collective-permute-done.7
  251.3 30.5 %all_gather.10 = f32[256,64]{1,0:T(8,128)S(1)} all-gather(f32[32,64]{1,0:T(8,128)S(1)} %copy.9), channel_id=1, replica_groups=mesh['cube'=4,'blk'=8] {'blk'}, dimensions={0}, use_global_device_ids=true | all-gather | bytes 73728 | tf_op jit(solution)/shard_map/all_gather | solution.py:103
  282.3 1.2 collective-permute-done.8
  283.7 1.0 collective-permute-done.9
  285.7 30.6 %all_gather.11 = f32[256,64]{1,0:T(8,128)S(1)} all-gather(f32[32,64]{1,0:T(8,128)S(1)} %fusion.1), channel_id=1, replica_groups=mesh['cube'=4,'blk'=8] {'blk'}, dimensions={0}, use_global_device_ids=true | all-gather | bytes 73728 | tf_op jit(solution)/shard_map/all_gather | solution.py:103
  (52 shorter events, 6.4 us)
Async XLA Ops:
  6.5 67.7 %reduce-scatter.8.cloned.1.call-start = ((), (), s32[]{:S(2)}) async-start(), calls=%async_computation.3 | async-start | bytes 147456 | tf_op jit(solution)/shard_map/reduce_scatter | solution.py:67
  6.5 1.9 copy-start.5
  6.5 67.7 %copy-start.1 = (f32[2,1,1,2,16,32]{5,4,3,2,1,0:T(8,128)S(1)}, f32[2,1,1,2,16,32]{5,4,3,2,1,0:T(8,128)}, u32[]{:S(2)}) copy-start(f32[2,1,1,2,16,32]{5,4,3,2,1,0:T(8,128)} %param.6) | copy-start | bytes 24580
  8.4 69.6 %copy-start = (f32[224,256]{1,0:T(8,128)S(1)}, f32[224,256]{1,0:T(8,128)}, u32[]{:S(2)}) copy-start(f32[224,256]{1,0:T(8,128)} %param.5) | copy-start | bytes 688132
  8.4 130.6 %reduce-scatter.10.cloned.1.call-start = ((), (), s32[]{:S(2)}) async-start(), calls=%async_computation.4 | async-start | bytes 147456
  75.1 1.6 copy-start.4
  75.4 1.2 collective-permute-start
  76.7 1.2 collective-permute-start.1
  79.0 131.2 %reduce-scatter.12.cloned.1.call-start = ((), (), s32[]{:S(2)}) async-start(), calls=%async_computation.5 | async-start | bytes 147456 | tf_op jit(solution)/shard_map/reduce_scatter | solution.py:67
  140.1 3.8 %collective-permute-start.2 = (f32[32,64]{1,0:T(8,128)S(1)}, f32[32,64]{1,0:T(8,128)S(1)}, u32[]{:S(2)}, u32[]{:S(2)}) collective-permute-start(f32[32,64]{1,0:T(8,128)S(1)} %slice_bitcast_fusion), channel_id=1, source_target_pairs={{0,16},{16,0},{8,24},{24,8},{1,17},{17,1},{9,25},{25,9},{2,18},{18... | collective-permute-start | bytes 24584 | tf_op jit(solution)/shard_map/ppermute | solution.py:14
  144.0 1.2 collective-permute-start.3
  145.1 3.9 %collective-permute-start.4 = (f32[64,64]{1,0:T(8,128)S(1)}, f32[64,64]{1,0:T(8,128)S(1)}, u32[]{:S(2)}, u32[]{:S(2)}) collective-permute-start(f32[64,64]{1,0:T(8,128)S(1)} %maximum_select_fusion.4), channel_id=1, source_target_pairs={{0,16},{16,0},{8,24},{24,8},{1,17},{17,1},{9,25},{25,9},{2,18},{18... | collective-permute-start | bytes 49160 | tf_op jit(solution)/shard_map/ppermute | solution.py:14
  241.4 3.9 %collective-permute-start.5 = (f32[64,64]{0,1:T(8,128)S(1)}, f32[64,64]{0,1:T(8,128)S(1)}, u32[]{:S(2)}, u32[]{:S(2)}) collective-permute-start(f32[64,64]{0,1:T(8,128)S(1)} %slice_select_fusion.2), channel_id=1, source_target_pairs={{0,16},{16,0},{8,24},{24,8},{1,17},{17,1},{9,25},{25,9},{2,18},{18... | collective-permute-start | bytes 49160 | tf_op jit(solution)/shard_map/ppermute | solution.py:14
  245.5 2.8 copy-start.2
  245.5 1.3 collective-permute-start.6
  246.8 3.9 %collective-permute-start.7 = (f32[32,64]{0,1:T(8,128)S(1)}, f32[32,64]{0,1:T(8,128)S(1)}, u32[]{:S(2)}, u32[]{:S(2)}) collective-permute-start(f32[32,64]{0,1:T(8,128)S(1)} %select_add_fusion.1), channel_id=1, source_target_pairs={{0,16},{16,0},{8,24},{24,8},{1,17},{17,1},{9,25},{25,9},{2,18},{18... | collective-permute-start | bytes 24584 | tf_op jit(solution)/shard_map/ppermute | solution.py:14
  282.2 1.2 collective-permute-start.8
  283.5 1.2 collective-permute-start.9
  284.8 0.7 copy-start.3
Sparse Core Ops, SparseCore 0:
  10.7 63.5 reduce-scatter.7
  79.1 59.8 reduce-scatter.9
  150.2 59.8 reduce-scatter.11
where the time goes:
time: 324 us
  waiting for transfers between devices  202 us (62%)
  blocking collectives  91.9 us (28%)
  between operations  13.3 us (4%)
  starting transfers between devices  6.67 us (2%)
  matrix products  6.6 us (2%)
    reduce_scatter x2, waiting for transfers between devices, body(): lax.psum_scatter(term_rows(jnp.int32(0), lax.axis_size('blk') * local_row...  126 us
    all_gather x3, blocking collectives, body(): lax.all_gather(work_rows, 'blk', axis=0, tiled=True)  91.9 us
    unnamed x4, waiting for transfers between devices  60 us
    ppermute x10, waiting for transfers between devices, from_partner(): return lax.ppermute(block, axis, route)  16.2 us
    ppermute x10, starting transfers between devices, from_partner(): return lax.ppermute(block, axis, route)  6.58 us
  transfers between devices with their start and end apart: 13, of which 13 were waited for; matrix products, arithmetic and copies ran while one was open for 0% of the time, Pallas kernels for 0%

commit v1 on v0

--- a/solution.py
+++ b/solution.py
@@ -2,6 +2,121 @@
 import jax.numpy as jnp
 from jax import lax
 from jax.sharding import PartitionSpec as P
+
+HIGHEST = lax.Precision.HIGHEST
+GATHER_BYTES = 8 * 2**20
+
+
+def swap(block, axis, mask):
+    count = lax.axis_size(axis)
+    return lax.ppermute(block, axis, [(i, i ^ mask) for i in range(count)])
+
+
+def gather_rows(block):
+    count = lax.axis_size("blk")
+    if count == 1:
+        return [block]
+    half = count // 2
+    far = swap(block, "blk", half)
+    near = {m: swap(block, "blk", m) for m in reversed(range(1, half))}
+    out = {0: block, half: far}
+    for m in reversed(range(1, half)):
+        out[m] = near[m]
+        out[m + half] = swap(far, "blk", m)
+    return [out[m] for m in range(count)]
+
+
+def by_bits(parts, index):
+    bit = 1
+    while bit < len(parts):
+        side = (index // bit) % 2 == 1
+        parts = [jnp.where(side, parts[j ^ bit], parts[j]) for j in range(len(parts))]
+        bit *= 2
+    return parts
+
+
+def gathered(right_side, diag_inverse, panels, extend_map):
+    levels, _, _, rows, cols = right_side.shape
+    width = diag_inverse.shape[1]
+    n_blk = lax.axis_size("blk")
+    cube = lax.axis_index("cube")
+    me = lax.axis_index("blk")
+    row_ids = jnp.arange(rows, dtype=jnp.int32)
+    onehot = (extend_map[:, 0, 0][..., None] == row_ids).astype(jnp.float32)
+    extend = jnp.einsum("lhmt,lhmr->tlhr", onehot, panels[:, 0, 0], precision=HIGHEST)
+    vectors = jnp.transpose(right_side[:, 0, 0], (1, 0, 2)).reshape(rows, levels * cols)
+    packed = jnp.concatenate([vectors, extend.reshape(rows, -1)], axis=1)
+    pad = -packed.size % width
+    packed = jnp.pad(packed.reshape(-1), (0, pad)).reshape(-1, width)
+    top = (2 ** (levels - 1) - 1) * rows
+    first = gather_rows(jnp.concatenate([diag_inverse[:top], packed], axis=0))
+    last = gather_rows(diag_inverse[top:])
+
+    small = jnp.stack([f[top:] for f in first]).reshape(n_blk, -1)[:, : small_size(rows, levels, cols)]
+    small = small.reshape(n_blk, rows, -1)
+    rhs = [
+        small[:, :, l * cols : (l + 1) * cols].reshape(n_blk * rows, cols) for l in range(levels)
+    ]
+    ext = small[:, :, levels * cols :].reshape(n_blk, rows, levels - 1, 2, rows)
+    ext = jnp.transpose(ext, (2, 3, 0, 1, 4))
+    same = (jnp.arange(n_blk) ^ me)[:, None] == jnp.arange(n_blk)[None, :]
+    ext = jnp.where(
+        same[None, None, :, None, :, None], ext[:, :, :, :, None, :], 0.0
+    ).reshape(levels - 1, 2 * n_blk * rows, n_blk * rows)
+
+    def diag_of(l):
+        span = 2**l
+        if l == levels - 1:
+            pieces = [p.reshape(span, 1, rows, width) for p in last]
+        else:
+            low = (span - 1) * rows
+            pieces = [p[low : low + span * rows].reshape(span, 1, rows, width) for p in first]
+        return jnp.concatenate(pieces, axis=1).reshape(span * n_blk * rows, width)
+
+    node = n_blk * rows
+    diags = [diag_of(l) for l in range(levels)]
+    z = rhs[0]
+    ys = []
+    for l in range(levels):
+        y = jnp.einsum("ab,ak->bk", diags[l], z, precision=HIGHEST)
+        ys.append(y)
+        if l + 1 < levels:
+            e = jnp.einsum("ab,bk->ak", ext[l], y, precision=HIGHEST)
+            mine = rhs[l + 1] - e[:node]
+            other = e[node:]
+            got = swap(jnp.concatenate([mine, other], axis=0), "cube", 2**l)
+            parts = {0: mine - got[node:], 2**l: got[:node] - other}
+            for j in reversed(range(l)):
+                keys = list(parts)
+                got = swap(jnp.concatenate([parts[k] for k in keys], axis=0), "cube", 2**j)
+                for i, k in enumerate(keys):
+                    parts[k ^ 2**j] = got[i * node : (i + 1) * node]
+            order = by_bits([parts[k] for k in range(2 ** (l + 1))], cube)
+            z = jnp.concatenate(order, axis=0)
+    outs = [None] * levels
+    w = ys[-1]
+    for l in reversed(range(levels)):
+        if l == 0:
+            own = diags[0][:rows]
+            outs[0] = jnp.einsum("ab,bk->ak", own, w, precision=HIGHEST)
+            break
+        x = jnp.einsum("ab,bk->ak", diags[l], w, precision=HIGHEST)
+        order = by_bits([x[p * node : (p + 1) * node] for p in range(2**l)], cube)
+        held = {k: order[k] for k in range(2**l)}
+        for j in range(l - 1):
+            keep = [k for k in held if not k & 2**j]
+            got = swap(jnp.concatenate([held[k ^ 2**j] for k in keep], axis=0), "cube", 2**j)
+            held = {k: held[k] + got[i * node : (i + 1) * node] for i, k in enumerate(keep)}
+        bit = 2 ** (l - 1)
+        got = swap(jnp.concatenate([held[bit], held[0]], axis=0), "cube", bit)
+        pair = jnp.concatenate([held[0], held[bit]], axis=0) + got
+        outs[l] = pair[:rows]
+        w = ys[l - 1] - jnp.einsum("ab,ak->bk", ext[l - 1], pair, precision=HIGHEST)
+    return jnp.stack(outs)[:, None, None]
+
+
+def small_size(rows, levels, cols):
+    return rows * (levels * cols + (levels - 1) * 2 * rows)
 
 
 def from_partner(block, axis, apart):
@@ -39,7 +154,7 @@
     return partial_value
 
 
-def body(right_side, diag_inverse, panels, extend_map):
+def stepwise(right_side, diag_inverse, panels, extend_map):
     highest = lax.Precision.HIGHEST
     levels = right_side.shape[0]
     local_rows = right_side.shape[3]
@@ -107,6 +222,12 @@
     return jnp.stack(results)[:, None, None]
 
 
+def body(right_side, diag_inverse, panels, extend_map):
+    if lax.axis_size("blk") * diag_inverse.size * 4 > GATHER_BYTES:
+        return stepwise(right_side, diag_inverse, panels, extend_map)
+    return gathered(right_side, diag_inverse, panels, extend_map)
+
+
 def solution(mesh):
     placed = (
         P(None, "cube", "blk", None, None),

time: 324 us -> 89.8 us (0.28)
  waiting for transfers between devices: 202 us -> 24.4 us
  blocking collectives: 91.9 us -> 0 us
  local copies, waits for them, and re-layouts: 2.9 us -> 26.1 us
  starting transfers between devices: 6.67 us -> 22.6 us
  between operations: 13.3 us -> 0.59 us
  matrix products: 6.6 us -> 12.6 us
    reduce_scatter x2 -> x0, waiting for transfers between devices: 126 us -> none  [body(): lax.psum_scatter(term_rows(jnp.int32(0), lax.axis_size('blk') * local_row...]
    all_gather x3 -> x0, blocking collectives: 91.9 us -> none  [body(): lax.all_gather(work_rows, 'blk', axis=0, tiled=True)]
    unnamed x4 -> x0, waiting for transfers between devices: 60 us -> none
    ppermute x10 -> x20, starting transfers between devices: 6.58 us -> 22.6 us  [swap(): return lax.ppermute(block, axis, [(i, i ^ mask) for i in range(count)])]
    ppermute x10 -> x20, waiting for transfers between devices: 16.2 us -> 24.4 us  [swap(): return lax.ppermute(block, axis, [(i, i ^ mask) for i in range(count)])]
    slice x0 -> x20, local copies, waits for them, and re-layouts: none -> 7.76 us  [the longest x8 3.4 us: diag_of(): p[low:low + span * rows].reshape(span, 1, rows, width)]
    dot_general x14 -> x11, matrix products: 6.6 us -> 12.6 us  [the longest x3 4.59 us: gathered(): y = jnp.einsum('ab,ak->bk', diags[l], z, precision=HIGHEST)]
    unnamed x15 -> x45, local copies, waits for them, and re-layouts: 2.12 us -> 8.09 us
  transfers between devices with their start and end apart: 13 -> 20, of which waited for: 13 -> 13; matrix products, arithmetic and copies ran while one was open for 0% -> 34% of each run, Pallas kernels for 0% -> 0%
where the time goes in v1:
time: 89.8 us; the launch traced here: 88.7 us
  local copies, waits for them, and re-layouts  26.1 us (29%)
  waiting for transfers between devices  24.4 us (27%)
  starting transfers between devices  22.6 us (25%)
  matrix products  12.6 us (14%)
  other arithmetic  2.54 us (3%)
    ppermute x20, waiting for transfers between devices, swap(): return lax.ppermute(block, axis, [(i, i ^ mask) for i in range(count)])  24.4 us
    ppermute x20, starting transfers between devices, swap(): return lax.ppermute(block, axis, [(i, i ^ mask) for i in range(count)])  22.6 us
    unnamed x45, local copies, waits for them, and re-layouts  8.09 us
    dot_general x3, matrix products, gathered(): y = jnp.einsum('ab,ak->bk', diags[l], z, precision=HIGHEST)  4.59 us
    squeeze x2, local copies, waits for them, and re-layouts, gathered(): w = ys[l - 1] - jnp.einsum('ab,ak->bk', ext[l - 1], pair, precision=HIGHEST)  4.15 us
    dot_general x2, matrix products, gathered(): e = jnp.einsum('ab,bk->ak', ext[l], y, precision=HIGHEST)  3.42 us
    slice x8, local copies, waits for them, and re-layouts, diag_of(): p[low:low + span * rows].reshape(span, 1, rows, width)  3.4 us
    concatenate x3, local copies, waits for them, and re-layouts, diag_of(): return jnp.concatenate(pieces, axis=1).reshape(span * n_blk * rows, width)  2.02 us
  transfers between devices with their start and end apart: 20, of which 13 were waited for; matrix products, arithmetic and copies ran while one was open for 34% of the time, Pallas kernels for 0%

profile of v1, /device:TPU:0, one launch (start us, length us, event | category | flops | bytes accessed | tf_op | source)
XLA Modules:
  0.0 88.7 jit_solution(11028649972490244376)
XLA Ops:
  3.9 3.0 %collective-permute-start = (f32[136,256]{1,0:T(8,128)S(1)}, f32[136,256]{1,0:T(8,128)S(1)}, u32[]{:S(2)}, u32[]{:S(2)}) collective-permute-start(f32[136,256]{1,0:T(8,128)S(1)} %pad_maximum_fusion), channel_id=1, source_target_pairs={{0,1},{1,0},{2,3},{3,2},{4,5},{5,4},{6,7},{7,6},{8,9},{9,8},{10,11... | collective-permute-start | bytes 417800 | tf_op jit(solution)/shard_map/ppermute | solution.py:12
  7.0 1.6 %collective-permute-start.1 = (f32[136,256]{1,0:T(8,128)S(1)}, f32[136,256]{1,0:T(8,128)S(1)}, u32[]{:S(2)}, u32[]{:S(2)}) collective-permute-start(f32[136,256]{1,0:T(8,128)S(1)} %pad_maximum_fusion), channel_id=1, source_target_pairs={{0,2},{1,3},{2,0},{3,1},{4,6},{5,7},{6,4},{7,5},{8,10},{9,11},{10,... | collective-permute-start | bytes 417800 | tf_op jit(solution)/shard_map/ppermute | solution.py:12
  10.1 3.0 %collective-permute-start.10 = (f32[128,256]{1,0:T(8,128)S(1)}, f32[128,256]{1,0:T(8,128)S(1)}, u32[]{:S(2)}, u32[]{:S(2)}) collective-permute-start(f32[128,256]{1,0:T(8,128)S(1)} %slice.194), channel_id=1, source_target_pairs={{0,3},{1,2},{2,1},{3,0},{4,7},{5,6},{6,5},{7,4},{8,11},{9,10},{10,... | collective-permute-start | bytes 393224 | tf_op jit(solution)/shard_map/ppermute | solution.py:12
  15.6 2.6 %collective-permute-start.11 = (f32[128,256]{1,0:T(8,128)S(1)}, f32[128,256]{1,0:T(8,128)}, u32[]{:S(2)}, u32[]{:S(2)}) collective-permute-start(f32[128,256]{1,0:T(8,128)S(1)} %slice.194), channel_id=1, source_target_pairs={{0,4},{1,5},{2,6},{3,7},{4,0},{5,1},{6,2},{7,3},{8,12},{9,13},{10,... | collective-permute-start | bytes 393224 | tf_op jit(solution)/shard_map/ppermute | solution.py:12
  20.4 3.4 %collective-permute-start.3 = (f32[136,256]{1,0:T(8,128)S(1)}, f32[136,256]{1,0:T(8,128)S(1)}, u32[]{:S(2)}, u32[]{:S(2)}) collective-permute-start(f32[136,256]{1,0:T(8,128)S(1)} %pad_maximum_fusion), channel_id=1, source_target_pairs={{0,4},{1,5},{2,6},{3,7},{4,0},{5,1},{6,2},{7,3},{8,12},{9,13},{10,... | collective-permute-start | bytes 417800 | tf_op jit(solution)/shard_map/ppermute | solution.py:12
  25.9 3.4 %collective-permute-done.3 = f32[136,256]{1,0:T(8,128)S(1)} collective-permute-done((f32[136,256]{1,0:T(8,128)S(1)}, f32[136,256]{1,0:T(8,128)S(1)}, u32[]{:S(2)}, u32[]{:S(2)}) %collective-permute-start.3) | collective-permute-done | bytes 139296 | tf_op jit(solution)/shard_map/ppermute | solution.py:12
  29.6 1.5 %collective-permute-start.5 = (f32[136,256]{1,0:T(8,128)S(1)}, f32[136,256]{1,0:T(8,128)S(1)}, u32[]{:S(2)}, u32[]{:S(2)}) collective-permute-start(f32[136,256]{1,0:T(8,128)S(1)} %collective-permute-done.3), channel_id=1, source_target_pairs={{0,2},{1,3},{2,0},{3,1},{4,6},{5,7},{6,4},{7,5},{8,10},{9,11},{10,... | collective-permute-start | bytes 417800 | tf_op jit(solution)/shard_map/ppermute | solution.py:12
  31.1 2.0 %collective-permute-start.6 = (f32[136,256]{1,0:T(8,128)S(1)}, f32[136,256]{1,0:T(8,128)S(1)}, u32[]{:S(2)}, u32[]{:S(2)}) collective-permute-start(f32[136,256]{1,0:T(8,128)S(1)} %collective-permute-done.3), channel_id=1, source_target_pairs={{0,3},{1,2},{2,1},{3,0},{4,7},{5,6},{6,5},{7,4},{8,11},{9,10},{10,... | collective-permute-start | bytes 417800 | tf_op jit(solution)/shard_map/ppermute | solution.py:12
  33.2 1.6 %collective-permute-done.4 = f32[136,256]{1,0:T(8,128)S(1)} collective-permute-done((f32[136,256]{1,0:T(8,128)S(1)}, f32[136,256]{1,0:T(8,128)S(1)}, u32[]{:S(2)}, u32[]{:S(2)}) %collective-permute-start.4) | collective-permute-done | bytes 139296 | tf_op jit(solution)/shard_map/ppermute | solution.py:12
  35.5 2.1 %collective-permute-done.6 = f32[136,256]{1,0:T(8,128)S(1)} collective-permute-done((f32[136,256]{1,0:T(8,128)S(1)}, f32[136,256]{1,0:T(8,128)S(1)}, u32[]{:S(2)}, u32[]{:S(2)}) %collective-permute-start.6) | collective-permute-done | bytes 139296 | tf_op jit(solution)/shard_map/ppermute | solution.py:12
  39.6 1.7 %fusion.17 = (f32[1,2,8,32,8,32]{5,4,3,2,1,0:T(8,128)}, f32[1,2,8,32,8,32]{5,4,3,2,1,0:T(8,128)S(1)}) fusion(f32[2,2,8,32,8,32]{5,4,3,2,1,0:T(8,128)S(1)} %broadcast_select_fusion), kind=kLoop, calls=%fused_computation.103 | loop fusion | bytes 2097152 | tf_op jit(solution)/shard_map/slice | solution.py:114
  41.4 2.8 %squeeze.16 = f32[512,256]{1,0:T(8,128)} reshape(f32[1,2,8,32,8,32]{5,4,3,2,1,0:T(8,128)} %get-tuple-element.5) | data formatting | bytes 1048576 | tf_op jit(solution)/shard_map/squeeze | solution.py:114
  44.2 1.4 %constant_dynamic-update-slice_fusion.2 = f32[1,8,32,256]{3,2,1,0:T(8,128)} fusion(f32[1,8,32,256]{3,2,1,0:T(8,128)} %copy-done.5, f32[136,256]{1,0:T(8,128)} %copy-done.8), kind=kLoop, calls=%fused_computation.29 | loop fusion | bytes 65536
  45.6 1.4 %constant_dynamic-update-slice_fusion.1 = f32[1,8,32,256]{3,2,1,0:T(8,128)} fusion(f32[1,8,32,256]{3,2,1,0:T(8,128)} %constant_dynamic-update-slice_fusion.2, f32[136,256]{1,0:T(8,128)} %copy-done.7), kind=kLoop, calls=%fused_computation.28 | loop fusion | bytes 65536
  49.6 1.7 %fusion.20 = f32[512,64]{0,1:T(8,128)S(1)} fusion(f32[512,256]{1,0:T(8,128)} %squeeze.16, f32[256,64]{0,1:T(8,128)S(1)} %fusion.19), kind=kOutput, calls=%fused_computation.106 | convolution fusion | flops 100663296 | bytes 720896 | tf_op jit(solution)/shard_map/ab,bk->ak/dot_general | solution.py:84
  55.0 1.4 %squeeze.17 = f32[512,256]{1,0:T(8,128)} reshape(f32[1,2,8,32,8,32]{5,4,3,2,1,0:T(8,128)S(1)} %get-tuple-element.6) | data formatting | bytes 1048576 | tf_op jit(solution)/shard_map/squeeze | solution.py:114
  59.7 1.5 %fusion.8 = f32[256,64]{0,1:T(8,128)S(1)} fusion(f32[512,256]{1,0:T(8,128)} %bitcast.97, f32[256,64]{0,1:T(8,128)S(1)} %get-tuple-element.13, f32[256,64]{0,1:T(8,128)S(1)} %get-tuple-element.12), kind=kOutput, calls=%fused_computation.15 | convolution fusion | flops 100696064 | bytes 720896 | tf_op jit(solution)/shard_map/ab,ak->bk/dot_general | solution.py:81
  61.2 1.7 %fusion.21 = f32[512,64]{0,1:T(8,128)S(1)} fusion(f32[512,256]{1,0:T(8,128)} %squeeze.17, f32[256,64]{0,1:T(8,128)S(1)} %fusion.8), kind=kOutput, calls=%fused_computation.107 | convolution fusion | flops 100663296 | bytes 720896 | tf_op jit(solution)/shard_map/ab,bk->ak/dot_general | solution.py:84
  63.0 1.6 %collective-permute-start.15 = (f32[512,64]{0,1:T(8,128)S(1)}, f32[512,64]{0,1:T(8,128)S(1)}, u32[]{:S(2)}, u32[]{:S(2)}) collective-permute-start(f32[512,64]{0,1:T(8,128)S(1)} %pad_maximum_fusion.2), channel_id=1, source_target_pairs={{0,16},{8,24},{16,0},{24,8},{1,17},{9,25},{17,1},{25,9},{2,18},{10... | collective-permute-start | bytes 393224 | tf_op jit(solution)/shard_map/ppermute | solution.py:12
  65.6 1.5 %collective-permute-start.14 = (f32[128,256]{1,0:T(8,128)}, f32[128,256]{1,0:T(8,128)S(1)}, u32[]{:S(2)}, u32[]{:S(2)}) collective-permute-start(f32[128,256]{1,0:T(8,128)} %collective-permute-done.11), channel_id=1, source_target_pairs={{0,3},{1,2},{2,1},{3,0},{4,7},{5,6},{6,5},{7,4},{8,11},{9,10},{10,... | collective-permute-start | bytes 393224 | tf_op jit(solution)/shard_map/ppermute | solution.py:12
  69.1 3.0 %collective-permute-done.13 = f32[128,256]{1,0:T(8,128)S(1)} collective-permute-done((f32[128,256]{1,0:T(8,128)}, f32[128,256]{1,0:T(8,128)S(1)}, u32[]{:S(2)}, u32[]{:S(2)}) %collective-permute-start.13) | collective-permute-done | bytes 131104 | tf_op jit(solution)/shard_map/ppermute | solution.py:12
  72.1 1.8 %collective-permute-done.14 = f32[128,256]{1,0:T(8,128)S(1)} collective-permute-done((f32[128,256]{1,0:T(8,128)}, f32[128,256]{1,0:T(8,128)S(1)}, u32[]{:S(2)}, u32[]{:S(2)}) %collective-permute-start.14) | collective-permute-done | bytes 131104 | tf_op jit(solution)/shard_map/ppermute | solution.py:12
  73.9 1.8 %fusion = f32[256,64]{1,0:T(8,128)S(1)} fusion(f32[1024,256]{1,0:T(8,128)S(1)} %bitcast.95, f32[256,64]{0,1:T(8,128)S(1)} %get-tuple-element.19, f32[256,64]{0,1:T(8,128)S(1)} %get-tuple-element.18, f32[256,64]{0,1:T(8,128)S(1)} %get-tuple-element.17, f32[256,64]{0,1:T(8,128)S(1)} %get-tuple-element.16), kind=kOutput, calls=%fused_computation.5 | convolution fusion | flops 201523200 | bytes 1376256 | tf_op jit(solution)/shard_map/ab,ak->bk/dot_general | solution.py:81
  79.0 5.0 %collective-permute-done.18 = f32[512,64]{0,1:T(8,128)S(1)} collective-permute-done((f32[512,64]{0,1:T(8,128)S(1)}, f32[512,64]{0,1:T(8,128)S(1)}, u32[]{:S(2)}, u32[]{:S(2)}) %collective-permute-start.18) | collective-permute-done | bytes 131104 | tf_op jit(solution)/shard_map/ppermute | solution.py:12
  (140 shorter events, 35.8 us)
Async XLA Ops:
  3.9 21.0 %collective-permute-start = (f32[136,256]{1,0:T(8,128)S(1)}, f32[136,256]{1,0:T(8,128)S(1)}, u32[]{:S(2)}, u32[]{:S(2)}) collective-permute-start(f32[136,256]{1,0:T(8,128)S(1)} %pad_maximum_fusion), channel_id=1, source_target_pairs={{0,1},{1,0},{2,3},{3,2},{4,5},{5,4},{6,7},{7,6},{8,9},{9,8},{10,11... | collective-permute-start | bytes 417800 | tf_op jit(solution)/shard_map/ppermute | solution.py:12
  7.0 18.1 %collective-permute-start.1 = (f32[136,256]{1,0:T(8,128)S(1)}, f32[136,256]{1,0:T(8,128)S(1)}, u32[]{:S(2)}, u32[]{:S(2)}) collective-permute-start(f32[136,256]{1,0:T(8,128)S(1)} %pad_maximum_fusion), channel_id=1, source_target_pairs={{0,2},{1,3},{2,0},{3,1},{4,6},{5,7},{6,4},{7,5},{8,10},{9,11},{10,... | collective-permute-start | bytes 417800 | tf_op jit(solution)/shard_map/ppermute | solution.py:12
  9.5 6.2 %collective-permute-start.8 = (f32[128,256]{1,0:T(8,128)S(1)}, f32[128,256]{1,0:T(8,128)S(1)}, u32[]{:S(2)}, u32[]{:S(2)}) collective-permute-start(f32[128,256]{1,0:T(8,128)S(1)} %slice.194), channel_id=1, source_target_pairs={{0,1},{1,0},{2,3},{3,2},{4,5},{5,4},{6,7},{7,6},{8,9},{9,8},{10,11... | collective-permute-start | bytes 393224 | tf_op jit(solution)/shard_map/ppermute | solution.py:12
  10.0 8.2 %collective-permute-start.9 = (f32[128,256]{1,0:T(8,128)S(1)}, f32[128,256]{1,0:T(8,128)S(1)}, u32[]{:S(2)}, u32[]{:S(2)}) collective-permute-start(f32[128,256]{1,0:T(8,128)S(1)} %slice.194), channel_id=1, source_target_pairs={{0,2},{1,3},{2,0},{3,1},{4,6},{5,7},{6,4},{7,5},{8,10},{9,11},{10,... | collective-permute-start | bytes 393224 | tf_op jit(solution)/shard_map/ppermute | solution.py:12
  10.1 10.4 %collective-permute-start.10 = (f32[128,256]{1,0:T(8,128)S(1)}, f32[128,256]{1,0:T(8,128)S(1)}, u32[]{:S(2)}, u32[]{:S(2)}) collective-permute-start(f32[128,256]{1,0:T(8,128)S(1)} %slice.194), channel_id=1, source_target_pairs={{0,3},{1,2},{2,1},{3,0},{4,7},{5,6},{6,5},{7,4},{8,11},{9,10},{10,... | collective-permute-start | bytes 393224 | tf_op jit(solution)/shard_map/ppermute | solution.py:12
  15.6 9.3 %collective-permute-start.11 = (f32[128,256]{1,0:T(8,128)S(1)}, f32[128,256]{1,0:T(8,128)}, u32[]{:S(2)}, u32[]{:S(2)}) collective-permute-start(f32[128,256]{1,0:T(8,128)S(1)} %slice.194), channel_id=1, source_target_pairs={{0,4},{1,5},{2,6},{3,7},{4,0},{5,1},{6,2},{7,3},{8,12},{9,13},{10,... | collective-permute-start | bytes 393224 | tf_op jit(solution)/shard_map/ppermute | solution.py:12
  18.3 7.5 %collective-permute-start.2 = (f32[136,256]{1,0:T(8,128)S(1)}, f32[136,256]{1,0:T(8,128)S(1)}, u32[]{:S(2)}, u32[]{:S(2)}) collective-permute-start(f32[136,256]{1,0:T(8,128)S(1)} %pad_maximum_fusion), channel_id=1, source_target_pairs={{0,3},{1,2},{2,1},{3,0},{4,7},{5,6},{6,5},{7,4},{8,11},{9,10},{10,... | collective-permute-start | bytes 417800 | tf_op jit(solution)/shard_map/ppermute | solution.py:12
  20.4 8.9 %collective-permute-start.3 = (f32[136,256]{1,0:T(8,128)S(1)}, f32[136,256]{1,0:T(8,128)S(1)}, u32[]{:S(2)}, u32[]{:S(2)}) collective-permute-start(f32[136,256]{1,0:T(8,128)S(1)} %pad_maximum_fusion), channel_id=1, source_target_pairs={{0,4},{1,5},{2,6},{3,7},{4,0},{5,1},{6,2},{7,3},{8,12},{9,13},{10,... | collective-permute-start | bytes 417800 | tf_op jit(solution)/shard_map/ppermute | solution.py:12
  25.0 42.1 %collective-permute-start.12 = (f32[128,256]{1,0:T(8,128)}, f32[128,256]{1,0:T(8,128)}, u32[]{:S(2)}, u32[]{:S(2)}) collective-permute-start(f32[128,256]{1,0:T(8,128)} %collective-permute-done.11), channel_id=1, source_target_pairs={{0,1},{1,0},{2,3},{3,2},{4,5},{5,4},{6,7},{7,6},{8,9},{9,8},{10,11... | collective-permute-start | bytes 393224 | tf_op jit(solution)/shard_map/ppermute | solution.py:12
  29.5 5.2 %collective-permute-start.4 = (f32[136,256]{1,0:T(8,128)S(1)}, f32[136,256]{1,0:T(8,128)S(1)}, u32[]{:S(2)}, u32[]{:S(2)}) collective-permute-start(f32[136,256]{1,0:T(8,128)S(1)} %collective-permute-done.3), channel_id=1, source_target_pairs={{0,1},{1,0},{2,3},{3,2},{4,5},{5,4},{6,7},{7,6},{8,9},{9,8},{10,11... | collective-permute-start | bytes 417800 | tf_op jit(solution)/shard_map/ppermute | solution.py:12
  29.6 5.8 %collective-permute-start.5 = (f32[136,256]{1,0:T(8,128)S(1)}, f32[136,256]{1,0:T(8,128)S(1)}, u32[]{:S(2)}, u32[]{:S(2)}) collective-permute-start(f32[136,256]{1,0:T(8,128)S(1)} %collective-permute-done.3), channel_id=1, source_target_pairs={{0,2},{1,3},{2,0},{3,1},{4,6},{5,7},{6,4},{7,5},{8,10},{9,11},{10,... | collective-permute-start | bytes 417800 | tf_op jit(solution)/shard_map/ppermute | solution.py:12
  31.1 6.5 %collective-permute-start.6 = (f32[136,256]{1,0:T(8,128)S(1)}, f32[136,256]{1,0:T(8,128)S(1)}, u32[]{:S(2)}, u32[]{:S(2)}) collective-permute-start(f32[136,256]{1,0:T(8,128)S(1)} %collective-permute-done.3), channel_id=1, source_target_pairs={{0,3},{1,2},{2,1},{3,0},{4,7},{5,6},{6,5},{7,4},{8,11},{9,10},{10,... | collective-permute-start | bytes 417800 | tf_op jit(solution)/shard_map/ppermute | solution.py:12
  33.2 5.9 %copy-start.3 = (f32[2,8,32,256]{3,2,1,0:T(8,128)}, f32[2,8,32,256]{3,2,1,0:T(8,128)S(1)}, u32[]{:S(2)}) copy-start(f32[2,8,32,256]{3,2,1,0:T(8,128)S(1)} %constant_dynamic-update-slice_fusion.19) | copy-start | bytes 1572868
  52.0 6.8 %collective-permute-start.7 = (f32[512,64]{0,1:T(8,128)}, f32[512,64]{0,1:T(8,128)}, u32[]{:S(2)}, u32[]{:S(2)}) collective-permute-start(f32[512,64]{0,1:T(8,128)} %pad_maximum_fusion.1), channel_id=1, source_target_pairs={{0,8},{8,0},{16,24},{24,16},{1,9},{9,1},{17,25},{25,17},{2,10},{10... | collective-permute-start | bytes 393224 | tf_op jit(solution)/shard_map/ppermute | solution.py:12
  61.2 22.9 %copy-start.2 = (f32[512,256]{1,0:T(8,128)S(1)}, f32[512,256]{1,0:T(8,128)}, u32[]{:S(2)}) copy-start(f32[512,256]{1,0:T(8,128)} %squeeze.17) | copy-start | bytes 1572868
  62.9 21.5 %copy-start.4 = (f32[2,8,32,256]{3,2,1,0:T(8,128)S(1)}, f32[2,8,32,256]{3,2,1,0:T(8,128)}, u32[]{:S(2)}) copy-start(f32[2,8,32,256]{3,2,1,0:T(8,128)} %constant_dynamic-update-slice_fusion.16) | copy-start | bytes 1572868
  63.0 6.0 %collective-permute-start.15 = (f32[512,64]{0,1:T(8,128)S(1)}, f32[512,64]{0,1:T(8,128)S(1)}, u32[]{:S(2)}, u32[]{:S(2)}) collective-permute-start(f32[512,64]{0,1:T(8,128)S(1)} %pad_maximum_fusion.2), channel_id=1, source_target_pairs={{0,16},{8,24},{16,0},{24,8},{1,17},{9,25},{17,1},{25,9},{2,18},{10... | collective-permute-start | bytes 393224 | tf_op jit(solution)/shard_map/ppermute | solution.py:12
  65.5 6.6 %collective-permute-start.13 = (f32[128,256]{1,0:T(8,128)}, f32[128,256]{1,0:T(8,128)S(1)}, u32[]{:S(2)}, u32[]{:S(2)}) collective-permute-start(f32[128,256]{1,0:T(8,128)} %collective-permute-done.11), channel_id=1, source_target_pairs={{0,2},{1,3},{2,0},{3,1},{4,6},{5,7},{6,4},{7,5},{8,10},{9,11},{10,... | collective-permute-start | bytes 393224 | tf_op jit(solution)/shard_map/ppermute | solution.py:12
  65.6 8.3 %collective-permute-start.14 = (f32[128,256]{1,0:T(8,128)}, f32[128,256]{1,0:T(8,128)S(1)}, u32[]{:S(2)}, u32[]{:S(2)}) collective-permute-start(f32[128,256]{1,0:T(8,128)} %collective-permute-done.11), channel_id=1, source_target_pairs={{0,3},{1,2},{2,1},{3,0},{4,7},{5,6},{6,5},{7,4},{8,11},{9,10},{10,... | collective-permute-start | bytes 393224 | tf_op jit(solution)/shard_map/ppermute | solution.py:12
  69.0 17.6 %copy-start.1 = (f32[512,256]{1,0:T(8,128)S(1)}, f32[512,256]{1,0:T(8,128)}, u32[]{:S(2)}) copy-start(f32[512,256]{1,0:T(8,128)} %squeeze.16) | copy-start | bytes 1572868
  69.0 4.9 %collective-permute-start.16 = (f32[512,64]{0,1:T(8,128)S(1)}, f32[512,64]{0,1:T(8,128)S(1)}, u32[]{:S(2)}, u32[]{:S(2)}) collective-permute-start(f32[512,64]{0,1:T(8,128)S(1)} %pad_maximum_fusion.3), channel_id=1, source_target_pairs={{0,8},{8,0},{16,24},{24,16},{1,9},{9,1},{17,25},{25,17},{2,10},{10... | collective-permute-start | bytes 393224 | tf_op jit(solution)/shard_map/ppermute | solution.py:12
  76.9 1.4 %collective-permute-start.17 = (f32[512,64]{0,1:T(8,128)S(1)}, f32[512,64]{0,1:T(8,128)S(1)}, u32[]{:S(2)}, u32[]{:S(2)}) collective-permute-start(f32[512,64]{0,1:T(8,128)S(1)} %pad_maximum_fusion.4), channel_id=1, source_target_pairs={{0,8},{8,0},{16,24},{24,16},{1,9},{9,1},{17,25},{25,17},{2,10},{10... | collective-permute-start | bytes 393224 | tf_op jit(solution)/shard_map/ppermute | solution.py:12
  78.4 5.6 %collective-permute-start.18 = (f32[512,64]{0,1:T(8,128)S(1)}, f32[512,64]{0,1:T(8,128)S(1)}, u32[]{:S(2)}, u32[]{:S(2)}) collective-permute-start(f32[512,64]{0,1:T(8,128)S(1)} %pad_maximum_fusion.5), channel_id=1, source_target_pairs={{0,16},{8,24},{16,0},{24,8},{1,17},{9,25},{17,1},{25,9},{2,18},{10... | collective-permute-start | bytes 393224 | tf_op jit(solution)/shard_map/ppermute | solution.py:12
  85.2 1.4 %collective-permute-start.19 = (f32[512,64]{0,1:T(8,128)S(1)}, f32[512,64]{0,1:T(8,128)S(1)}, u32[]{:S(2)}, u32[]{:S(2)}) collective-permute-start(f32[512,64]{0,1:T(8,128)S(1)} %pad_maximum_fusion.6), channel_id=1, source_target_pairs={{0,8},{8,0},{16,24},{24,16},{1,9},{9,1},{17,25},{25,17},{2,10},{10... | collective-permute-start | bytes 393224 | tf_op jit(solution)/shard_map/ppermute | solution.py:12
  (5 other events, 9.8 us)

commit v2 on v0

--- a/solution.py
+++ b/solution.py
@@ -1,7 +1,230 @@
+import functools
+
 import jax
 import jax.numpy as jnp
 from jax import lax
+from jax.experimental import pallas as pl
+from jax.experimental.pallas import tpu as pltpu
 from jax.sharding import PartitionSpec as P
+
+HIGHEST = lax.Precision.HIGHEST
+GATHER_BYTES = 8 * 2**20
+
+
+def dot(a, b):
+    return lax.dot_general(
+        a, b, (((1,), (0,)), ((), ())), precision=HIGHEST, preferred_element_type=jnp.float32
+    )
+
+
+def dot_t(a, b):
+    return lax.dot_general(
+        a, b, (((0,), (0,)), ((), ())), precision=HIGHEST, preferred_element_type=jnp.float32
+    )
+
+
+def swap(block, axis, mask):
+    count = lax.axis_size(axis)
+    return lax.ppermute(block, axis, [(i, i ^ mask) for i in range(count)])
+
+
+def gather_rows(block):
+    half = lax.axis_size("blk") // 2
+    far = swap(block, "blk", half)
+    near = {m: swap(block, "blk", m) for m in reversed(range(1, half))}
+    out = {0: block, half: far}
+    for m in reversed(range(1, half)):
+        out[m] = near[m]
+        out[m + half] = swap(far, "blk", m)
+    return [out[m] for m in range(2 * half)]
+
+
+class Packing:
+    def __init__(self, levels, rows, cols, width, n_blk):
+        self.levels, self.rows, self.cols, self.width, self.n_blk = levels, rows, cols, width, n_blk
+        self.top = (2 ** (levels - 1) - 1) * rows
+        self.low = (levels - 1) * (cols + 2 * rows)
+        self.fold = width // cols
+        self.fits = (
+            self.low == width
+            and width == n_blk * rows
+            and rows % (8 * self.fold) == 0
+            and n_blk == 2 ** (n_blk.bit_length() - 1)
+        )
+        self.height = self.top + rows + rows // self.fold
+
+    def rhs(self, piece, level):
+        rows, cols = self.rows, self.cols
+        if level < self.levels - 1:
+            return piece[self.top : self.top + rows, level * cols : (level + 1) * cols]
+        start, step = self.top + rows, rows // self.fold
+        return jnp.concatenate(
+            [piece[start : start + step, j * cols : (j + 1) * cols] for j in range(self.fold)], axis=0
+        )
+
+    def extend(self, piece, level):
+        rows = self.rows
+        first = (self.levels - 1) * self.cols + level * 2 * rows
+        return jnp.concatenate(
+            [piece[self.top : self.top + rows, first + h * rows : first + (h + 1) * rows] for h in (0, 1)],
+            axis=0,
+        )
+
+    def diag(self, pieces, level, first=None):
+        first = (2**level - 1) * self.rows if first is None else first
+        return jnp.concatenate(
+            [
+                q[first + p * self.rows : first + (p + 1) * self.rows, :]
+                for p in range(2**level)
+                for q in pieces
+            ],
+            axis=0,
+        )
+
+
+def pack_kernel(pk, rhs_ref, panels_ref, maps_ref, diag_ref, out_ref):
+    rows, cols = pk.rows, pk.cols
+    out_ref[: pk.top, :] = diag_ref[: pk.top, :]
+    parts = [rhs_ref[l] for l in range(pk.levels - 1)]
+    for l in range(pk.levels - 1):
+        for h in (0, 1):
+            panel = panels_ref[l, h]
+            row_ids = lax.broadcasted_iota(jnp.int32, (rows, panel.shape[0]), 0)
+            names = maps_ref[2 * l + h : 2 * l + h + 1, :]
+            onehot = jnp.where(row_ids == names, 1.0, 0.0).astype(jnp.float32)
+            parts.append(dot(onehot, panel))
+    out_ref[pk.top : pk.top + rows, :] = jnp.concatenate(parts, axis=1)
+    last = rhs_ref[pk.levels - 1]
+    step = rows // pk.fold
+    out_ref[pk.top + rows :, :] = jnp.concatenate(
+        [last[j * step : (j + 1) * step] for j in range(pk.fold)], axis=1
+    )
+
+
+def block_of(pk, m):
+    place = (lax.axis_index("blk") ^ m) * pk.rows
+    return pl.ds(pl.multiple_of(place, pk.rows), pk.rows)
+
+
+def extend_out(pk, level, pieces, y_ref, send_ref):
+    rows, node = pk.rows, pk.width
+    for m, piece in enumerate(pieces):
+        e = dot(pk.extend(piece, level), y_ref[block_of(pk, m), :])
+        send_ref[m * rows : (m + 1) * rows, :] = pk.rhs(piece, level + 1) - e[:rows]
+        send_ref[node + m * rows : node + (m + 1) * rows, :] = e[rows:]
+
+
+def first_kernel(pk, *refs):
+    pieces, (send_ref, y_ref) = refs[: pk.n_blk], refs[pk.n_blk :]
+    z = jnp.concatenate([pk.rhs(q, 0) for q in pieces], axis=0)
+    y_ref[...] = dot_t(pk.diag(pieces, 0), z)
+    extend_out(pk, 0, pieces, y_ref, send_ref)
+
+
+def middle_kernel(pk, *refs):
+    pieces, (mine_ref, got_ref, send_ref, y_ref) = refs[: pk.n_blk], refs[pk.n_blk :]
+    node = pk.width
+    own = mine_ref[:node] - got_ref[node:]
+    other = got_ref[:node] - mine_ref[node:]
+    upper = lax.axis_index("cube") % 2 == 1
+    z = jnp.concatenate([jnp.where(upper, other, own), jnp.where(upper, own, other)], axis=0)
+    y_ref[...] = dot_t(pk.diag(pieces, 1), z)
+    extend_out(pk, 1, pieces, y_ref, send_ref)
+
+
+def top_kernel(pk, *refs):
+    pieces, (mine_ref, got_ref, keep_ref, send_ref, vec_ref) = refs[: pk.n_blk], refs[pk.n_blk :]
+    node = pk.width
+    cube = lax.axis_index("cube")
+
+    def part(k):
+        return pl.ds(pl.multiple_of((cube ^ k) * node, node), node)
+
+    vec_ref[part(0), :] = mine_ref[:node]
+    vec_ref[part(2), :] = mine_ref[node:]
+    vec_ref[part(1), :] = got_ref[:node]
+    vec_ref[part(3), :] = got_ref[node:]
+    diag = pk.diag(pieces, 2, 0)
+    vec_ref[...] = dot(diag, dot_t(diag, vec_ref[...]))
+    keep_ref[:node] = vec_ref[part(0), :]
+    keep_ref[node:] = vec_ref[part(2), :]
+    send_ref[:node] = vec_ref[part(1), :]
+    send_ref[node:] = vec_ref[part(3), :]
+
+
+def reduce_rows(pk, level, pieces, y_ref, pair, w_ref):
+    rows, node = pk.rows, pk.width
+    for m, piece in enumerate(pieces):
+        both = jnp.concatenate(
+            [pair[m * rows : (m + 1) * rows], pair[node + m * rows : node + (m + 1) * rows]], axis=0
+        )
+        place = block_of(pk, m)
+        w_ref[place, :] = y_ref[place, :] - dot_t(pk.extend(piece, level), both)
+
+
+def down_kernel(pk, *refs):
+    pieces, (y_ref, mine_ref, got_ref, keep_ref, send_ref, top_ref, w_ref) = refs[: pk.n_blk], refs[pk.n_blk :]
+    node = pk.width
+    pair = mine_ref[...] + got_ref[...]
+    top_ref[...] = pair[: pk.rows]
+    reduce_rows(pk, 1, pieces, y_ref, pair, w_ref)
+    x = dot(pk.diag(pieces, 1), w_ref[...])
+    upper = lax.axis_index("cube") % 2 == 1
+    own = jnp.where(upper, x[node:], x[:node])
+    other = jnp.where(upper, x[:node], x[node:])
+    keep_ref[:node] = own
+    keep_ref[node:] = other
+    send_ref[:node] = other
+    send_ref[node:] = own
+
+
+def last_kernel(pk, *refs):
+    pieces, (y_ref, mine_ref, got_ref, top_ref, out_ref, w_ref) = refs[: pk.n_blk], refs[pk.n_blk :]
+    pair = mine_ref[...] + got_ref[...]
+    out_ref[2] = top_ref[...]
+    out_ref[1] = pair[: pk.rows]
+    reduce_rows(pk, 0, pieces, y_ref, pair, w_ref)
+    out_ref[0] = dot(pieces[0][: pk.rows, :], w_ref[...])
+
+
+def call(kernel, pk, args, outs, scratch=()):
+    vmem = pl.BlockSpec(memory_space=pltpu.VMEM)
+    return pl.pallas_call(
+        functools.partial(kernel, pk),
+        out_shape=[jax.ShapeDtypeStruct(s, jnp.float32) for s in outs],
+        in_specs=[vmem] * len(args),
+        out_specs=[vmem] * len(outs),
+        scratch_shapes=[pltpu.VMEM(s, jnp.float32) for s in scratch],
+        compiler_params=pltpu.CompilerParams(vmem_limit_bytes=24 * 2**20),
+    )(*args)
+
+
+def gathered(pk, right_side, diag_inverse, panels, extend_map):
+    rows, cols, node = pk.rows, pk.cols, pk.width
+    one, two = (node, cols), (2 * node, cols)
+    maps = extend_map.reshape(-1, extend_map.shape[-1])
+    (packed,) = call(
+        pack_kernel,
+        pk,
+        [right_side[:, 0, 0], panels[:, 0, 0], maps, diag_inverse],
+        [(pk.height, pk.width)],
+    )
+    first = gather_rows(packed)
+    last = gather_rows(diag_inverse[pk.top :])
+
+    send, y0 = call(first_kernel, pk, first, [two, one])
+    got = swap(send, "cube", 1)
+    send, y1 = call(middle_kernel, pk, [*first, send, got], [two, one])
+    got = swap(send, "cube", 2)
+    held = jnp.concatenate([send[:node] - got[node:], got[:node] - send[node:]], axis=0)
+    got = swap(held, "cube", 1)
+    keep, send = call(top_kernel, pk, [*last, held, got], [two, two], [(4 * node, cols)])
+    held = keep + swap(send, "cube", 1)
+    got = swap(jnp.concatenate([held[node:], held[:node]], axis=0), "cube", 2)
+    keep, send, top = call(down_kernel, pk, [*first, y1, held, got], [two, two, (rows, cols)], [one])
+    got = swap(send, "cube", 1)
+    (out,) = call(last_kernel, pk, [*first, y0, keep, got, top], [(3, rows, cols)], [one])
+    return out[:, None, None]
 
 
 def from_partner(block, axis, apart):
@@ -39,7 +262,7 @@
     return partial_value
 
 
-def body(right_side, diag_inverse, panels, extend_map):
+def stepwise(right_side, diag_inverse, panels, extend_map):
     highest = lax.Precision.HIGHEST
     levels = right_side.shape[0]
     local_rows = right_side.shape[3]
@@ -106,6 +329,15 @@
         results[tree_level] = parent
     return jnp.stack(results)[:, None, None]
 
+def body(right_side, diag_inverse, panels, extend_map):
+    levels, _, _, rows, cols = right_side.shape
+    n_blk = lax.axis_size("blk")
+    pk = Packing(levels, rows, cols, diag_inverse.shape[1], n_blk)
+    small = n_blk * diag_inverse.size * 4 <= GATHER_BYTES
+    if levels == 3 and lax.axis_size("cube") == 4 and pk.fits and small:
+        return gathered(pk, right_side, diag_inverse, panels, extend_map)
+    return stepwise(right_side, diag_inverse, panels, extend_map)
+
 
 def solution(mesh):
     placed = (

time: 324 us -> 64.8 us (0.20)
  waiting for transfers between devices: 202 us -> 28.9 us
  blocking collectives: 91.9 us -> 0 us
  starting transfers between devices: 6.67 us -> 23.2 us
  between operations: 13.3 us -> 0.14 us
  Pallas kernels: 0 us -> 9.04 us
  matrix products: 6.6 us -> 0 us
    reduce_scatter x2 -> x0, waiting for transfers between devices: 126 us -> none  [body(): lax.psum_scatter(term_rows(jnp.int32(0), lax.axis_size('blk') * local_row...]
    all_gather x3 -> x0, blocking collectives: 91.9 us -> none  [body(): lax.all_gather(work_rows, 'blk', axis=0, tiled=True)]
    unnamed x4 -> x0, waiting for transfers between devices: 60 us -> none
    ppermute x10 -> x20, starting transfers between devices: 6.58 us -> 23.2 us  [swap(): return lax.ppermute(block, axis, [(i, i ^ mask) for i in range(count)])]
    ppermute x10 -> x20, waiting for transfers between devices: 16.2 us -> 28.9 us  [swap(): return lax.ppermute(block, axis, [(i, i ^ mask) for i in range(count)])]
    pallas_call x0 -> x6, Pallas kernels: none -> 9.04 us  [call(): pl.pallas_call(functools.partial(kernel, pk), out_shape=[jax.ShapeDtypeSt...]
    dot_general x14 -> x0, matrix products: 6.6 us -> none  [the longest x3 2.35 us: term_rows(): return jnp.einsum('ir,ik->rk', diag_block, column, precision=highest)]
  transfers between devices with their start and end apart: 13 -> 20, of which waited for: 13 -> 12; matrix products, arithmetic and copies ran while one was open for 0% -> 0% of each run, Pallas kernels for 0% -> 2%
where the time goes in v2:
time: 64.8 us; the launch traced here: 64.6 us
  waiting for transfers between devices  28.9 us (45%)
  starting transfers between devices  23.2 us (36%)
  Pallas kernels  9.04 us (14%)
  local copies, waits for them, and re-layouts  3.2 us (5%)
    ppermute x20, waiting for transfers between devices, swap(): return lax.ppermute(block, axis, [(i, i ^ mask) for i in range(count)])  28.9 us
    ppermute x20, starting transfers between devices, swap(): return lax.ppermute(block, axis, [(i, i ^ mask) for i in range(count)])  23.2 us
    pallas_call x6, Pallas kernels, call(): pl.pallas_call(functools.partial(kernel, pk), out_shape=[jax.ShapeDtypeSt...  9.04 us
    unnamed x8, local copies, waits for them, and re-layouts  3.17 us
  transfers between devices with their start and end apart: 20, of which 12 were waited for; matrix products, arithmetic and copies ran while one was open for 0% of the time, Pallas kernels for 2%

profile of v2, /device:TPU:0, one launch (start us, length us, event | category | flops | bytes accessed | tf_op | source)
XLA Modules:
  0.0 64.6 jit_solution(9376110984111115977)
XLA Ops:
  3.4 4.1 %collective-permute-start.3 = (f32[136,256]{1,0:T(8,128)S(1)}, f32[136,256]{1,0:T(8,128)S(1)}, u32[]{:S(2)}, u32[]{:S(2)}) collective-permute-start(f32[136,256]{1,0:T(8,128)S(1)} %shard_map.46.refs_0_), channel_id=1, source_target_pairs={{0,4},{1,5},{2,6},{3,7},{4,0},{5,1},{6,2},{7,3},{8,12},{9,13},{10,... | collective-permute-start | bytes 417800 | tf_op jit(solution)/shard_map/ppermute | solution.py:28
  7.6 2.5 %collective-permute-start.2 = (f32[136,256]{1,0:T(8,128)S(1)}, f32[136,256]{1,0:T(8,128)S(1)}, u32[]{:S(2)}, u32[]{:S(2)}) collective-permute-start(f32[136,256]{1,0:T(8,128)S(1)} %shard_map.46.refs_0_), channel_id=1, source_target_pairs={{0,3},{1,2},{2,1},{3,0},{4,7},{5,6},{6,5},{7,4},{8,11},{9,10},{10,... | collective-permute-start | bytes 417800 | tf_op jit(solution)/shard_map/ppermute | solution.py:28
  11.0 3.3 %collective-permute-done.3.refs_4_ = f32[136,256]{1,0:T(8,128)S(1)} collective-permute-done((f32[136,256]{1,0:T(8,128)S(1)}, f32[136,256]{1,0:T(8,128)S(1)}, u32[]{:S(2)}, u32[]{:S(2)}) %collective-permute-start.3) | collective-permute-done | bytes 139296 | tf_op jit(solution)/shard_map/ppermute | solution.py:28
  14.3 1.6 %collective-permute-start.6 = (f32[136,256]{1,0:T(8,128)S(1)}, f32[136,256]{1,0:T(8,128)S(1)}, u32[]{:S(2)}, u32[]{:S(2)}) collective-permute-start(f32[136,256]{1,0:T(8,128)S(1)} %collective-permute-done.3.refs_4_), channel_id=1, source_target_pairs={{0,3},{1,2},{2,1},{3,0},{4,7},{5,6},{6,5},{7,4},{8,11},{9,10},{10,... | collective-permute-start | bytes 417800 | tf_op jit(solution)/shard_map/ppermute | solution.py:28
  15.9 1.4 %collective-permute-start.5 = (f32[136,256]{1,0:T(8,128)S(1)}, f32[136,256]{1,0:T(8,128)S(1)}, u32[]{:S(2)}, u32[]{:S(2)}) collective-permute-start(f32[136,256]{1,0:T(8,128)S(1)} %collective-permute-done.3.refs_4_), channel_id=1, source_target_pairs={{0,2},{1,3},{2,0},{3,1},{4,6},{5,7},{6,4},{7,5},{8,10},{9,11},{10,... | collective-permute-start | bytes 417800 | tf_op jit(solution)/shard_map/ppermute | solution.py:28
  18.0 1.5 %collective-permute-done.1.refs_2_ = f32[136,256]{1,0:T(8,128)S(1)} collective-permute-done((f32[136,256]{1,0:T(8,128)S(1)}, f32[136,256]{1,0:T(8,128)S(1)}, u32[]{:S(2)}, u32[]{:S(2)}) %collective-permute-start.1) | collective-permute-done | bytes 139296 | tf_op jit(solution)/shard_map/ppermute | solution.py:28
  19.6 3.3 %collective-permute-done.6.refs_7_ = f32[136,256]{1,0:T(8,128)S(1)} collective-permute-done((f32[136,256]{1,0:T(8,128)S(1)}, f32[136,256]{1,0:T(8,128)S(1)}, u32[]{:S(2)}, u32[]{:S(2)}) %collective-permute-start.6) | collective-permute-done | bytes 139296 | tf_op jit(solution)/shard_map/ppermute | solution.py:28
  22.9 1.5 %collective-permute-done.5.refs_6_ = f32[136,256]{1,0:T(8,128)S(1)} collective-permute-done((f32[136,256]{1,0:T(8,128)S(1)}, f32[136,256]{1,0:T(8,128)S(1)}, u32[]{:S(2)}, u32[]{:S(2)}) %collective-permute-start.5) | collective-permute-done | bytes 139296 | tf_op jit(solution)/shard_map/ppermute | solution.py:28
  24.4 1.3 %shard_map.47 = (f32[512,64]{1,0:T(8,128)S(1)}, f32[256,64]{1,0:T(8,128)S(1)}) custom-call(f32[136,256]{1,0:T(8,128)S(1)} %shard_map.46.refs_0_, f32[136,256]{1,0:T(8,128)S(1)} %collective-permute-done.refs_1_, f32[136,256]{1,0:T(8,128)S(1)} %collective-permute-done.1.refs_2_, f32[136,256]{1,0:T(8,128)S(1)} %collective-permute-done.2.refs_3_, ...), custom_call_target="tpu_custom_call" | custom-call | tf_op jit(solution)/shard_map/pallas_call | solution.py:192
  25.7 1.8 %collective-permute-start.11 = (f32[128,256]{1,0:T(8,128)S(1)}, f32[128,256]{1,0:T(8,128)S(1)}, u32[]{:S(2)}, u32[]{:S(2)}) collective-permute-start(f32[128,256]{1,0:T(8,128)S(1)} %slice.21.refs_0_), channel_id=1, source_target_pairs={{0,4},{1,5},{2,6},{3,7},{4,0},{5,1},{6,2},{7,3},{8,12},{9,13},{10,... | collective-permute-start | bytes 393224 | tf_op jit(solution)/shard_map/ppermute | solution.py:28
  27.5 1.3 %shard_map.48 = (f32[512,64]{1,0:T(8,128)S(1)}, f32[256,64]{1,0:T(8,128)S(1)}) custom-call(f32[136,256]{1,0:T(8,128)S(1)} %shard_map.46.refs_0_, f32[136,256]{1,0:T(8,128)S(1)} %collective-permute-done.refs_1_, f32[136,256]{1,0:T(8,128)S(1)} %collective-permute-done.1.refs_2_, f32[136,256]{1,0:T(8,128)S(1)} %collective-permute-done.2.refs_3_, ...), custom_call_target="tpu_custom_call" | custom-call | tf_op jit(solution)/shard_map/pallas_call | solution.py:192
  28.9 1.6 %collective-permute-start.15 = (f32[512,64]{1,0:T(8,128)S(1)}, f32[512,64]{1,0:T(8,128)S(1)}, u32[]{:S(2)}, u32[]{:S(2)}) collective-permute-start(f32[512,64]{1,0:T(8,128)S(1)} %get-tuple-element.17), channel_id=1, source_target_pairs={{0,16},{8,24},{16,0},{24,8},{1,17},{9,25},{17,1},{25,9},{2,18},{10... | collective-permute-start | bytes 393224 | tf_op jit(solution)/shard_map/ppermute | solution.py:28
  30.4 2.6 %collective-permute-start.10 = (f32[128,256]{1,0:T(8,128)S(1)}, f32[128,256]{1,0:T(8,128)S(1)}, u32[]{:S(2)}, u32[]{:S(2)}) collective-permute-start(f32[128,256]{1,0:T(8,128)S(1)} %slice.21.refs_0_), channel_id=1, source_target_pairs={{0,3},{1,2},{2,1},{3,0},{4,7},{5,6},{6,5},{7,4},{8,11},{9,10},{10,... | collective-permute-start | bytes 393224 | tf_op jit(solution)/shard_map/ppermute | solution.py:28
  33.9 1.6 %collective-permute-done.11.refs_4_ = f32[128,256]{1,0:T(8,128)S(1)} collective-permute-done((f32[128,256]{1,0:T(8,128)S(1)}, f32[128,256]{1,0:T(8,128)S(1)}, u32[]{:S(2)}, u32[]{:S(2)}) %collective-permute-start.11) | collective-permute-done | bytes 131104 | tf_op jit(solution)/shard_map/ppermute | solution.py:28
  37.3 1.8 %collective-permute-start.13 = (f32[128,256]{1,0:T(8,128)S(1)}, f32[128,256]{1,0:T(8,128)S(1)}, u32[]{:S(2)}, u32[]{:S(2)}) collective-permute-start(f32[128,256]{1,0:T(8,128)S(1)} %collective-permute-done.11.refs_4_), channel_id=1, source_target_pairs={{0,2},{1,3},{2,0},{3,1},{4,6},{5,7},{6,4},{7,5},{8,10},{9,11},{10,... | collective-permute-start | bytes 393224 | tf_op jit(solution)/shard_map/ppermute | solution.py:28
  39.2 1.5 %collective-permute-start.12 = (f32[128,256]{1,0:T(8,128)S(1)}, f32[128,256]{1,0:T(8,128)S(1)}, u32[]{:S(2)}, u32[]{:S(2)}) collective-permute-start(f32[128,256]{1,0:T(8,128)S(1)} %collective-permute-done.11.refs_4_), channel_id=1, source_target_pairs={{0,1},{1,0},{2,3},{3,2},{4,5},{5,4},{6,7},{7,6},{8,9},{9,8},{10,11... | collective-permute-start | bytes 393224 | tf_op jit(solution)/shard_map/ppermute | solution.py:28
  41.2 2.8 %collective-permute-done.14.refs_7_ = f32[128,256]{1,0:T(8,128)S(1)} collective-permute-done((f32[128,256]{1,0:T(8,128)S(1)}, f32[128,256]{1,0:T(8,128)S(1)}, u32[]{:S(2)}, u32[]{:S(2)}) %collective-permute-start.14) | collective-permute-done | bytes 131104 | tf_op jit(solution)/shard_map/ppermute | solution.py:28
  44.0 2.6 %collective-permute-done.13.refs_6_ = f32[128,256]{1,0:T(8,128)S(1)} collective-permute-done((f32[128,256]{1,0:T(8,128)S(1)}, f32[128,256]{1,0:T(8,128)S(1)}, u32[]{:S(2)}, u32[]{:S(2)}) %collective-permute-start.13) | collective-permute-done | bytes 131104 | tf_op jit(solution)/shard_map/ppermute | solution.py:28
  46.6 3.6 %shard_map.49 = (f32[512,64]{1,0:T(8,128)S(1)}, f32[512,64]{1,0:T(8,128)S(1)}) custom-call(f32[128,256]{1,0:T(8,128)S(1)} %slice.21.refs_0_, f32[128,256]{1,0:T(8,128)S(1)} %collective-permute-done.8.refs_1_, f32[128,256]{1,0:T(8,128)S(1)} %collective-permute-done.9.refs_2_, f32[128,256]{1,0:T(8,128)S(1)} %collective-permute-done.10.refs_3_, ...), custom_call_target="tpu_custom_call" | custom-call | tf_op jit(solution)/shard_map/pallas_call | solution.py:192
  50.3 1.5 %collective-permute-done.17 = f32[512,64]{1,0:T(8,128)S(1)} collective-permute-done((f32[512,64]{1,0:T(8,128)S(1)}, f32[512,64]{1,0:T(8,128)S(1)}, u32[]{:S(2)}, u32[]{:S(2)}) %collective-permute-start.17) | collective-permute-done | bytes 131104 | tf_op jit(solution)/shard_map/ppermute | solution.py:28
  52.5 7.9 %collective-permute-done.18.refs_10_ = f32[512,64]{1,0:T(8,128)S(1)} collective-permute-done((f32[512,64]{1,0:T(8,128)S(1)}, f32[512,64]{1,0:T(8,128)S(1)}, u32[]{:S(2)}, u32[]{:S(2)}) %collective-permute-start.18) | collective-permute-done | bytes 131104 | tf_op jit(solution)/shard_map/ppermute | solution.py:28
  60.3 1.2 %shard_map.50 = (f32[512,64]{1,0:T(8,128)S(1)}, f32[512,64]{1,0:T(8,128)S(1)}, f32[32,64]{1,0:T(8,128)S(1)}) custom-call(f32[136,256]{1,0:T(8,128)S(1)} %shard_map.46.refs_0_, f32[136,256]{1,0:T(8,128)S(1)} %collective-permute-done.refs_1_, f32[136,256]{1,0:T(8,128)S(1)} %collective-permute-done.1.refs_2_, f32[136,256]{1,0:T(8,128)S(1)} %collective-permute-done.2.refs_3_, ...), custom_call_target="tpu_custom_call" | custom-call | tf_op jit(solution)/shard_map/pallas_call | solution.py:192
  61.6 1.5 %collective-permute-done.19.refs_10_ = f32[512,64]{1,0:T(8,128)S(1)} collective-permute-done((f32[512,64]{1,0:T(8,128)S(1)}, f32[512,64]{1,0:T(8,128)S(1)}, u32[]{:S(2)}, u32[]{:S(2)}) %collective-permute-start.19) | collective-permute-done | bytes 131104 | tf_op jit(solution)/shard_map/ppermute | solution.py:28
  63.2 1.4 %shard_map.51 = f32[3,32,64]{2,1,0:T(8,128)} custom-call(f32[136,256]{1,0:T(8,128)S(1)} %shard_map.46.refs_0_, f32[136,256]{1,0:T(8,128)S(1)} %collective-permute-done.refs_1_, f32[136,256]{1,0:T(8,128)S(1)} %collective-permute-done.1.refs_2_, f32[136,256]{1,0:T(8,128)S(1)} %collective-permute-done.2.refs_3_, f32[136,256]{1,0:T(8,128)S(1)} %collective-permute-done.3.refs_4_, ...), custom_call_target="tpu_custom_call" | custom-call | tf_op jit(solution)/shard_map/pallas_call | solution.py:192
  (36 shorter events, 9.1 us)
Async XLA Ops:
  0.0 0.7 %copy-start.3 = (s32[2,1,1,2,16]{4,3,2,1,0:T(2,128)S(1)}, s32[2,1,1,2,16]{4,3,2,1,0:T(2,128)}, u32[]{:S(2)}) copy-start(s32[2,1,1,2,16]{4,3,2,1,0:T(2,128)} %param.7) | copy-start | bytes 772
  0.7 0.9 %copy-start = (f32[224,256]{1,0:T(8,128)S(1)}, f32[224,256]{1,0:T(8,128)}, u32[]{:S(2)}) copy-start(f32[224,256]{1,0:T(8,128)} %diag_ref.1) | copy-start | bytes 688132
  1.6 0.8 %copy-start.1 = (f32[3,1,1,32,64]{4,3,2,1,0:T(8,128)S(1)}, f32[3,1,1,32,64]{4,3,2,1,0:T(8,128)}, u32[]{:S(2)}) copy-start(f32[3,1,1,32,64]{4,3,2,1,0:T(8,128)} %param.4) | copy-start | bytes 73732
  2.4 0.8 %copy-start.2 = (f32[2,1,1,2,16,32]{5,4,3,2,1,0:T(8,128)S(1)}, f32[2,1,1,2,16,32]{5,4,3,2,1,0:T(8,128)}, u32[]{:S(2)}) copy-start(f32[2,1,1,2,16,32]{5,4,3,2,1,0:T(8,128)} %param.6) | copy-start | bytes 24580
  3.4 10.9 %collective-permute-start.3 = (f32[136,256]{1,0:T(8,128)S(1)}, f32[136,256]{1,0:T(8,128)S(1)}, u32[]{:S(2)}, u32[]{:S(2)}) collective-permute-start(f32[136,256]{1,0:T(8,128)S(1)} %shard_map.46.refs_0_), channel_id=1, source_target_pairs={{0,4},{1,5},{2,6},{3,7},{4,0},{5,1},{6,2},{7,3},{8,12},{9,13},{10,... | collective-permute-start | bytes 417800 | tf_op jit(solution)/shard_map/ppermute | solution.py:28
  7.6 9.8 %collective-permute-start.2 = (f32[136,256]{1,0:T(8,128)S(1)}, f32[136,256]{1,0:T(8,128)S(1)}, u32[]{:S(2)}, u32[]{:S(2)}) collective-permute-start(f32[136,256]{1,0:T(8,128)S(1)} %shard_map.46.refs_0_), channel_id=1, source_target_pairs={{0,3},{1,2},{2,1},{3,0},{4,7},{5,6},{6,5},{7,4},{8,11},{9,10},{10,... | collective-permute-start | bytes 417800 | tf_op jit(solution)/shard_map/ppermute | solution.py:28
  10.1 9.5 %collective-permute-start.1 = (f32[136,256]{1,0:T(8,128)S(1)}, f32[136,256]{1,0:T(8,128)S(1)}, u32[]{:S(2)}, u32[]{:S(2)}) collective-permute-start(f32[136,256]{1,0:T(8,128)S(1)} %shard_map.46.refs_0_), channel_id=1, source_target_pairs={{0,2},{1,3},{2,0},{3,1},{4,6},{5,7},{6,4},{7,5},{8,10},{9,11},{10,... | collective-permute-start | bytes 417800 | tf_op jit(solution)/shard_map/ppermute | solution.py:28
  10.5 9.0 %collective-permute-start = (f32[136,256]{1,0:T(8,128)S(1)}, f32[136,256]{1,0:T(8,128)S(1)}, u32[]{:S(2)}, u32[]{:S(2)}) collective-permute-start(f32[136,256]{1,0:T(8,128)S(1)} %shard_map.46.refs_0_), channel_id=1, source_target_pairs={{0,1},{1,0},{2,3},{3,2},{4,5},{5,4},{6,7},{7,6},{8,9},{9,8},{10,11... | collective-permute-start | bytes 417800 | tf_op jit(solution)/shard_map/ppermute | solution.py:28
  14.3 8.6 %collective-permute-start.6 = (f32[136,256]{1,0:T(8,128)S(1)}, f32[136,256]{1,0:T(8,128)S(1)}, u32[]{:S(2)}, u32[]{:S(2)}) collective-permute-start(f32[136,256]{1,0:T(8,128)S(1)} %collective-permute-done.3.refs_4_), channel_id=1, source_target_pairs={{0,3},{1,2},{2,1},{3,0},{4,7},{5,6},{6,5},{7,4},{8,11},{9,10},{10,... | collective-permute-start | bytes 417800 | tf_op jit(solution)/shard_map/ppermute | solution.py:28
  15.9 8.5 %collective-permute-start.5 = (f32[136,256]{1,0:T(8,128)S(1)}, f32[136,256]{1,0:T(8,128)S(1)}, u32[]{:S(2)}, u32[]{:S(2)}) collective-permute-start(f32[136,256]{1,0:T(8,128)S(1)} %collective-permute-done.3.refs_4_), channel_id=1, source_target_pairs={{0,2},{1,3},{2,0},{3,1},{4,6},{5,7},{6,4},{7,5},{8,10},{9,11},{10,... | collective-permute-start | bytes 417800 | tf_op jit(solution)/shard_map/ppermute | solution.py:28
  17.4 7.1 %collective-permute-start.4 = (f32[136,256]{1,0:T(8,128)S(1)}, f32[136,256]{1,0:T(8,128)S(1)}, u32[]{:S(2)}, u32[]{:S(2)}) collective-permute-start(f32[136,256]{1,0:T(8,128)S(1)} %collective-permute-done.3.refs_4_), channel_id=1, source_target_pairs={{0,1},{1,0},{2,3},{3,2},{4,5},{5,4},{6,7},{7,6},{8,9},{9,8},{10,11... | collective-permute-start | bytes 417800 | tf_op jit(solution)/shard_map/ppermute | solution.py:28
  25.7 1.9 %collective-permute-start.7 = (f32[512,64]{1,0:T(8,128)S(1)}, f32[512,64]{1,0:T(8,128)S(1)}, u32[]{:S(2)}, u32[]{:S(2)}) collective-permute-start(f32[512,64]{1,0:T(8,128)S(1)} %get-tuple-element.15.refs_8_), channel_id=1, source_target_pairs={{0,8},{8,0},{16,24},{24,16},{1,9},{9,1},{17,25},{25,17},{2,10},{10... | collective-permute-start | bytes 393224 | tf_op jit(solution)/shard_map/ppermute | solution.py:28
  25.7 9.8 %collective-permute-start.11 = (f32[128,256]{1,0:T(8,128)S(1)}, f32[128,256]{1,0:T(8,128)S(1)}, u32[]{:S(2)}, u32[]{:S(2)}) collective-permute-start(f32[128,256]{1,0:T(8,128)S(1)} %slice.21.refs_0_), channel_id=1, source_target_pairs={{0,4},{1,5},{2,6},{3,7},{4,0},{5,1},{6,2},{7,3},{8,12},{9,13},{10,... | collective-permute-start | bytes 393224 | tf_op jit(solution)/shard_map/ppermute | solution.py:28
  28.9 8.5 %collective-permute-start.15 = (f32[512,64]{1,0:T(8,128)S(1)}, f32[512,64]{1,0:T(8,128)S(1)}, u32[]{:S(2)}, u32[]{:S(2)}) collective-permute-start(f32[512,64]{1,0:T(8,128)S(1)} %get-tuple-element.17), channel_id=1, source_target_pairs={{0,16},{8,24},{16,0},{24,8},{1,17},{9,25},{17,1},{25,9},{2,18},{10... | collective-permute-start | bytes 393224 | tf_op jit(solution)/shard_map/ppermute | solution.py:28
  30.4 8.7 %collective-permute-start.10 = (f32[128,256]{1,0:T(8,128)S(1)}, f32[128,256]{1,0:T(8,128)S(1)}, u32[]{:S(2)}, u32[]{:S(2)}) collective-permute-start(f32[128,256]{1,0:T(8,128)S(1)} %slice.21.refs_0_), channel_id=1, source_target_pairs={{0,3},{1,2},{2,1},{3,0},{4,7},{5,6},{6,5},{7,4},{8,11},{9,10},{10,... | collective-permute-start | bytes 393224 | tf_op jit(solution)/shard_map/ppermute | solution.py:28
  33.1 8.1 %collective-permute-start.9 = (f32[128,256]{1,0:T(8,128)S(1)}, f32[128,256]{1,0:T(8,128)S(1)}, u32[]{:S(2)}, u32[]{:S(2)}) collective-permute-start(f32[128,256]{1,0:T(8,128)S(1)} %slice.21.refs_0_), channel_id=1, source_target_pairs={{0,2},{1,3},{2,0},{3,1},{4,6},{5,7},{6,4},{7,5},{8,10},{9,11},{10,... | collective-permute-start | bytes 393224 | tf_op jit(solution)/shard_map/ppermute | solution.py:28
  33.1 8.1 %collective-permute-start.8 = (f32[128,256]{1,0:T(8,128)S(1)}, f32[128,256]{1,0:T(8,128)S(1)}, u32[]{:S(2)}, u32[]{:S(2)}) collective-permute-start(f32[128,256]{1,0:T(8,128)S(1)} %slice.21.refs_0_), channel_id=1, source_target_pairs={{0,1},{1,0},{2,3},{3,2},{4,5},{5,4},{6,7},{7,6},{8,9},{9,8},{10,11... | collective-permute-start | bytes 393224 | tf_op jit(solution)/shard_map/ppermute | solution.py:28
  35.5 8.5 %collective-permute-start.14 = (f32[128,256]{1,0:T(8,128)S(1)}, f32[128,256]{1,0:T(8,128)S(1)}, u32[]{:S(2)}, u32[]{:S(2)}) collective-permute-start(f32[128,256]{1,0:T(8,128)S(1)} %collective-permute-done.11.refs_4_), channel_id=1, source_target_pairs={{0,3},{1,2},{2,1},{3,0},{4,7},{5,6},{6,5},{7,4},{8,11},{9,10},{10,... | collective-permute-start | bytes 393224 | tf_op jit(solution)/shard_map/ppermute | solution.py:28
  37.3 9.3 %collective-permute-start.13 = (f32[128,256]{1,0:T(8,128)S(1)}, f32[128,256]{1,0:T(8,128)S(1)}, u32[]{:S(2)}, u32[]{:S(2)}) collective-permute-start(f32[128,256]{1,0:T(8,128)S(1)} %collective-permute-done.11.refs_4_), channel_id=1, source_target_pairs={{0,2},{1,3},{2,0},{3,1},{4,6},{5,7},{6,4},{7,5},{8,10},{9,11},{10,... | collective-permute-start | bytes 393224 | tf_op jit(solution)/shard_map/ppermute | solution.py:28
  39.2 7.4 %collective-permute-start.12 = (f32[128,256]{1,0:T(8,128)S(1)}, f32[128,256]{1,0:T(8,128)S(1)}, u32[]{:S(2)}, u32[]{:S(2)}) collective-permute-start(f32[128,256]{1,0:T(8,128)S(1)} %collective-permute-done.11.refs_4_), channel_id=1, source_target_pairs={{0,1},{1,0},{2,3},{3,2},{4,5},{5,4},{6,7},{7,6},{8,9},{9,8},{10,11... | collective-permute-start | bytes 393224 | tf_op jit(solution)/shard_map/ppermute | solution.py:28
  41.2 5.4 %collective-permute-start.16 = (f32[512,64]{1,0:T(8,128)S(1)}, f32[512,64]{1,0:T(8,128)S(1)}, u32[]{:S(2)}, u32[]{:S(2)}) collective-permute-start(f32[512,64]{1,0:T(8,128)S(1)} %pad_maximum_fusion.refs_8_), channel_id=1, source_target_pairs={{0,8},{8,0},{16,24},{24,16},{1,9},{9,1},{17,25},{25,17},{2,10},{10... | collective-permute-start | bytes 393224 | tf_op jit(solution)/shard_map/ppermute | solution.py:28
  50.2 1.6 %collective-permute-start.17 = (f32[512,64]{1,0:T(8,128)S(1)}, f32[512,64]{1,0:T(8,128)S(1)}, u32[]{:S(2)}, u32[]{:S(2)}) collective-permute-start(f32[512,64]{1,0:T(8,128)S(1)} %get-tuple-element.19), channel_id=1, source_target_pairs={{0,8},{8,0},{16,24},{24,16},{1,9},{9,1},{17,25},{25,17},{2,10},{10... | collective-permute-start | bytes 393224 | tf_op jit(solution)/shard_map/ppermute | solution.py:28
  51.9 8.4 %collective-permute-start.18 = (f32[512,64]{1,0:T(8,128)S(1)}, f32[512,64]{1,0:T(8,128)S(1)}, u32[]{:S(2)}, u32[]{:S(2)}) collective-permute-start(f32[512,64]{1,0:T(8,128)S(1)} %pad_maximum_fusion.1), channel_id=1, source_target_pairs={{0,16},{8,24},{16,0},{24,8},{1,17},{9,25},{17,1},{25,9},{2,18},{10... | collective-permute-start | bytes 393224 | tf_op jit(solution)/shard_map/ppermute | solution.py:28
  61.6 1.6 %collective-permute-start.19 = (f32[512,64]{1,0:T(8,128)S(1)}, f32[512,64]{1,0:T(8,128)S(1)}, u32[]{:S(2)}, u32[]{:S(2)}) collective-permute-start(f32[512,64]{1,0:T(8,128)S(1)} %get-tuple-element.21), channel_id=1, source_target_pairs={{0,8},{8,0},{16,24},{24,16},{1,9},{9,1},{17,25},{25,17},{2,10},{10... | collective-permute-start | bytes 393224 | tf_op jit(solution)/shard_map/ppermute | solution.py:28

commit v3 on v2

--- a/solution.py
+++ b/solution.py
@@ -28,15 +28,37 @@
     return lax.ppermute(block, axis, [(i, i ^ mask) for i in range(count)])
 
 
+def ring_place(blk, count):
+    return jnp.where(blk % 2 == 0, blk // 2, count - 1 - blk // 2)
+
+
+def ring_group(place, count):
+    return jnp.where(place < count // 2, 2 * place, 2 * (count - 1 - place) + 1)
+
+
+def ring_step(block):
+    cubes, count = lax.axis_size("cube"), lax.axis_size("blk")
+    order = list(range(0, count, 2)) + list(range(count - 1, 0, -2))
+    route = [
+        (c * count + order[i], c * count + order[(i + 1 - 2 * (c % 2)) % count])
+        for c in range(cubes)
+        for i in range(count)
+    ]
+    return lax.ppermute(block, ("cube", "blk"), route)
+
+
+def ring_offsets(count):
+    return [0] + [x for r in range(1, count // 2) for x in (r, -r)] + [count // 2]
+
+
 def gather_rows(block):
-    half = lax.axis_size("blk") // 2
-    far = swap(block, "blk", half)
-    near = {m: swap(block, "blk", m) for m in reversed(range(1, half))}
-    out = {0: block, half: far}
-    for m in reversed(range(1, half)):
-        out[m] = near[m]
-        out[m + half] = swap(far, "blk", m)
-    return [out[m] for m in range(2 * half)]
+    height = block.shape[0]
+    moving = jnp.concatenate([block, swap(block, "cube", 1)], axis=0)
+    out = [block]
+    for _ in range(1, lax.axis_size("blk") // 2):
+        moving = ring_step(moving)
+        out += [moving[:height], swap(moving[height:], "cube", 1)]
+    return out + [ring_step(moving[:height])]
 
 
 class Packing:
@@ -70,160 +92,206 @@
             axis=0,
         )
 
-    def diag(self, pieces, level, first=None):
+    def diag(self, pieces, level, diag_ref, first=None):
         first = (2**level - 1) * self.rows if first is None else first
-        return jnp.concatenate(
-            [
-                q[first + p * self.rows : first + (p + 1) * self.rows, :]
-                for p in range(2**level)
-                for q in pieces
-            ],
-            axis=0,
-        )
-
-
-def pack_kernel(pk, rhs_ref, panels_ref, maps_ref, diag_ref, out_ref):
-    rows, cols = pk.rows, pk.cols
-    out_ref[: pk.top, :] = diag_ref[: pk.top, :]
-    parts = [rhs_ref[l] for l in range(pk.levels - 1)]
+        for m, piece in enumerate(pieces):
+            for p in range(2**level):
+                diag_ref[block_of(self, m, p), :] = piece[first + p * self.rows : first + (p + 1) * self.rows, :]
+
+
+def pack_kernel(pk, rhs_hbm, panels_hbm, maps_hbm, diag_hbm, out_ref, last_ref, rhs_ref, panels_ref, maps_ref, sems):
+    rows = pk.rows
+    pairs = [
+        (rhs_hbm, rhs_ref),
+        (panels_hbm, panels_ref),
+        (maps_hbm, maps_ref),
+        (diag_hbm.at[: pk.top], out_ref.at[: pk.top]),
+        (diag_hbm.at[pk.top :], last_ref),
+    ]
+    copies = [pltpu.make_async_copy(a, b, sems.at[i]) for i, (a, b) in enumerate(pairs)]
+    for copy in copies:
+        copy.start()
+    for copy in copies[:3]:
+        copy.wait()
+    parts = [rhs_ref[l, 0, 0] for l in range(pk.levels - 1)]
     for l in range(pk.levels - 1):
         for h in (0, 1):
-            panel = panels_ref[l, h]
+            panel = panels_ref[l, 0, 0, h]
             row_ids = lax.broadcasted_iota(jnp.int32, (rows, panel.shape[0]), 0)
-            names = maps_ref[2 * l + h : 2 * l + h + 1, :]
+            names = maps_ref[l, 0, 0, h : h + 1, :]
             onehot = jnp.where(row_ids == names, 1.0, 0.0).astype(jnp.float32)
             parts.append(dot(onehot, panel))
     out_ref[pk.top : pk.top + rows, :] = jnp.concatenate(parts, axis=1)
-    last = rhs_ref[pk.levels - 1]
+    last = rhs_ref[pk.levels - 1, 0, 0]
     step = rows // pk.fold
     out_ref[pk.top + rows :, :] = jnp.concatenate(
         [last[j * step : (j + 1) * step] for j in range(pk.fold)], axis=1
     )
-
-
-def block_of(pk, m):
-    place = (lax.axis_index("blk") ^ m) * pk.rows
-    return pl.ds(pl.multiple_of(place, pk.rows), pk.rows)
+    for copy in copies[3:]:
+        copy.wait()
+
+
+def block_of(pk, m, p=0):
+    count = pk.n_blk
+    place = ring_place(lax.axis_index("blk"), count)
+    turn = ring_offsets(count)[m] * (1 - 2 * (lax.axis_index("cube") % 2))
+    group = ring_group((place - turn + count) % count, count)
+    return pl.ds(pl.multiple_of(p * pk.width + group * pk.rows, pk.rows), pk.rows)
 
 
 def extend_out(pk, level, pieces, y_ref, send_ref):
-    rows, node = pk.rows, pk.width
+    rows, cols = pk.rows, pk.cols
     for m, piece in enumerate(pieces):
-        e = dot(pk.extend(piece, level), y_ref[block_of(pk, m), :])
-        send_ref[m * rows : (m + 1) * rows, :] = pk.rhs(piece, level + 1) - e[:rows]
-        send_ref[node + m * rows : node + (m + 1) * rows, :] = e[rows:]
+        place = block_of(pk, m)
+        e = dot(pk.extend(piece, level), y_ref[place, :])
+        send_ref[place, :cols] = pk.rhs(piece, level + 1) - e[:rows]
+        send_ref[place, cols:] = e[rows:]
 
 
 def first_kernel(pk, *refs):
-    pieces, (send_ref, y_ref) = refs[: pk.n_blk], refs[pk.n_blk :]
-    z = jnp.concatenate([pk.rhs(q, 0) for q in pieces], axis=0)
-    y_ref[...] = dot_t(pk.diag(pieces, 0), z)
+    pieces, (send_ref, y_ref, diag_ref, z_ref) = refs[: pk.n_blk], refs[pk.n_blk :]
+    pk.diag(pieces, 0, diag_ref)
+    for m, piece in enumerate(pieces):
+        z_ref[block_of(pk, m), :] = pk.rhs(piece, 0)
+    y_ref[...] = dot_t(diag_ref[...], z_ref[...])
     extend_out(pk, 0, pieces, y_ref, send_ref)
 
 
 def middle_kernel(pk, *refs):
-    pieces, (mine_ref, got_ref, send_ref, y_ref) = refs[: pk.n_blk], refs[pk.n_blk :]
-    node = pk.width
-    own = mine_ref[:node] - got_ref[node:]
-    other = got_ref[:node] - mine_ref[node:]
+    pieces, (mine_ref, got_ref, send_ref, y_ref, diag_ref) = refs[: pk.n_blk], refs[pk.n_blk :]
+    cols = pk.cols
+    own = mine_ref[:, :cols] - got_ref[:, cols:]
+    other = got_ref[:, :cols] - mine_ref[:, cols:]
     upper = lax.axis_index("cube") % 2 == 1
     z = jnp.concatenate([jnp.where(upper, other, own), jnp.where(upper, own, other)], axis=0)
-    y_ref[...] = dot_t(pk.diag(pieces, 1), z)
+    pk.diag(pieces, 1, diag_ref)
+    y_ref[...] = dot_t(diag_ref[...], z)
     extend_out(pk, 1, pieces, y_ref, send_ref)
 
 
+def meet_kernel(pk, mine_ref, got_ref, out_ref):
+    cols = pk.cols
+    out_ref[:, :cols] = mine_ref[:, :cols] - got_ref[:, cols:]
+    out_ref[:, cols:] = got_ref[:, :cols] - mine_ref[:, cols:]
+
+
 def top_kernel(pk, *refs):
-    pieces, (mine_ref, got_ref, keep_ref, send_ref, vec_ref) = refs[: pk.n_blk], refs[pk.n_blk :]
-    node = pk.width
+    pieces, (mine_ref, got_ref, keep_ref, send_ref, diag_ref, vec_ref) = refs[: pk.n_blk], refs[pk.n_blk :]
+    node, cols = pk.width, pk.cols
     cube = lax.axis_index("cube")
 
     def part(k):
         return pl.ds(pl.multiple_of((cube ^ k) * node, node), node)
 
-    vec_ref[part(0), :] = mine_ref[:node]
-    vec_ref[part(2), :] = mine_ref[node:]
-    vec_ref[part(1), :] = got_ref[:node]
-    vec_ref[part(3), :] = got_ref[node:]
-    diag = pk.diag(pieces, 2, 0)
+    pk.diag(pieces, 2, diag_ref, 0)
+    vec_ref[part(0), :] = mine_ref[:, :cols]
+    vec_ref[part(2), :] = mine_ref[:, cols:]
+    vec_ref[part(1), :] = got_ref[:, :cols]
+    vec_ref[part(3), :] = got_ref[:, cols:]
+    diag = diag_ref[...]
     vec_ref[...] = dot(diag, dot_t(diag, vec_ref[...]))
-    keep_ref[:node] = vec_ref[part(0), :]
-    keep_ref[node:] = vec_ref[part(2), :]
-    send_ref[:node] = vec_ref[part(1), :]
-    send_ref[node:] = vec_ref[part(3), :]
-
-
-def reduce_rows(pk, level, pieces, y_ref, pair, w_ref):
-    rows, node = pk.rows, pk.width
+    keep_ref[:, :cols] = vec_ref[part(0), :]
+    keep_ref[:, cols:] = vec_ref[part(2), :]
+    send_ref[:, :cols] = vec_ref[part(1), :]
+    send_ref[:, cols:] = vec_ref[part(3), :]
+
+
+def turn_kernel(pk, mine_ref, got_ref, held_ref, send_ref):
+    cols = pk.cols
+    held = mine_ref[...] + got_ref[...]
+    held_ref[...] = held
+    send_ref[:, :cols] = held[:, cols:]
+    send_ref[:, cols:] = held[:, :cols]
+
+
+def reduce_rows(pk, level, pieces, y_ref, mine_ref, got_ref, w_ref):
+    cols = pk.cols
     for m, piece in enumerate(pieces):
-        both = jnp.concatenate(
-            [pair[m * rows : (m + 1) * rows], pair[node + m * rows : node + (m + 1) * rows]], axis=0
-        )
         place = block_of(pk, m)
+        pair = mine_ref[place, :] + got_ref[place, :]
+        both = jnp.concatenate([pair[:, :cols], pair[:, cols:]], axis=0)
         w_ref[place, :] = y_ref[place, :] - dot_t(pk.extend(piece, level), both)
 
 
 def down_kernel(pk, *refs):
-    pieces, (y_ref, mine_ref, got_ref, keep_ref, send_ref, top_ref, w_ref) = refs[: pk.n_blk], refs[pk.n_blk :]
-    node = pk.width
-    pair = mine_ref[...] + got_ref[...]
-    top_ref[...] = pair[: pk.rows]
-    reduce_rows(pk, 1, pieces, y_ref, pair, w_ref)
-    x = dot(pk.diag(pieces, 1), w_ref[...])
+    pieces, refs = refs[: pk.n_blk], refs[pk.n_blk :]
+    y_ref, mine_ref, got_ref, keep_ref, send_ref, top_ref, w_ref, diag_ref = refs
+    node, cols = pk.width, pk.cols
+    own_rows = block_of(pk, 0)
+    top_ref[...] = mine_ref[own_rows, :cols] + got_ref[own_rows, :cols]
+    pk.diag(pieces, 1, diag_ref)
+    reduce_rows(pk, 1, pieces, y_ref, mine_ref, got_ref, w_ref)
+    x = dot(diag_ref[...], w_ref[...])
     upper = lax.axis_index("cube") % 2 == 1
     own = jnp.where(upper, x[node:], x[:node])
     other = jnp.where(upper, x[:node], x[node:])
-    keep_ref[:node] = own
-    keep_ref[node:] = other
-    send_ref[:node] = other
-    send_ref[node:] = own
+    keep_ref[:, :cols] = own
+    keep_ref[:, cols:] = other
+    send_ref[:, :cols] = other
+    send_ref[:, cols:] = own
 
 
 def last_kernel(pk, *refs):
     pieces, (y_ref, mine_ref, got_ref, top_ref, out_ref, w_ref) = refs[: pk.n_blk], refs[pk.n_blk :]
-    pair = mine_ref[...] + got_ref[...]
+    cols = pk.cols
+    own_rows = block_of(pk, 0)
     out_ref[2] = top_ref[...]
-    out_ref[1] = pair[: pk.rows]
-    reduce_rows(pk, 0, pieces, y_ref, pair, w_ref)
+    out_ref[1] = mine_ref[own_rows, :cols] + got_ref[own_rows, :cols]
+    reduce_rows(pk, 0, pieces, y_ref, mine_ref, got_ref, w_ref)
     out_ref[0] = dot(pieces[0][: pk.rows, :], w_ref[...])
 
 
-def call(kernel, pk, args, outs, scratch=()):
+def call(kernel, pk, args, outs, scratch=(), place=pltpu.VMEM, room=24):
     vmem = pl.BlockSpec(memory_space=pltpu.VMEM)
     return pl.pallas_call(
         functools.partial(kernel, pk),
         out_shape=[jax.ShapeDtypeStruct(s, jnp.float32) for s in outs],
-        in_specs=[vmem] * len(args),
+        in_specs=[pl.BlockSpec(memory_space=place)] * len(args),
         out_specs=[vmem] * len(outs),
-        scratch_shapes=[pltpu.VMEM(s, jnp.float32) for s in scratch],
-        compiler_params=pltpu.CompilerParams(vmem_limit_bytes=24 * 2**20),
+        scratch_shapes=scratch,
+        compiler_params=pltpu.CompilerParams(vmem_limit_bytes=room * 2**20),
     )(*args)
+
+
+def tie(value, other):
+    return lax.optimization_barrier((value, other))[0]
 
 
 def gathered(pk, right_side, diag_inverse, panels, extend_map):
     rows, cols, node = pk.rows, pk.cols, pk.width
-    one, two = (node, cols), (2 * node, cols)
-    maps = extend_map.reshape(-1, extend_map.shape[-1])
-    (packed,) = call(
+    one, two = (node, cols), (node, 2 * cols)
+
+    def work(*shapes):
+        return [pltpu.VMEM(s, jnp.float32) for s in shapes]
+
+    inputs = [right_side, panels, extend_map, diag_inverse]
+    packed, top = call(
         pack_kernel,
         pk,
-        [right_side[:, 0, 0], panels[:, 0, 0], maps, diag_inverse],
-        [(pk.height, pk.width)],
+        inputs,
+        [(pk.height, node), (diag_inverse.shape[0] - pk.top, node)],
+        [pltpu.VMEM(a.shape, a.dtype) for a in inputs[:3]] + [pltpu.SemaphoreType.DMA((5,))],
+        pltpu.HBM,
+        60,
     )
     first = gather_rows(packed)
-    last = gather_rows(diag_inverse[pk.top :])
-
-    send, y0 = call(first_kernel, pk, first, [two, one])
+    last = gather_rows(top)
+    send, y0 = call(first_kernel, pk, first, [two, one], work((node, node), one))
     got = swap(send, "cube", 1)
-    send, y1 = call(middle_kernel, pk, [*first, send, got], [two, one])
+    send, y1 = call(middle_kernel, pk, [*first, send, got], [two, one], work((2 * node, node)))
     got = swap(send, "cube", 2)
-    held = jnp.concatenate([send[:node] - got[node:], got[:node] - send[node:]], axis=0)
+    (held,) = call(meet_kernel, pk, [send, got], [two])
     got = swap(held, "cube", 1)
-    keep, send = call(top_kernel, pk, [*last, held, got], [two, two], [(4 * node, cols)])
-    held = keep + swap(send, "cube", 1)
-    got = swap(jnp.concatenate([held[node:], held[:node]], axis=0), "cube", 2)
-    keep, send, top = call(down_kernel, pk, [*first, y1, held, got], [two, two, (rows, cols)], [one])
+    keep, send = call(
+        top_kernel, pk, [*last, held, got], [two, two], work((4 * node, node), (4 * node, cols))
+    )
+    held, send = call(turn_kernel, pk, [keep, swap(send, "cube", 1)], [two, two])
+    got = swap(send, "cube", 2)
+    keep, send, top = call(
+        down_kernel, pk, [*first, y1, held, got], [two, two, (rows, cols)], work(one, (2 * node, node))
+    )
     got = swap(send, "cube", 1)
-    (out,) = call(last_kernel, pk, [*first, y0, keep, got, top], [(3, rows, cols)], [one])
+    (out,) = call(last_kernel, pk, [*first, y0, keep, got, top], [(3, rows, cols)], work(one))
     return out[:, None, None]
 
 

time: 64.8 us -> 57.1 us (0.88)
  waiting for transfers between devices: 28.9 us -> 22.7 us
  local copies, waits for them, and re-layouts: 3.2 us -> 0.12 us
  Pallas kernels: 9.04 us -> 11.4 us
  starting transfers between devices: 23.2 us -> 21.6 us
  other arithmetic: 0.1 us -> 0.94 us
    ppermute x20 -> x14, starting transfers between devices: 23.2 us -> 5.75 us  [swap(): return lax.ppermute(block, axis, [(i, i ^ mask) for i in range(count)])]
    ppermute x20 -> x14, waiting for transfers between devices: 28.9 us -> 12 us  [swap(): return lax.ppermute(block, axis, [(i, i ^ mask) for i in range(count)])]
    ppermute x0 -> x8, starting transfers between devices: none -> 15.8 us  [ring_step(): return lax.ppermute(block, ('cube', 'blk'), route)]
    ppermute x0 -> x8, waiting for transfers between devices: none -> 10.7 us  [ring_step(): return lax.ppermute(block, ('cube', 'blk'), route)]
    unnamed x8 -> x4, local copies, waits for them, and re-layouts: 3.17 us -> 0.01 us
    pallas_call x6 -> x8, Pallas kernels: 9.04 us -> 11.4 us  [call(): pl.pallas_call(functools.partial(kernel, pk), out_shape=[jax.ShapeDtypeSt...]
    concatenate x2, other arithmetic: 0.04 us -> 0.94 us  [gather_rows(): moving = jnp.concatenate([block, swap(block, 'cube', 1)], axis=0)]
  transfers between devices with their start and end apart: 20 -> 22, of which waited for: 12 -> 15; matrix products, arithmetic and copies ran while one was open for 0% -> 0% of each run, Pallas kernels for 2% -> 5%
where the time goes in v3:
time: 57.1 us; the launch traced here: 56.9 us
  waiting for transfers between devices  22.7 us (40%)
  starting transfers between devices  21.6 us (38%)
  Pallas kernels  11.4 us (20%)
  other arithmetic  0.94 us (2%)
    ppermute x8, starting transfers between devices, ring_step(): return lax.ppermute(block, ('cube', 'blk'), route)  15.8 us
    ppermute x14, waiting for transfers between devices, swap(): return lax.ppermute(block, axis, [(i, i ^ mask) for i in range(count)])  12 us
    pallas_call x8, Pallas kernels, call(): pl.pallas_call(functools.partial(kernel, pk), out_shape=[jax.ShapeDtypeSt...  11.4 us
    ppermute x8, waiting for transfers between devices, ring_step(): return lax.ppermute(block, ('cube', 'blk'), route)  10.7 us
    ppermute x14, starting transfers between devices, swap(): return lax.ppermute(block, axis, [(i, i ^ mask) for i in range(count)])  5.75 us
  transfers between devices with their start and end apart: 22, of which 15 were waited for; matrix products, arithmetic and copies ran while one was open for 0% of the time, Pallas kernels for 5%

profile of v3, /device:TPU:0, one launch (start us, length us, event | category | flops | bytes accessed | tf_op | source)
XLA Modules:
  0.0 56.9 jit_solution(7237148821063932036)
XLA Ops:
  0.0 1.8 %shard_map.46 = (f32[136,256]{1,0:T(8,128)}, f32[128,256]{1,0:T(8,128)}) custom-call(f32[3,1,1,32,64]{4,3,2,1,0:T(8,128)} %rhs_hbm.1, f32[2,1,1,2,16,32]{5,4,3,2,1,0:T(8,128)} %panels_hbm.1, s32[2,1,1,2,16]{4,3,2,1,0:T(2,128)} %maps_hbm.1, f32[224,256]{1,0:T(8,128)} %diag_hbm.1), custom_call_target="tpu_custom_call" | custom-call | tf_op jit(solution)/shard_map/pallas_call | solution.py:246
  4.5 3.0 %collective-permute-start.1 = (f32[272,256]{1,0:T(8,128)S(1)}, f32[272,256]{1,0:T(8,128)S(1)}, u32[]{:S(2)}, u32[]{:S(2)}) collective-permute-start(f32[272,256]{1,0:T(8,128)S(1)} %pad_maximum_fusion), channel_id=1, source_target_pairs={{0,2},{2,4},{4,6},{6,7},{7,5},{5,3},{3,1},{1,0},{8,9},{10,8},{12,1... | collective-permute-start | bytes 835592 | tf_op jit(solution)/shard_map/ppermute | solution.py:47
  7.5 1.3 %collective-permute-done.9 = f32[128,256]{1,0:T(8,128)S(1)} collective-permute-done((f32[128,256]{1,0:T(8,128)S(1)}, f32[128,256]{1,0:T(8,128)S(1)}, u32[]{:S(2)}, u32[]{:S(2)}) %collective-permute-start.9) | collective-permute-done | bytes 131104 | tf_op jit(solution)/shard_map/ppermute | solution.py:28
  8.9 1.6 %collective-permute-start.10 = (f32[256,256]{1,0:T(8,128)S(1)}, f32[256,256]{1,0:T(8,128)S(1)}, u32[]{:S(2)}, u32[]{:S(2)}) collective-permute-start(f32[256,256]{1,0:T(8,128)S(1)} %pad_maximum_fusion.1), channel_id=1, source_target_pairs={{0,2},{2,4},{4,6},{6,7},{7,5},{5,3},{3,1},{1,0},{8,9},{10,8},{12,1... | collective-permute-start | bytes 786440 | tf_op jit(solution)/shard_map/ppermute | solution.py:47
  10.5 1.5 %collective-permute-done.1 = f32[272,256]{1,0:T(8,128)S(1)} collective-permute-done((f32[272,256]{1,0:T(8,128)S(1)}, f32[272,256]{1,0:T(8,128)S(1)}, u32[]{:S(2)}, u32[]{:S(2)}) %collective-permute-start.1) | collective-permute-done | bytes 278560 | tf_op jit(solution)/shard_map/ppermute | solution.py:47
  12.0 2.1 %collective-permute-start.3 = (f32[272,256]{1,0:T(8,128)S(1)}, f32[272,256]{1,0:T(8,128)S(1)}, u32[]{:S(2)}, u32[]{:S(2)}) collective-permute-start(f32[272,256]{1,0:T(8,128)S(1)} %collective-permute-done.1), channel_id=1, source_target_pairs={{0,2},{2,4},{4,6},{6,7},{7,5},{5,3},{3,1},{1,0},{8,9},{10,8},{12,1... | collective-permute-start | bytes 835592 | tf_op jit(solution)/shard_map/ppermute | solution.py:47
  15.3 1.6 %collective-permute-start.12 = (f32[256,256]{1,0:T(8,128)S(1)}, f32[256,256]{1,0:T(8,128)S(1)}, u32[]{:S(2)}, u32[]{:S(2)}) collective-permute-start(f32[256,256]{1,0:T(8,128)S(1)} %collective-permute-done.10), channel_id=1, source_target_pairs={{0,2},{2,4},{4,6},{6,7},{7,5},{5,3},{3,1},{1,0},{8,9},{10,8},{12,1... | collective-permute-start | bytes 786440 | tf_op jit(solution)/shard_map/ppermute | solution.py:47
  16.9 1.6 %collective-permute-done.3 = f32[272,256]{1,0:T(8,128)S(1)} collective-permute-done((f32[272,256]{1,0:T(8,128)S(1)}, f32[272,256]{1,0:T(8,128)S(1)}, u32[]{:S(2)}, u32[]{:S(2)}) %collective-permute-start.3) | collective-permute-done | bytes 278560 | tf_op jit(solution)/shard_map/ppermute | solution.py:47
  18.5 2.1 %collective-permute-start.5 = (f32[272,256]{1,0:T(8,128)S(1)}, f32[272,256]{1,0:T(8,128)S(1)}, u32[]{:S(2)}, u32[]{:S(2)}) collective-permute-start(f32[272,256]{1,0:T(8,128)S(1)} %collective-permute-done.3), channel_id=1, source_target_pairs={{0,2},{2,4},{4,6},{6,7},{7,5},{5,3},{3,1},{1,0},{8,9},{10,8},{12,1... | collective-permute-start | bytes 835592 | tf_op jit(solution)/shard_map/ppermute | solution.py:47
  21.7 1.7 %collective-permute-start.14 = (f32[256,256]{1,0:T(8,128)S(1)}, f32[256,256]{1,0:T(8,128)S(1)}, u32[]{:S(2)}, u32[]{:S(2)}) collective-permute-start(f32[256,256]{1,0:T(8,128)S(1)} %collective-permute-done.12), channel_id=1, source_target_pairs={{0,2},{2,4},{4,6},{6,7},{7,5},{5,3},{3,1},{1,0},{8,9},{10,8},{12,1... | collective-permute-start | bytes 786440 | tf_op jit(solution)/shard_map/ppermute | solution.py:47
  23.5 1.6 %collective-permute-done.5 = f32[272,256]{1,0:T(8,128)S(1)} collective-permute-done((f32[272,256]{1,0:T(8,128)S(1)}, f32[272,256]{1,0:T(8,128)S(1)}, u32[]{:S(2)}, u32[]{:S(2)}) %collective-permute-start.5) | collective-permute-done | bytes 278560 | tf_op jit(solution)/shard_map/ppermute | solution.py:47
  25.2 2.1 %collective-permute-start.7 = (f32[136,256]{1,0:T(8,128)S(1)}, f32[136,256]{1,0:T(8,128)S(1)}, u32[]{:S(2)}, u32[]{:S(2)}) collective-permute-start(f32[136,256]{1,0:T(8,128)S(1)} %get-tuple-element.32.refs_5_), channel_id=1, source_target_pairs={{0,2},{2,4},{4,6},{6,7},{7,5},{5,3},{3,1},{1,0},{8,9},{10,8},{12,1... | collective-permute-start | bytes 417800 | tf_op jit(solution)/shard_map/ppermute | solution.py:47
  27.5 2.8 %collective-permute-done.7.refs_7_ = f32[136,256]{1,0:T(8,128)S(1)} collective-permute-done((f32[136,256]{1,0:T(8,128)S(1)}, f32[136,256]{1,0:T(8,128)S(1)}, u32[]{:S(2)}, u32[]{:S(2)}) %collective-permute-start.7) | collective-permute-done | bytes 139296 | tf_op jit(solution)/shard_map/ppermute | solution.py:47
  30.3 1.3 %shard_map.47 = (f32[256,128]{1,0:T(8,128)S(1)}, f32[256,64]{1,0:T(8,128)S(1)}) custom-call(f32[136,256]{1,0:T(8,128)S(1)} %copy-done, f32[136,256]{1,0:T(8,128)S(1)} %get-tuple-element.36.refs_1_, f32[136,256]{1,0:T(8,128)S(1)} %collective-permute-done.2.refs_2_, f32[136,256]{1,0:T(8,128)S(1)} %get-tuple-element.34.refs_3_, ...), custom_call_target="tpu_custom_call" | custom-call | tf_op jit(solution)/shard_map/pallas_call | solution.py:246
  33.0 1.5 %shard_map.48 = (f32[256,128]{1,0:T(8,128)S(1)}, f32[256,64]{1,0:T(8,128)S(1)}) custom-call(f32[136,256]{1,0:T(8,128)S(1)} %copy-done, f32[136,256]{1,0:T(8,128)S(1)} %get-tuple-element.36.refs_1_, f32[136,256]{1,0:T(8,128)S(1)} %collective-permute-done.2.refs_2_, f32[136,256]{1,0:T(8,128)S(1)} %get-tuple-element.34.refs_3_, ...), custom_call_target="tpu_custom_call" | custom-call | tf_op jit(solution)/shard_map/pallas_call | solution.py:246
  34.5 2.0 %collective-permute-start.17 = (f32[256,128]{1,0:T(8,128)S(1)}, f32[256,128]{1,0:T(8,128)S(1)}, u32[]{:S(2)}, u32[]{:S(2)}) collective-permute-start(f32[256,128]{1,0:T(8,128)S(1)} %get-tuple-element.23.mine_ref), channel_id=1, source_target_pairs={{0,16},{8,24},{16,0},{24,8},{1,17},{9,25},{17,1},{25,9},{2,18},{10... | collective-permute-start | bytes 393224 | tf_op jit(solution)/shard_map/ppermute | solution.py:28
  36.6 1.6 %collective-permute-start.16 = (f32[128,256]{1,0:T(8,128)S(1)}, f32[128,256]{1,0:T(8,128)S(1)}, u32[]{:S(2)}, u32[]{:S(2)}) collective-permute-start(f32[128,256]{1,0:T(8,128)S(1)} %get-tuple-element.38.refs_5_), channel_id=1, source_target_pairs={{0,2},{2,4},{4,6},{6,7},{7,5},{5,3},{3,1},{1,0},{8,9},{10,8},{12,1... | collective-permute-start | bytes 393224 | tf_op jit(solution)/shard_map/ppermute | solution.py:47
  38.2 2.1 %collective-permute-done.17.got_ref = f32[256,128]{1,0:T(8,128)S(1)} collective-permute-done((f32[256,128]{1,0:T(8,128)S(1)}, f32[256,128]{1,0:T(8,128)S(1)}, u32[]{:S(2)}, u32[]{:S(2)}) %collective-permute-start.17) | collective-permute-done | bytes 131104 | tf_op jit(solution)/shard_map/ppermute | solution.py:28
  41.9 3.8 %shard_map.50 = (f32[256,128]{1,0:T(8,128)S(1)}, f32[256,128]{1,0:T(8,128)S(1)}) custom-call(f32[128,256]{1,0:T(8,128)S(1)} %copy-done.1, f32[128,256]{1,0:T(8,128)S(1)} %get-tuple-element.42.refs_1_, f32[128,256]{1,0:T(8,128)S(1)} %collective-permute-done.11.refs_2_, f32[128,256]{1,0:T(8,128)S(1)} %get-tuple-element.40.refs_3_, ...), custom_call_target="tpu_custom_call" | custom-call | tf_op jit(solution)/shard_map/pallas_call | solution.py:246
  47.3 1.8 %collective-permute-start.20 = (f32[256,128]{1,0:T(8,128)S(1)}, f32[256,128]{1,0:T(8,128)S(1)}, u32[]{:S(2)}, u32[]{:S(2)}) collective-permute-start(f32[256,128]{1,0:T(8,128)S(1)} %get-tuple-element.27), channel_id=1, source_target_pairs={{0,16},{8,24},{16,0},{24,8},{1,17},{9,25},{17,1},{25,9},{2,18},{10... | collective-permute-start | bytes 393224 | tf_op jit(solution)/shard_map/ppermute | solution.py:28
  49.1 3.8 %collective-permute-done.20.refs_10_ = f32[256,128]{1,0:T(8,128)S(1)} collective-permute-done((f32[256,128]{1,0:T(8,128)S(1)}, f32[256,128]{1,0:T(8,128)S(1)}, u32[]{:S(2)}, u32[]{:S(2)}) %collective-permute-start.20) | collective-permute-done | bytes 131104 | tf_op jit(solution)/shard_map/ppermute | solution.py:28
  52.9 1.3 %shard_map.52 = (f32[256,128]{1,0:T(8,128)S(1)}, f32[256,128]{1,0:T(8,128)S(1)}, f32[32,64]{1,0:T(8,128)S(1)}) custom-call(f32[136,256]{1,0:T(8,128)S(1)} %copy-done, f32[136,256]{1,0:T(8,128)S(1)} %get-tuple-element.36.refs_1_, f32[136,256]{1,0:T(8,128)S(1)} %collective-permute-done.2.refs_2_, f32[136,256]{1,0:T(8,128)S(1)} %get-tuple-element.34.refs_3_, ...), custom_call_target="tpu_custom_call" | custom-call | tf_op jit(solution)/shard_map/pallas_call | solution.py:246
  54.2 1.3 %collective-permute-done.21.refs_10_ = f32[256,128]{1,0:T(8,128)S(1)} collective-permute-done((f32[256,128]{1,0:T(8,128)S(1)}, f32[256,128]{1,0:T(8,128)S(1)}, u32[]{:S(2)}, u32[]{:S(2)}) %collective-permute-start.21) | collective-permute-done | bytes 131104 | tf_op jit(solution)/shard_map/ppermute | solution.py:28
  55.6 1.4 %shard_map.53 = f32[3,32,64]{2,1,0:T(8,128)} custom-call(f32[136,256]{1,0:T(8,128)S(1)} %copy-done, f32[136,256]{1,0:T(8,128)S(1)} %get-tuple-element.36.refs_1_, f32[136,256]{1,0:T(8,128)S(1)} %collective-permute-done.2.refs_2_, f32[136,256]{1,0:T(8,128)S(1)} %get-tuple-element.34.refs_3_, f32[136,256]{1,0:T(8,128)S(1)} %collective-permute-done.4.refs_4_, ...), custom_call_target="tpu_custom_call" | custom-call | tf_op jit(solution)/shard_map/pallas_call | solution.py:246
  (40 shorter events, 10.0 us)
Async XLA Ops:
  1.8 5.7 %copy-start.1 = (f32[128,256]{1,0:T(8,128)S(1)}, f32[128,256]{1,0:T(8,128)}, u32[]{:S(2)}) copy-start(f32[128,256]{1,0:T(8,128)} %get-tuple-element.22.refs_0_) | copy-start | bytes 393220
  1.9 1.7 %collective-permute-start = (f32[136,256]{1,0:T(8,128)}, f32[136,256]{1,0:T(8,128)S(1)}, u32[]{:S(2)}, u32[]{:S(2)}) collective-permute-start(f32[136,256]{1,0:T(8,128)} %get-tuple-element.18.refs_0_), channel_id=1, source_target_pairs={{0,8},{8,0},{16,24},{24,16},{1,9},{9,1},{17,25},{25,17},{2,10},{10... | collective-permute-start | bytes 417800 | tf_op jit(solution)/shard_map/ppermute | solution.py:28
  4.5 7.5 %collective-permute-start.1 = (f32[272,256]{1,0:T(8,128)S(1)}, f32[272,256]{1,0:T(8,128)S(1)}, u32[]{:S(2)}, u32[]{:S(2)}) collective-permute-start(f32[272,256]{1,0:T(8,128)S(1)} %pad_maximum_fusion), channel_id=1, source_target_pairs={{0,2},{2,4},{4,6},{6,7},{7,5},{5,3},{3,1},{1,0},{8,9},{10,8},{12,1... | collective-permute-start | bytes 835592 | tf_op jit(solution)/shard_map/ppermute | solution.py:47
  7.5 1.3 %collective-permute-start.9 = (f32[128,256]{1,0:T(8,128)S(1)}, f32[128,256]{1,0:T(8,128)S(1)}, u32[]{:S(2)}, u32[]{:S(2)}) collective-permute-start(f32[128,256]{1,0:T(8,128)S(1)} %copy-done.1), channel_id=1, source_target_pairs={{0,8},{8,0},{16,24},{24,16},{1,9},{9,1},{17,25},{25,17},{2,10},{10... | collective-permute-start | bytes 393224 | tf_op jit(solution)/shard_map/ppermute | solution.py:28
  8.9 6.4 %collective-permute-start.10 = (f32[256,256]{1,0:T(8,128)S(1)}, f32[256,256]{1,0:T(8,128)S(1)}, u32[]{:S(2)}, u32[]{:S(2)}) collective-permute-start(f32[256,256]{1,0:T(8,128)S(1)} %pad_maximum_fusion.1), channel_id=1, source_target_pairs={{0,2},{2,4},{4,6},{6,7},{7,5},{5,3},{3,1},{1,0},{8,9},{10,8},{12,1... | collective-permute-start | bytes 786440 | tf_op jit(solution)/shard_map/ppermute | solution.py:47
  12.0 6.5 %collective-permute-start.3 = (f32[272,256]{1,0:T(8,128)S(1)}, f32[272,256]{1,0:T(8,128)S(1)}, u32[]{:S(2)}, u32[]{:S(2)}) collective-permute-start(f32[272,256]{1,0:T(8,128)S(1)} %collective-permute-done.1), channel_id=1, source_target_pairs={{0,2},{2,4},{4,6},{6,7},{7,5},{5,3},{3,1},{1,0},{8,9},{10,8},{12,1... | collective-permute-start | bytes 835592 | tf_op jit(solution)/shard_map/ppermute | solution.py:47
  15.3 6.4 %collective-permute-start.12 = (f32[256,256]{1,0:T(8,128)S(1)}, f32[256,256]{1,0:T(8,128)S(1)}, u32[]{:S(2)}, u32[]{:S(2)}) collective-permute-start(f32[256,256]{1,0:T(8,128)S(1)} %collective-permute-done.10), channel_id=1, source_target_pairs={{0,2},{2,4},{4,6},{6,7},{7,5},{5,3},{3,1},{1,0},{8,9},{10,8},{12,1... | collective-permute-start | bytes 786440 | tf_op jit(solution)/shard_map/ppermute | solution.py:47
  18.5 6.5 %collective-permute-start.5 = (f32[272,256]{1,0:T(8,128)S(1)}, f32[272,256]{1,0:T(8,128)S(1)}, u32[]{:S(2)}, u32[]{:S(2)}) collective-permute-start(f32[272,256]{1,0:T(8,128)S(1)} %collective-permute-done.3), channel_id=1, source_target_pairs={{0,2},{2,4},{4,6},{6,7},{7,5},{5,3},{3,1},{1,0},{8,9},{10,8},{12,1... | collective-permute-start | bytes 835592 | tf_op jit(solution)/shard_map/ppermute | solution.py:47
  20.6 6.7 %collective-permute-start.2 = (f32[136,256]{1,0:T(8,128)S(1)}, f32[136,256]{1,0:T(8,128)S(1)}, u32[]{:S(2)}, u32[]{:S(2)}) collective-permute-start(f32[136,256]{1,0:T(8,128)S(1)} %get-tuple-element.35), channel_id=1, source_target_pairs={{0,8},{8,0},{16,24},{24,16},{1,9},{9,1},{17,25},{25,17},{2,10},{10... | collective-permute-start | bytes 417800 | tf_op jit(solution)/shard_map/ppermute | solution.py:28
  21.7 14.8 %collective-permute-start.14 = (f32[256,256]{1,0:T(8,128)S(1)}, f32[256,256]{1,0:T(8,128)S(1)}, u32[]{:S(2)}, u32[]{:S(2)}) collective-permute-start(f32[256,256]{1,0:T(8,128)S(1)} %collective-permute-done.12), channel_id=1, source_target_pairs={{0,2},{2,4},{4,6},{6,7},{7,5},{5,3},{3,1},{1,0},{8,9},{10,8},{12,1... | collective-permute-start | bytes 786440 | tf_op jit(solution)/shard_map/ppermute | solution.py:47
  23.4 4.1 %collective-permute-start.4 = (f32[136,256]{1,0:T(8,128)S(1)}, f32[136,256]{1,0:T(8,128)S(1)}, u32[]{:S(2)}, u32[]{:S(2)}) collective-permute-start(f32[136,256]{1,0:T(8,128)S(1)} %get-tuple-element.33), channel_id=1, source_target_pairs={{0,8},{8,0},{16,24},{24,16},{1,9},{9,1},{17,25},{25,17},{2,10},{10... | collective-permute-start | bytes 417800 | tf_op jit(solution)/shard_map/ppermute | solution.py:28
  25.1 2.4 %collective-permute-start.6 = (f32[136,256]{1,0:T(8,128)S(1)}, f32[136,256]{1,0:T(8,128)S(1)}, u32[]{:S(2)}, u32[]{:S(2)}) collective-permute-start(f32[136,256]{1,0:T(8,128)S(1)} %get-tuple-element.31), channel_id=1, source_target_pairs={{0,8},{8,0},{16,24},{24,16},{1,9},{9,1},{17,25},{25,17},{2,10},{10... | collective-permute-start | bytes 417800 | tf_op jit(solution)/shard_map/ppermute | solution.py:28
  25.2 5.1 %copy-start = (f32[136,256]{1,0:T(8,128)S(1)}, f32[136,256]{1,0:T(8,128)}, u32[]{:S(2)}) copy-start(f32[136,256]{1,0:T(8,128)} %get-tuple-element.18.refs_0_) | copy-start | bytes 417796
  25.2 5.1 %collective-permute-start.7 = (f32[136,256]{1,0:T(8,128)S(1)}, f32[136,256]{1,0:T(8,128)S(1)}, u32[]{:S(2)}, u32[]{:S(2)}) collective-permute-start(f32[136,256]{1,0:T(8,128)S(1)} %get-tuple-element.32.refs_5_), channel_id=1, source_target_pairs={{0,2},{2,4},{4,6},{6,7},{7,5},{5,3},{3,1},{1,0},{8,9},{10,8},{12,1... | collective-permute-start | bytes 417800 | tf_op jit(solution)/shard_map/ppermute | solution.py:47
  27.3 13.3 %collective-permute-start.11 = (f32[128,256]{1,0:T(8,128)S(1)}, f32[128,256]{1,0:T(8,128)S(1)}, u32[]{:S(2)}, u32[]{:S(2)}) collective-permute-start(f32[128,256]{1,0:T(8,128)S(1)} %get-tuple-element.41), channel_id=1, source_target_pairs={{0,8},{8,0},{16,24},{24,16},{1,9},{9,1},{17,25},{25,17},{2,10},{10... | collective-permute-start | bytes 393224 | tf_op jit(solution)/shard_map/ppermute | solution.py:28
  31.6 1.4 %collective-permute-start.8 = (f32[256,128]{1,0:T(8,128)S(1)}, f32[256,128]{1,0:T(8,128)S(1)}, u32[]{:S(2)}, u32[]{:S(2)}) collective-permute-start(f32[256,128]{1,0:T(8,128)S(1)} %get-tuple-element.20.refs_8_), channel_id=1, source_target_pairs={{0,8},{8,0},{16,24},{24,16},{1,9},{9,1},{17,25},{25,17},{2,10},{10... | collective-permute-start | bytes 393224 | tf_op jit(solution)/shard_map/ppermute | solution.py:28
  31.7 8.9 %collective-permute-start.13 = (f32[128,256]{1,0:T(8,128)S(1)}, f32[128,256]{1,0:T(8,128)S(1)}, u32[]{:S(2)}, u32[]{:S(2)}) collective-permute-start(f32[128,256]{1,0:T(8,128)S(1)} %get-tuple-element.39), channel_id=1, source_target_pairs={{0,8},{8,0},{16,24},{24,16},{1,9},{9,1},{17,25},{25,17},{2,10},{10... | collective-permute-start | bytes 393224 | tf_op jit(solution)/shard_map/ppermute | solution.py:28
  34.5 5.8 %collective-permute-start.17 = (f32[256,128]{1,0:T(8,128)S(1)}, f32[256,128]{1,0:T(8,128)S(1)}, u32[]{:S(2)}, u32[]{:S(2)}) collective-permute-start(f32[256,128]{1,0:T(8,128)S(1)} %get-tuple-element.23.mine_ref), channel_id=1, source_target_pairs={{0,16},{8,24},{16,0},{24,8},{1,17},{9,25},{17,1},{25,9},{2,18},{10... | collective-permute-start | bytes 393224 | tf_op jit(solution)/shard_map/ppermute | solution.py:28
  36.5 4.1 %collective-permute-start.15 = (f32[128,256]{1,0:T(8,128)S(1)}, f32[128,256]{1,0:T(8,128)S(1)}, u32[]{:S(2)}, u32[]{:S(2)}) collective-permute-start(f32[128,256]{1,0:T(8,128)S(1)} %get-tuple-element.37), channel_id=1, source_target_pairs={{0,8},{8,0},{16,24},{24,16},{1,9},{9,1},{17,25},{25,17},{2,10},{10... | collective-permute-start | bytes 393224 | tf_op jit(solution)/shard_map/ppermute | solution.py:28
  36.6 5.0 %collective-permute-start.16 = (f32[128,256]{1,0:T(8,128)S(1)}, f32[128,256]{1,0:T(8,128)S(1)}, u32[]{:S(2)}, u32[]{:S(2)}) collective-permute-start(f32[128,256]{1,0:T(8,128)S(1)} %get-tuple-element.38.refs_5_), channel_id=1, source_target_pairs={{0,2},{2,4},{4,6},{6,7},{7,5},{5,3},{3,1},{1,0},{8,9},{10,8},{12,1... | collective-permute-start | bytes 393224 | tf_op jit(solution)/shard_map/ppermute | solution.py:47
  40.5 1.4 %collective-permute-start.18 = (f32[256,128]{1,0:T(8,128)S(1)}, f32[256,128]{1,0:T(8,128)S(1)}, u32[]{:S(2)}, u32[]{:S(2)}) collective-permute-start(f32[256,128]{1,0:T(8,128)S(1)} %shard_map.49.refs_8_), channel_id=1, source_target_pairs={{0,8},{8,0},{16,24},{24,16},{1,9},{9,1},{17,25},{25,17},{2,10},{10... | collective-permute-start | bytes 393224 | tf_op jit(solution)/shard_map/ppermute | solution.py:28
  45.7 1.4 %collective-permute-start.19 = (f32[256,128]{1,0:T(8,128)S(1)}, f32[256,128]{1,0:T(8,128)S(1)}, u32[]{:S(2)}, u32[]{:S(2)}) collective-permute-start(f32[256,128]{1,0:T(8,128)S(1)} %get-tuple-element.25), channel_id=1, source_target_pairs={{0,8},{8,0},{16,24},{24,16},{1,9},{9,1},{17,25},{25,17},{2,10},{10... | collective-permute-start | bytes 393224 | tf_op jit(solution)/shard_map/ppermute | solution.py:28
  47.3 5.6 %collective-permute-start.20 = (f32[256,128]{1,0:T(8,128)S(1)}, f32[256,128]{1,0:T(8,128)S(1)}, u32[]{:S(2)}, u32[]{:S(2)}) collective-permute-start(f32[256,128]{1,0:T(8,128)S(1)} %get-tuple-element.27), channel_id=1, source_target_pairs={{0,16},{8,24},{16,0},{24,8},{1,17},{9,25},{17,1},{25,9},{2,18},{10... | collective-permute-start | bytes 393224 | tf_op jit(solution)/shard_map/ppermute | solution.py:28
  54.2 1.4 %collective-permute-start.21 = (f32[256,128]{1,0:T(8,128)S(1)}, f32[256,128]{1,0:T(8,128)S(1)}, u32[]{:S(2)}, u32[]{:S(2)}) collective-permute-start(f32[256,128]{1,0:T(8,128)S(1)} %get-tuple-element.29), channel_id=1, source_target_pairs={{0,8},{8,0},{16,24},{24,16},{1,9},{9,1},{17,25},{25,17},{2,10},{10... | collective-permute-start | bytes 393224 | tf_op jit(solution)/shard_map/ppermute | solution.py:28

commit v4 on v3

--- a/solution.py
+++ b/solution.py
@@ -7,20 +7,28 @@
 from jax.experimental.pallas import tpu as pltpu
 from jax.sharding import PartitionSpec as P
 
-HIGHEST = lax.Precision.HIGHEST
 GATHER_BYTES = 8 * 2**20
 
 
+def split(a):
+    high = a.astype(jnp.bfloat16)
+    return high, (a - high.astype(jnp.float32)).astype(jnp.bfloat16)
+
+
+def product(a, b, dims):
+    def term(x, y):
+        return lax.dot_general(x, y, (dims, ((), ())), preferred_element_type=jnp.float32)
+
+    (a_high, a_low), (b_high, b_low) = a, b
+    return term(a_high, b_high) + (term(a_high, b_low) + term(a_low, b_high))
+
+
 def dot(a, b):
-    return lax.dot_general(
-        a, b, (((1,), (0,)), ((), ())), precision=HIGHEST, preferred_element_type=jnp.float32
-    )
+    return product(split(a), split(b), ((1,), (0,)))
 
 
 def dot_t(a, b):
-    return lax.dot_general(
-        a, b, (((0,), (0,)), ((), ())), precision=HIGHEST, preferred_element_type=jnp.float32
-    )
+    return product(split(a), split(b), ((0,), (0,)))
 
 
 def swap(block, axis, mask):
@@ -120,7 +128,9 @@
             row_ids = lax.broadcasted_iota(jnp.int32, (rows, panel.shape[0]), 0)
             names = maps_ref[l, 0, 0, h : h + 1, :]
             onehot = jnp.where(row_ids == names, 1.0, 0.0).astype(jnp.float32)
-            parts.append(dot(onehot, panel))
+            parts.append(
+                jnp.dot(onehot, panel, precision=lax.Precision.HIGHEST, preferred_element_type=jnp.float32)
+            )
     out_ref[pk.top : pk.top + rows, :] = jnp.concatenate(parts, axis=1)
     last = rhs_ref[pk.levels - 1, 0, 0]
     step = rows // pk.fold
@@ -188,8 +198,9 @@
     vec_ref[part(2), :] = mine_ref[:, cols:]
     vec_ref[part(1), :] = got_ref[:, :cols]
     vec_ref[part(3), :] = got_ref[:, cols:]
-    diag = diag_ref[...]
-    vec_ref[...] = dot(diag, dot_t(diag, vec_ref[...]))
+    diag = split(diag_ref[...])
+    y = product(diag, split(vec_ref[...]), ((0,), (0,)))
+    vec_ref[...] = product(diag, split(y), ((1,), (0,)))
     keep_ref[:, :cols] = vec_ref[part(0), :]
     keep_ref[:, cols:] = vec_ref[part(2), :]
     send_ref[:, :cols] = vec_ref[part(1), :]

time: 57.1 us -> 53.2 us (0.932)
  Pallas kernels: 11.4 us -> 7.43 us
    pallas_call x8, Pallas kernels: 11.4 us -> 7.43 us  [call(): pl.pallas_call(functools.partial(kernel, pk), out_shape=[jax.ShapeDtypeSt...]
  transfers between devices with their start and end apart: 22 -> 22, of which waited for: 15 -> 15; matrix products, arithmetic and copies ran while one was open for 0% -> 0% of each run, Pallas kernels for 5% -> 3%
where the time goes in v4:
time: 53.2 us; the launch traced here: 53 us
  waiting for transfers between devices  22.7 us (43%)
  starting transfers between devices  21.6 us (41%)
  Pallas kernels  7.43 us (14%)
  other arithmetic  0.94 us (2%)
    ppermute x8, starting transfers between devices, ring_step(): return lax.ppermute(block, ('cube', 'blk'), route)  15.8 us
    ppermute x14, waiting for transfers between devices, swap(): return lax.ppermute(block, axis, [(i, i ^ mask) for i in range(count)])  12 us
    ppermute x8, waiting for transfers between devices, ring_step(): return lax.ppermute(block, ('cube', 'blk'), route)  10.7 us
    pallas_call x8, Pallas kernels, call(): pl.pallas_call(functools.partial(kernel, pk), out_shape=[jax.ShapeDtypeSt...  7.43 us
    ppermute x14, starting transfers between devices, swap(): return lax.ppermute(block, axis, [(i, i ^ mask) for i in range(count)])  5.8 us
  transfers between devices with their start and end apart: 22, of which 15 were waited for; matrix products, arithmetic and copies ran while one was open for 0% of the time, Pallas kernels for 3%

profile of v4, /device:TPU:0, one launch (start us, length us, event | category | flops | bytes accessed | tf_op | source)
XLA Modules:
  0.0 53.0 jit_solution(9076630062923616834)
XLA Ops:
  0.0 1.8 %shard_map.46 = (f32[136,256]{1,0:T(8,128)}, f32[128,256]{1,0:T(8,128)}) custom-call(f32[3,1,1,32,64]{4,3,2,1,0:T(8,128)} %rhs_hbm.1, f32[2,1,1,2,16,32]{5,4,3,2,1,0:T(8,128)} %panels_hbm.1, s32[2,1,1,2,16]{4,3,2,1,0:T(2,128)} %maps_hbm.1, f32[224,256]{1,0:T(8,128)} %diag_hbm.1), custom_call_target="tpu_custom_call" | custom-call | tf_op jit(solution)/shard_map/pallas_call | solution.py:257
  2.4 1.2 %collective-permute-done = f32[136,256]{1,0:T(8,128)S(1)} collective-permute-done((f32[136,256]{1,0:T(8,128)}, f32[136,256]{1,0:T(8,128)S(1)}, u32[]{:S(2)}, u32[]{:S(2)}) %collective-permute-start) | collective-permute-done | bytes 139296 | tf_op jit(solution)/shard_map/ppermute | solution.py:36
  4.5 3.0 %collective-permute-start.1 = (f32[272,256]{1,0:T(8,128)S(1)}, f32[272,256]{1,0:T(8,128)S(1)}, u32[]{:S(2)}, u32[]{:S(2)}) collective-permute-start(f32[272,256]{1,0:T(8,128)S(1)} %pad_maximum_fusion), channel_id=1, source_target_pairs={{0,2},{2,4},{4,6},{6,7},{7,5},{5,3},{3,1},{1,0},{8,9},{10,8},{12,1... | collective-permute-start | bytes 835592 | tf_op jit(solution)/shard_map/ppermute | solution.py:55
  7.5 1.3 %collective-permute-done.9 = f32[128,256]{1,0:T(8,128)S(1)} collective-permute-done((f32[128,256]{1,0:T(8,128)S(1)}, f32[128,256]{1,0:T(8,128)S(1)}, u32[]{:S(2)}, u32[]{:S(2)}) %collective-permute-start.9) | collective-permute-done | bytes 131104 | tf_op jit(solution)/shard_map/ppermute | solution.py:36
  8.9 1.6 %collective-permute-start.10 = (f32[256,256]{1,0:T(8,128)S(1)}, f32[256,256]{1,0:T(8,128)S(1)}, u32[]{:S(2)}, u32[]{:S(2)}) collective-permute-start(f32[256,256]{1,0:T(8,128)S(1)} %pad_maximum_fusion.1), channel_id=1, source_target_pairs={{0,2},{2,4},{4,6},{6,7},{7,5},{5,3},{3,1},{1,0},{8,9},{10,8},{12,1... | collective-permute-start | bytes 786440 | tf_op jit(solution)/shard_map/ppermute | solution.py:55
  10.5 1.5 %collective-permute-done.1 = f32[272,256]{1,0:T(8,128)S(1)} collective-permute-done((f32[272,256]{1,0:T(8,128)S(1)}, f32[272,256]{1,0:T(8,128)S(1)}, u32[]{:S(2)}, u32[]{:S(2)}) %collective-permute-start.1) | collective-permute-done | bytes 278560 | tf_op jit(solution)/shard_map/ppermute | solution.py:55
  12.0 2.1 %collective-permute-start.3 = (f32[272,256]{1,0:T(8,128)S(1)}, f32[272,256]{1,0:T(8,128)S(1)}, u32[]{:S(2)}, u32[]{:S(2)}) collective-permute-start(f32[272,256]{1,0:T(8,128)S(1)} %collective-permute-done.1), channel_id=1, source_target_pairs={{0,2},{2,4},{4,6},{6,7},{7,5},{5,3},{3,1},{1,0},{8,9},{10,8},{12,1... | collective-permute-start | bytes 835592 | tf_op jit(solution)/shard_map/ppermute | solution.py:55
  14.0 1.2 %collective-permute-done.10 = f32[256,256]{1,0:T(8,128)S(1)} collective-permute-done((f32[256,256]{1,0:T(8,128)S(1)}, f32[256,256]{1,0:T(8,128)S(1)}, u32[]{:S(2)}, u32[]{:S(2)}) %collective-permute-start.10) | collective-permute-done | bytes 262176 | tf_op jit(solution)/shard_map/ppermute | solution.py:55
  15.3 1.6 %collective-permute-start.12 = (f32[256,256]{1,0:T(8,128)S(1)}, f32[256,256]{1,0:T(8,128)S(1)}, u32[]{:S(2)}, u32[]{:S(2)}) collective-permute-start(f32[256,256]{1,0:T(8,128)S(1)} %collective-permute-done.10), channel_id=1, source_target_pairs={{0,2},{2,4},{4,6},{6,7},{7,5},{5,3},{3,1},{1,0},{8,9},{10,8},{12,1... | collective-permute-start | bytes 786440 | tf_op jit(solution)/shard_map/ppermute | solution.py:55
  16.9 1.6 %collective-permute-done.3 = f32[272,256]{1,0:T(8,128)S(1)} collective-permute-done((f32[272,256]{1,0:T(8,128)S(1)}, f32[272,256]{1,0:T(8,128)S(1)}, u32[]{:S(2)}, u32[]{:S(2)}) %collective-permute-start.3) | collective-permute-done | bytes 278560 | tf_op jit(solution)/shard_map/ppermute | solution.py:55
  18.5 2.1 %collective-permute-start.5 = (f32[272,256]{1,0:T(8,128)S(1)}, f32[272,256]{1,0:T(8,128)S(1)}, u32[]{:S(2)}, u32[]{:S(2)}) collective-permute-start(f32[272,256]{1,0:T(8,128)S(1)} %collective-permute-done.3), channel_id=1, source_target_pairs={{0,2},{2,4},{4,6},{6,7},{7,5},{5,3},{3,1},{1,0},{8,9},{10,8},{12,1... | collective-permute-start | bytes 835592 | tf_op jit(solution)/shard_map/ppermute | solution.py:55
  21.7 1.7 %collective-permute-start.14 = (f32[256,256]{1,0:T(8,128)S(1)}, f32[256,256]{1,0:T(8,128)S(1)}, u32[]{:S(2)}, u32[]{:S(2)}) collective-permute-start(f32[256,256]{1,0:T(8,128)S(1)} %collective-permute-done.12), channel_id=1, source_target_pairs={{0,2},{2,4},{4,6},{6,7},{7,5},{5,3},{3,1},{1,0},{8,9},{10,8},{12,1... | collective-permute-start | bytes 786440 | tf_op jit(solution)/shard_map/ppermute | solution.py:55
  23.5 1.6 %collective-permute-done.5 = f32[272,256]{1,0:T(8,128)S(1)} collective-permute-done((f32[272,256]{1,0:T(8,128)S(1)}, f32[272,256]{1,0:T(8,128)S(1)}, u32[]{:S(2)}, u32[]{:S(2)}) %collective-permute-start.5) | collective-permute-done | bytes 278560 | tf_op jit(solution)/shard_map/ppermute | solution.py:55
  25.2 2.1 %collective-permute-start.7 = (f32[136,256]{1,0:T(8,128)S(1)}, f32[136,256]{1,0:T(8,128)S(1)}, u32[]{:S(2)}, u32[]{:S(2)}) collective-permute-start(f32[136,256]{1,0:T(8,128)S(1)} %get-tuple-element.32.refs_5_), channel_id=1, source_target_pairs={{0,2},{2,4},{4,6},{6,7},{7,5},{5,3},{3,1},{1,0},{8,9},{10,8},{12,1... | collective-permute-start | bytes 417800 | tf_op jit(solution)/shard_map/ppermute | solution.py:55
  27.5 2.8 %collective-permute-done.7.refs_7_ = f32[136,256]{1,0:T(8,128)S(1)} collective-permute-done((f32[136,256]{1,0:T(8,128)S(1)}, f32[136,256]{1,0:T(8,128)S(1)}, u32[]{:S(2)}, u32[]{:S(2)}) %collective-permute-start.7) | collective-permute-done | bytes 139296 | tf_op jit(solution)/shard_map/ppermute | solution.py:55
  33.3 2.1 %collective-permute-start.17 = (f32[256,128]{1,0:T(8,128)S(1)}, f32[256,128]{1,0:T(8,128)S(1)}, u32[]{:S(2)}, u32[]{:S(2)}) collective-permute-start(f32[256,128]{1,0:T(8,128)S(1)} %get-tuple-element.23.mine_ref), channel_id=1, source_target_pairs={{0,16},{8,24},{16,0},{24,8},{1,17},{9,25},{17,1},{25,9},{2,18},{10... | collective-permute-start | bytes 393224 | tf_op jit(solution)/shard_map/ppermute | solution.py:36
  35.5 1.6 %collective-permute-start.16 = (f32[128,256]{1,0:T(8,128)S(1)}, f32[128,256]{1,0:T(8,128)S(1)}, u32[]{:S(2)}, u32[]{:S(2)}) collective-permute-start(f32[128,256]{1,0:T(8,128)S(1)} %get-tuple-element.38.refs_5_), channel_id=1, source_target_pairs={{0,2},{2,4},{4,6},{6,7},{7,5},{5,3},{3,1},{1,0},{8,9},{10,8},{12,1... | collective-permute-start | bytes 393224 | tf_op jit(solution)/shard_map/ppermute | solution.py:55
  37.1 2.1 %collective-permute-done.17.got_ref = f32[256,128]{1,0:T(8,128)S(1)} collective-permute-done((f32[256,128]{1,0:T(8,128)S(1)}, f32[256,128]{1,0:T(8,128)S(1)}, u32[]{:S(2)}, u32[]{:S(2)}) %collective-permute-start.17) | collective-permute-done | bytes 131104 | tf_op jit(solution)/shard_map/ppermute | solution.py:36
  40.8 1.4 %shard_map.50 = (f32[256,128]{1,0:T(8,128)S(1)}, f32[256,128]{1,0:T(8,128)S(1)}) custom-call(f32[128,256]{1,0:T(8,128)S(1)} %copy-done.1, f32[128,256]{1,0:T(8,128)S(1)} %get-tuple-element.42.refs_1_, f32[128,256]{1,0:T(8,128)S(1)} %collective-permute-done.11.refs_2_, f32[128,256]{1,0:T(8,128)S(1)} %get-tuple-element.40.refs_3_, ...), custom_call_target="tpu_custom_call" | custom-call | tf_op jit(solution)/shard_map/pallas_call | solution.py:257
  42.4 1.2 %collective-permute-done.19.got_ref = f32[256,128]{1,0:T(8,128)S(1)} collective-permute-done((f32[256,128]{1,0:T(8,128)S(1)}, f32[256,128]{1,0:T(8,128)S(1)}, u32[]{:S(2)}, u32[]{:S(2)}) %collective-permute-start.19) | collective-permute-done | bytes 131104 | tf_op jit(solution)/shard_map/ppermute | solution.py:36
  43.7 1.8 %collective-permute-start.20 = (f32[256,128]{1,0:T(8,128)S(1)}, f32[256,128]{1,0:T(8,128)S(1)}, u32[]{:S(2)}, u32[]{:S(2)}) collective-permute-start(f32[256,128]{1,0:T(8,128)S(1)} %get-tuple-element.27), channel_id=1, source_target_pairs={{0,16},{8,24},{16,0},{24,8},{1,17},{9,25},{17,1},{25,9},{2,18},{10... | collective-permute-start | bytes 393224 | tf_op jit(solution)/shard_map/ppermute | solution.py:36
  45.5 3.8 %collective-permute-done.20.refs_10_ = f32[256,128]{1,0:T(8,128)S(1)} collective-permute-done((f32[256,128]{1,0:T(8,128)S(1)}, f32[256,128]{1,0:T(8,128)S(1)}, u32[]{:S(2)}, u32[]{:S(2)}) %collective-permute-start.20) | collective-permute-done | bytes 131104 | tf_op jit(solution)/shard_map/ppermute | solution.py:36
  50.5 1.3 %collective-permute-done.21.refs_10_ = f32[256,128]{1,0:T(8,128)S(1)} collective-permute-done((f32[256,128]{1,0:T(8,128)S(1)}, f32[256,128]{1,0:T(8,128)S(1)}, u32[]{:S(2)}, u32[]{:S(2)}) %collective-permute-start.21) | collective-permute-done | bytes 131104 | tf_op jit(solution)/shard_map/ppermute | solution.py:36
  51.8 1.2 %shard_map.53 = f32[3,32,64]{2,1,0:T(8,128)} custom-call(f32[136,256]{1,0:T(8,128)S(1)} %copy-done, f32[136,256]{1,0:T(8,128)S(1)} %get-tuple-element.36.refs_1_, f32[136,256]{1,0:T(8,128)S(1)} %collective-permute-done.2.refs_2_, f32[136,256]{1,0:T(8,128)S(1)} %get-tuple-element.34.refs_3_, f32[136,256]{1,0:T(8,128)S(1)} %collective-permute-done.4.refs_4_, ...), custom_call_target="tpu_custom_call" | custom-call | tf_op jit(solution)/shard_map/pallas_call | solution.py:257
  (40 shorter events, 9.0 us)
Async XLA Ops:
  1.8 5.7 %copy-start.1 = (f32[128,256]{1,0:T(8,128)S(1)}, f32[128,256]{1,0:T(8,128)}, u32[]{:S(2)}) copy-start(f32[128,256]{1,0:T(8,128)} %get-tuple-element.22.refs_0_) | copy-start | bytes 393220
  1.9 1.7 %collective-permute-start = (f32[136,256]{1,0:T(8,128)}, f32[136,256]{1,0:T(8,128)S(1)}, u32[]{:S(2)}, u32[]{:S(2)}) collective-permute-start(f32[136,256]{1,0:T(8,128)} %get-tuple-element.18.refs_0_), channel_id=1, source_target_pairs={{0,8},{8,0},{16,24},{24,16},{1,9},{9,1},{17,25},{25,17},{2,10},{10... | collective-permute-start | bytes 417800 | tf_op jit(solution)/shard_map/ppermute | solution.py:36
  4.5 7.5 %collective-permute-start.1 = (f32[272,256]{1,0:T(8,128)S(1)}, f32[272,256]{1,0:T(8,128)S(1)}, u32[]{:S(2)}, u32[]{:S(2)}) collective-permute-start(f32[272,256]{1,0:T(8,128)S(1)} %pad_maximum_fusion), channel_id=1, source_target_pairs={{0,2},{2,4},{4,6},{6,7},{7,5},{5,3},{3,1},{1,0},{8,9},{10,8},{12,1... | collective-permute-start | bytes 835592 | tf_op jit(solution)/shard_map/ppermute | solution.py:55
  7.5 1.3 %collective-permute-start.9 = (f32[128,256]{1,0:T(8,128)S(1)}, f32[128,256]{1,0:T(8,128)S(1)}, u32[]{:S(2)}, u32[]{:S(2)}) collective-permute-start(f32[128,256]{1,0:T(8,128)S(1)} %copy-done.1), channel_id=1, source_target_pairs={{0,8},{8,0},{16,24},{24,16},{1,9},{9,1},{17,25},{25,17},{2,10},{10... | collective-permute-start | bytes 393224 | tf_op jit(solution)/shard_map/ppermute | solution.py:36
  8.9 6.4 %collective-permute-start.10 = (f32[256,256]{1,0:T(8,128)S(1)}, f32[256,256]{1,0:T(8,128)S(1)}, u32[]{:S(2)}, u32[]{:S(2)}) collective-permute-start(f32[256,256]{1,0:T(8,128)S(1)} %pad_maximum_fusion.1), channel_id=1, source_target_pairs={{0,2},{2,4},{4,6},{6,7},{7,5},{5,3},{3,1},{1,0},{8,9},{10,8},{12,1... | collective-permute-start | bytes 786440 | tf_op jit(solution)/shard_map/ppermute | solution.py:55
  12.0 6.5 %collective-permute-start.3 = (f32[272,256]{1,0:T(8,128)S(1)}, f32[272,256]{1,0:T(8,128)S(1)}, u32[]{:S(2)}, u32[]{:S(2)}) collective-permute-start(f32[272,256]{1,0:T(8,128)S(1)} %collective-permute-done.1), channel_id=1, source_target_pairs={{0,2},{2,4},{4,6},{6,7},{7,5},{5,3},{3,1},{1,0},{8,9},{10,8},{12,1... | collective-permute-start | bytes 835592 | tf_op jit(solution)/shard_map/ppermute | solution.py:55
  15.3 6.4 %collective-permute-start.12 = (f32[256,256]{1,0:T(8,128)S(1)}, f32[256,256]{1,0:T(8,128)S(1)}, u32[]{:S(2)}, u32[]{:S(2)}) collective-permute-start(f32[256,256]{1,0:T(8,128)S(1)} %collective-permute-done.10), channel_id=1, source_target_pairs={{0,2},{2,4},{4,6},{6,7},{7,5},{5,3},{3,1},{1,0},{8,9},{10,8},{12,1... | collective-permute-start | bytes 786440 | tf_op jit(solution)/shard_map/ppermute | solution.py:55
  18.5 6.5 %collective-permute-start.5 = (f32[272,256]{1,0:T(8,128)S(1)}, f32[272,256]{1,0:T(8,128)S(1)}, u32[]{:S(2)}, u32[]{:S(2)}) collective-permute-start(f32[272,256]{1,0:T(8,128)S(1)} %collective-permute-done.3), channel_id=1, source_target_pairs={{0,2},{2,4},{4,6},{6,7},{7,5},{5,3},{3,1},{1,0},{8,9},{10,8},{12,1... | collective-permute-start | bytes 835592 | tf_op jit(solution)/shard_map/ppermute | solution.py:55
  20.6 6.7 %collective-permute-start.2 = (f32[136,256]{1,0:T(8,128)S(1)}, f32[136,256]{1,0:T(8,128)S(1)}, u32[]{:S(2)}, u32[]{:S(2)}) collective-permute-start(f32[136,256]{1,0:T(8,128)S(1)} %get-tuple-element.35), channel_id=1, source_target_pairs={{0,8},{8,0},{16,24},{24,16},{1,9},{9,1},{17,25},{25,17},{2,10},{10... | collective-permute-start | bytes 417800 | tf_op jit(solution)/shard_map/ppermute | solution.py:36
  21.7 13.7 %collective-permute-start.14 = (f32[256,256]{1,0:T(8,128)S(1)}, f32[256,256]{1,0:T(8,128)S(1)}, u32[]{:S(2)}, u32[]{:S(2)}) collective-permute-start(f32[256,256]{1,0:T(8,128)S(1)} %collective-permute-done.12), channel_id=1, source_target_pairs={{0,2},{2,4},{4,6},{6,7},{7,5},{5,3},{3,1},{1,0},{8,9},{10,8},{12,1... | collective-permute-start | bytes 786440 | tf_op jit(solution)/shard_map/ppermute | solution.py:55
  23.4 4.1 %collective-permute-start.4 = (f32[136,256]{1,0:T(8,128)S(1)}, f32[136,256]{1,0:T(8,128)S(1)}, u32[]{:S(2)}, u32[]{:S(2)}) collective-permute-start(f32[136,256]{1,0:T(8,128)S(1)} %get-tuple-element.33), channel_id=1, source_target_pairs={{0,8},{8,0},{16,24},{24,16},{1,9},{9,1},{17,25},{25,17},{2,10},{10... | collective-permute-start | bytes 417800 | tf_op jit(solution)/shard_map/ppermute | solution.py:36
  25.1 2.4 %collective-permute-start.6 = (f32[136,256]{1,0:T(8,128)S(1)}, f32[136,256]{1,0:T(8,128)S(1)}, u32[]{:S(2)}, u32[]{:S(2)}) collective-permute-start(f32[136,256]{1,0:T(8,128)S(1)} %get-tuple-element.31), channel_id=1, source_target_pairs={{0,8},{8,0},{16,24},{24,16},{1,9},{9,1},{17,25},{25,17},{2,10},{10... | collective-permute-start | bytes 417800 | tf_op jit(solution)/shard_map/ppermute | solution.py:36
  25.2 5.1 %copy-start = (f32[136,256]{1,0:T(8,128)S(1)}, f32[136,256]{1,0:T(8,128)}, u32[]{:S(2)}) copy-start(f32[136,256]{1,0:T(8,128)} %get-tuple-element.18.refs_0_) | copy-start | bytes 417796
  25.2 5.1 %collective-permute-start.7 = (f32[136,256]{1,0:T(8,128)S(1)}, f32[136,256]{1,0:T(8,128)S(1)}, u32[]{:S(2)}, u32[]{:S(2)}) collective-permute-start(f32[136,256]{1,0:T(8,128)S(1)} %get-tuple-element.32.refs_5_), channel_id=1, source_target_pairs={{0,2},{2,4},{4,6},{6,7},{7,5},{5,3},{3,1},{1,0},{8,9},{10,8},{12,1... | collective-permute-start | bytes 417800 | tf_op jit(solution)/shard_map/ppermute | solution.py:55
  27.3 12.1 %collective-permute-start.11 = (f32[128,256]{1,0:T(8,128)S(1)}, f32[128,256]{1,0:T(8,128)S(1)}, u32[]{:S(2)}, u32[]{:S(2)}) collective-permute-start(f32[128,256]{1,0:T(8,128)S(1)} %get-tuple-element.41), channel_id=1, source_target_pairs={{0,8},{8,0},{16,24},{24,16},{1,9},{9,1},{17,25},{25,17},{2,10},{10... | collective-permute-start | bytes 393224 | tf_op jit(solution)/shard_map/ppermute | solution.py:36
  31.1 1.4 %collective-permute-start.8 = (f32[256,128]{1,0:T(8,128)S(1)}, f32[256,128]{1,0:T(8,128)S(1)}, u32[]{:S(2)}, u32[]{:S(2)}) collective-permute-start(f32[256,128]{1,0:T(8,128)S(1)} %get-tuple-element.20.refs_8_), channel_id=1, source_target_pairs={{0,8},{8,0},{16,24},{24,16},{1,9},{9,1},{17,25},{25,17},{2,10},{10... | collective-permute-start | bytes 393224 | tf_op jit(solution)/shard_map/ppermute | solution.py:36
  31.2 8.3 %collective-permute-start.13 = (f32[128,256]{1,0:T(8,128)S(1)}, f32[128,256]{1,0:T(8,128)S(1)}, u32[]{:S(2)}, u32[]{:S(2)}) collective-permute-start(f32[128,256]{1,0:T(8,128)S(1)} %get-tuple-element.39), channel_id=1, source_target_pairs={{0,8},{8,0},{16,24},{24,16},{1,9},{9,1},{17,25},{25,17},{2,10},{10... | collective-permute-start | bytes 393224 | tf_op jit(solution)/shard_map/ppermute | solution.py:36
  33.3 5.9 %collective-permute-start.17 = (f32[256,128]{1,0:T(8,128)S(1)}, f32[256,128]{1,0:T(8,128)S(1)}, u32[]{:S(2)}, u32[]{:S(2)}) collective-permute-start(f32[256,128]{1,0:T(8,128)S(1)} %get-tuple-element.23.mine_ref), channel_id=1, source_target_pairs={{0,16},{8,24},{16,0},{24,8},{1,17},{9,25},{17,1},{25,9},{2,18},{10... | collective-permute-start | bytes 393224 | tf_op jit(solution)/shard_map/ppermute | solution.py:36
  35.4 4.1 %collective-permute-start.15 = (f32[128,256]{1,0:T(8,128)S(1)}, f32[128,256]{1,0:T(8,128)S(1)}, u32[]{:S(2)}, u32[]{:S(2)}) collective-permute-start(f32[128,256]{1,0:T(8,128)S(1)} %get-tuple-element.37), channel_id=1, source_target_pairs={{0,8},{8,0},{16,24},{24,16},{1,9},{9,1},{17,25},{25,17},{2,10},{10... | collective-permute-start | bytes 393224 | tf_op jit(solution)/shard_map/ppermute | solution.py:36
  35.5 5.0 %collective-permute-start.16 = (f32[128,256]{1,0:T(8,128)S(1)}, f32[128,256]{1,0:T(8,128)S(1)}, u32[]{:S(2)}, u32[]{:S(2)}) collective-permute-start(f32[128,256]{1,0:T(8,128)S(1)} %get-tuple-element.38.refs_5_), channel_id=1, source_target_pairs={{0,2},{2,4},{4,6},{6,7},{7,5},{5,3},{3,1},{1,0},{8,9},{10,8},{12,1... | collective-permute-start | bytes 393224 | tf_op jit(solution)/shard_map/ppermute | solution.py:55
  39.4 1.4 %collective-permute-start.18 = (f32[256,128]{1,0:T(8,128)S(1)}, f32[256,128]{1,0:T(8,128)S(1)}, u32[]{:S(2)}, u32[]{:S(2)}) collective-permute-start(f32[256,128]{1,0:T(8,128)S(1)} %shard_map.49.refs_8_), channel_id=1, source_target_pairs={{0,8},{8,0},{16,24},{24,16},{1,9},{9,1},{17,25},{25,17},{2,10},{10... | collective-permute-start | bytes 393224 | tf_op jit(solution)/shard_map/ppermute | solution.py:36
  42.2 1.4 %collective-permute-start.19 = (f32[256,128]{1,0:T(8,128)S(1)}, f32[256,128]{1,0:T(8,128)S(1)}, u32[]{:S(2)}, u32[]{:S(2)}) collective-permute-start(f32[256,128]{1,0:T(8,128)S(1)} %get-tuple-element.25), channel_id=1, source_target_pairs={{0,8},{8,0},{16,24},{24,16},{1,9},{9,1},{17,25},{25,17},{2,10},{10... | collective-permute-start | bytes 393224 | tf_op jit(solution)/shard_map/ppermute | solution.py:36
  43.7 5.6 %collective-permute-start.20 = (f32[256,128]{1,0:T(8,128)S(1)}, f32[256,128]{1,0:T(8,128)S(1)}, u32[]{:S(2)}, u32[]{:S(2)}) collective-permute-start(f32[256,128]{1,0:T(8,128)S(1)} %get-tuple-element.27), channel_id=1, source_target_pairs={{0,16},{8,24},{16,0},{24,8},{1,17},{9,25},{17,1},{25,9},{2,18},{10... | collective-permute-start | bytes 393224 | tf_op jit(solution)/shard_map/ppermute | solution.py:36
  50.4 1.4 %collective-permute-start.21 = (f32[256,128]{1,0:T(8,128)S(1)}, f32[256,128]{1,0:T(8,128)S(1)}, u32[]{:S(2)}, u32[]{:S(2)}) collective-permute-start(f32[256,128]{1,0:T(8,128)S(1)} %get-tuple-element.29), channel_id=1, source_target_pairs={{0,8},{8,0},{16,24},{24,16},{1,9},{9,1},{17,25},{25,17},{2,10},{10... | collective-permute-start | bytes 393224 | tf_op jit(solution)/shard_map/ppermute | solution.py:36

commit v5 on v4

--- a/solution.py
+++ b/solution.py
@@ -44,11 +44,11 @@
     return jnp.where(place < count // 2, 2 * place, 2 * (count - 1 - place) + 1)
 
 
-def ring_step(block):
+def ring_step(block, even, odd):
     cubes, count = lax.axis_size("cube"), lax.axis_size("blk")
     order = list(range(0, count, 2)) + list(range(count - 1, 0, -2))
     route = [
-        (c * count + order[i], c * count + order[(i + 1 - 2 * (c % 2)) % count])
+        (c * count + order[i], c * count + order[(i + (odd if c % 2 else even)) % count])
         for c in range(cubes)
         for i in range(count)
     ]
@@ -64,9 +64,18 @@
     moving = jnp.concatenate([block, swap(block, "cube", 1)], axis=0)
     out = [block]
     for _ in range(1, lax.axis_size("blk") // 2):
-        moving = ring_step(moving)
+        moving = ring_step(moving, 1, -1)
         out += [moving[:height], swap(moving[height:], "cube", 1)]
-    return out + [ring_step(moving[:height])]
+    return out + [ring_step(moving[:height], 1, -1)]
+
+
+def gather_both_ways(block):
+    out = [block]
+    up = down = block
+    for _ in range(1, lax.axis_size("blk") // 2):
+        up, down = ring_step(up, 1, 1), ring_step(down, -1, -1)
+        out += [up, down]
+    return out + [ring_step(up, 1, 1)]
 
 
 class Packing:
@@ -100,11 +109,11 @@
             axis=0,
         )
 
-    def diag(self, pieces, level, diag_ref, first=None):
+    def diag(self, pieces, level, diag_ref, place_of, first=None):
         first = (2**level - 1) * self.rows if first is None else first
         for m, piece in enumerate(pieces):
             for p in range(2**level):
-                diag_ref[block_of(self, m, p), :] = piece[first + p * self.rows : first + (p + 1) * self.rows, :]
+                diag_ref[place_of(self, m, p), :] = piece[first + p * self.rows : first + (p + 1) * self.rows, :]
 
 
 def pack_kernel(pk, rhs_hbm, panels_hbm, maps_hbm, diag_hbm, out_ref, last_ref, rhs_ref, panels_ref, maps_ref, sems):
@@ -141,12 +150,15 @@
         copy.wait()
 
 
-def block_of(pk, m, p=0):
+def block_of(pk, m, p=0, side=1):
     count = pk.n_blk
     place = ring_place(lax.axis_index("blk"), count)
-    turn = ring_offsets(count)[m] * (1 - 2 * (lax.axis_index("cube") % 2))
-    group = ring_group((place - turn + count) % count, count)
+    group = ring_group((place - ring_offsets(count)[m] * side + count) % count, count)
     return pl.ds(pl.multiple_of(p * pk.width + group * pk.rows, pk.rows), pk.rows)
+
+
+def shared_block_of(pk, m, p=0):
+    return block_of(pk, m, p, 1 - 2 * (lax.axis_index("cube") % 2))
 
 
 def extend_out(pk, level, pieces, y_ref, send_ref):
@@ -160,7 +172,7 @@
 
 def first_kernel(pk, *refs):
     pieces, (send_ref, y_ref, diag_ref, z_ref) = refs[: pk.n_blk], refs[pk.n_blk :]
-    pk.diag(pieces, 0, diag_ref)
+    pk.diag(pieces, 0, diag_ref, block_of)
     for m, piece in enumerate(pieces):
         z_ref[block_of(pk, m), :] = pk.rhs(piece, 0)
     y_ref[...] = dot_t(diag_ref[...], z_ref[...])
@@ -174,7 +186,7 @@
     other = got_ref[:, :cols] - mine_ref[:, cols:]
     upper = lax.axis_index("cube") % 2 == 1
     z = jnp.concatenate([jnp.where(upper, other, own), jnp.where(upper, own, other)], axis=0)
-    pk.diag(pieces, 1, diag_ref)
+    pk.diag(pieces, 1, diag_ref, block_of)
     y_ref[...] = dot_t(diag_ref[...], z)
     extend_out(pk, 1, pieces, y_ref, send_ref)
 
@@ -193,7 +205,7 @@
     def part(k):
         return pl.ds(pl.multiple_of((cube ^ k) * node, node), node)
 
-    pk.diag(pieces, 2, diag_ref, 0)
+    pk.diag(pieces, 2, diag_ref, shared_block_of, 0)
     vec_ref[part(0), :] = mine_ref[:, :cols]
     vec_ref[part(2), :] = mine_ref[:, cols:]
     vec_ref[part(1), :] = got_ref[:, :cols]
@@ -230,7 +242,7 @@
     node, cols = pk.width, pk.cols
     own_rows = block_of(pk, 0)
     top_ref[...] = mine_ref[own_rows, :cols] + got_ref[own_rows, :cols]
-    pk.diag(pieces, 1, diag_ref)
+    pk.diag(pieces, 1, diag_ref, block_of)
     reduce_rows(pk, 1, pieces, y_ref, mine_ref, got_ref, w_ref)
     x = dot(diag_ref[...], w_ref[...])
     upper = lax.axis_index("cube") % 2 == 1
@@ -285,12 +297,12 @@
         pltpu.HBM,
         60,
     )
-    first = gather_rows(packed)
+    first = gather_both_ways(packed)
     last = gather_rows(top)
     send, y0 = call(first_kernel, pk, first, [two, one], work((node, node), one))
     got = swap(send, "cube", 1)
     send, y1 = call(middle_kernel, pk, [*first, send, got], [two, one], work((2 * node, node)))
-    got = swap(send, "cube", 2)
+    got = tie(swap(send, "cube", 2), last[7])
     (held,) = call(meet_kernel, pk, [send, got], [two])
     got = swap(held, "cube", 1)
     keep, send = call(

time: 53.2 us -> 51.8 us (0.974)
  starting transfers between devices: 21.6 us -> 19.6 us
  waiting for transfers between devices: 22.7 us -> 23.5 us
    ppermute x14 -> x10, starting transfers between devices: 5.8 us -> 4.37 us  [swap(): return lax.ppermute(block, axis, [(i, i ^ mask) for i in range(count)])]
    ppermute x8 -> x11, waiting for transfers between devices: 10.7 us -> 11.4 us  [ring_step(): return lax.ppermute(block, ('cube', 'blk'), route)]
    ppermute x8 -> x11, starting transfers between devices: 15.8 us -> 15.3 us  [ring_step(): return lax.ppermute(block, ('cube', 'blk'), route)]
    ppermute x14 -> x10, waiting for transfers between devices: 12 us -> 12.1 us  [swap(): return lax.ppermute(block, axis, [(i, i ^ mask) for i in range(count)])]
  transfers between devices with their start and end apart: 22 -> 21, of which waited for: 15 -> 14; matrix products, arithmetic and copies ran while one was open for 0% -> 2% of each run, Pallas kernels for 3% -> 3%
where the time goes in v5:
time: 51.8 us; the launch traced here: 51.7 us
  waiting for transfers between devices  23.5 us (45%)
  starting transfers between devices  19.6 us (38%)
  Pallas kernels  7.43 us (14%)
  other arithmetic  0.92 us (2%)
    ppermute x11, starting transfers between devices, ring_step(): return lax.ppermute(block, ('cube', 'blk'), route)  15.3 us
    ppermute x10, waiting for transfers between devices, swap(): return lax.ppermute(block, axis, [(i, i ^ mask) for i in range(count)])  12.1 us
    ppermute x11, waiting for transfers between devices, ring_step(): return lax.ppermute(block, ('cube', 'blk'), route)  11.4 us
    pallas_call x8, Pallas kernels, call(): pl.pallas_call(functools.partial(kernel, pk), out_shape=[jax.ShapeDtypeSt...  7.43 us
    ppermute x10, starting transfers between devices, swap(): return lax.ppermute(block, axis, [(i, i ^ mask) for i in range(count)])  4.37 us
  transfers between devices with their start and end apart: 21, of which 14 were waited for; matrix products, arithmetic and copies ran while one was open for 2% of the time, Pallas kernels for 3%

profile of v5, /device:TPU:0, one launch (start us, length us, event | category | flops | bytes accessed | tf_op | source)
XLA Modules:
  0.0 51.7 jit_solution(3830779646087834361)
XLA Ops:
  0.0 1.8 %shard_map.46 = (f32[136,256]{1,0:T(8,128)}, f32[128,256]{1,0:T(8,128)}) custom-call(f32[3,1,1,32,64]{4,3,2,1,0:T(8,128)} %rhs_hbm.1, f32[2,1,1,2,16,32]{5,4,3,2,1,0:T(8,128)} %panels_hbm.1, s32[2,1,1,2,16]{4,3,2,1,0:T(2,128)} %maps_hbm.1, f32[224,256]{1,0:T(8,128)} %diag_hbm.1), custom_call_target="tpu_custom_call" | custom-call | tf_op jit(solution)/shard_map/pallas_call | solution.py:269
  2.4 2.6 %collective-permute-start = (f32[136,256]{1,0:T(8,128)}, f32[136,256]{1,0:T(8,128)S(1)}, u32[]{:S(2)}, u32[]{:S(2)}) collective-permute-start(f32[136,256]{1,0:T(8,128)} %get-tuple-element.19.refs_0_), channel_id=1, source_target_pairs={{0,2},{2,4},{4,6},{6,7},{7,5},{5,3},{3,1},{1,0},{8,10},{10,12},{12... | collective-permute-start | bytes 417800 | tf_op jit(solution)/shard_map/ppermute | solution.py:55
  5.0 0.9 %pad_maximum_fusion = f32[256,256]{1,0:T(8,128)S(1)} fusion(f32[128,256]{1,0:T(8,128)S(1)} %collective-permute-done.8, f32[128,256]{1,0:T(8,128)} %get-tuple-element.23.refs_0_), kind=kLoop, calls=%fused_computation | loop fusion | flops 65536 | bytes 524288 | tf_op jit(solution)/shard_map/concatenate | solution.py:64
  5.9 1.6 %collective-permute-start.9 = (f32[256,256]{1,0:T(8,128)S(1)}, f32[256,256]{1,0:T(8,128)S(1)}, u32[]{:S(2)}, u32[]{:S(2)}) collective-permute-start(f32[256,256]{1,0:T(8,128)S(1)} %pad_maximum_fusion), channel_id=1, source_target_pairs={{0,2},{2,4},{4,6},{6,7},{7,5},{5,3},{3,1},{1,0},{8,9},{10,8},{12,1... | collective-permute-start | bytes 786440 | tf_op jit(solution)/shard_map/ppermute | solution.py:55
  8.0 1.5 %collective-permute-done.refs_1_ = f32[136,256]{1,0:T(8,128)S(1)} collective-permute-done((f32[136,256]{1,0:T(8,128)}, f32[136,256]{1,0:T(8,128)S(1)}, u32[]{:S(2)}, u32[]{:S(2)}) %collective-permute-start) | collective-permute-done | bytes 139296 | tf_op jit(solution)/shard_map/ppermute | solution.py:55
  9.5 1.7 %collective-permute-start.2 = (f32[136,256]{1,0:T(8,128)S(1)}, f32[136,256]{1,0:T(8,128)S(1)}, u32[]{:S(2)}, u32[]{:S(2)}) collective-permute-start(f32[136,256]{1,0:T(8,128)S(1)} %collective-permute-done.refs_1_), channel_id=1, source_target_pairs={{0,2},{2,4},{4,6},{6,7},{7,5},{5,3},{3,1},{1,0},{8,10},{10,12},{12... | collective-permute-start | bytes 417800 | tf_op jit(solution)/shard_map/ppermute | solution.py:55
  11.2 1.4 %collective-permute-done.9 = f32[256,256]{1,0:T(8,128)S(1)} collective-permute-done((f32[256,256]{1,0:T(8,128)S(1)}, f32[256,256]{1,0:T(8,128)S(1)}, u32[]{:S(2)}, u32[]{:S(2)}) %collective-permute-start.9) | collective-permute-done | bytes 262176 | tf_op jit(solution)/shard_map/ppermute | solution.py:55
  12.6 1.9 %collective-permute-start.11 = (f32[256,256]{1,0:T(8,128)S(1)}, f32[256,256]{1,0:T(8,128)S(1)}, u32[]{:S(2)}, u32[]{:S(2)}) collective-permute-start(f32[256,256]{1,0:T(8,128)S(1)} %collective-permute-done.9), channel_id=1, source_target_pairs={{0,2},{2,4},{4,6},{6,7},{7,5},{5,3},{3,1},{1,0},{8,9},{10,8},{12,1... | collective-permute-start | bytes 786440 | tf_op jit(solution)/shard_map/ppermute | solution.py:55
  15.3 1.7 %collective-permute-start.4 = (f32[136,256]{1,0:T(8,128)S(1)}, f32[136,256]{1,0:T(8,128)S(1)}, u32[]{:S(2)}, u32[]{:S(2)}) collective-permute-start(f32[136,256]{1,0:T(8,128)S(1)} %collective-permute-done.2.refs_3_), channel_id=1, source_target_pairs={{0,2},{2,4},{4,6},{6,7},{7,5},{5,3},{3,1},{1,0},{8,10},{10,12},{12... | collective-permute-start | bytes 417800 | tf_op jit(solution)/shard_map/ppermute | solution.py:55
  17.0 3.4 %collective-permute-done.3.refs_4_ = f32[136,256]{1,0:T(8,128)S(1)} collective-permute-done((f32[136,256]{1,0:T(8,128)S(1)}, f32[136,256]{1,0:T(8,128)S(1)}, u32[]{:S(2)}, u32[]{:S(2)}) %collective-permute-start.3) | collective-permute-done | bytes 139296 | tf_op jit(solution)/shard_map/ppermute | solution.py:55
  22.0 1.9 %collective-permute-start.6 = (f32[136,256]{1,0:T(8,128)S(1)}, f32[136,256]{1,0:T(8,128)S(1)}, u32[]{:S(2)}, u32[]{:S(2)}) collective-permute-start(f32[136,256]{1,0:T(8,128)S(1)} %collective-permute-done.4.refs_5_), channel_id=1, source_target_pairs={{0,2},{2,4},{4,6},{6,7},{7,5},{5,3},{3,1},{1,0},{8,10},{10,12},{12... | collective-permute-start | bytes 417800 | tf_op jit(solution)/shard_map/ppermute | solution.py:55
  23.9 1.6 %collective-permute-start.13 = (f32[256,256]{1,0:T(8,128)S(1)}, f32[256,256]{1,0:T(8,128)S(1)}, u32[]{:S(2)}, u32[]{:S(2)}) collective-permute-start(f32[256,256]{1,0:T(8,128)S(1)} %collective-permute-done.11), channel_id=1, source_target_pairs={{0,2},{2,4},{4,6},{6,7},{7,5},{5,3},{3,1},{1,0},{8,9},{10,8},{12,1... | collective-permute-start | bytes 786440 | tf_op jit(solution)/shard_map/ppermute | solution.py:55
  25.5 1.2 %collective-permute-done.5.refs_6_ = f32[136,256]{1,0:T(8,128)S(1)} collective-permute-done((f32[136,256]{1,0:T(8,128)S(1)}, f32[136,256]{1,0:T(8,128)S(1)}, u32[]{:S(2)}, u32[]{:S(2)}) %collective-permute-start.5) | collective-permute-done | bytes 139296 | tf_op jit(solution)/shard_map/ppermute | solution.py:55
  26.7 1.5 %collective-permute-done.6.refs_7_ = f32[136,256]{1,0:T(8,128)S(1)} collective-permute-done((f32[136,256]{1,0:T(8,128)S(1)}, f32[136,256]{1,0:T(8,128)S(1)}, u32[]{:S(2)}, u32[]{:S(2)}) %collective-permute-start.6) | collective-permute-done | bytes 139296 | tf_op jit(solution)/shard_map/ppermute | solution.py:55
  31.2 1.5 %collective-permute-start.16 = (f32[256,128]{1,0:T(8,128)S(1)}, f32[256,128]{1,0:T(8,128)S(1)}, u32[]{:S(2)}, u32[]{:S(2)}) collective-permute-start(f32[256,128]{1,0:T(8,128)S(1)} %get-tuple-element.24.mine_ref), channel_id=1, source_target_pairs={{0,16},{8,24},{16,0},{24,8},{1,17},{9,25},{17,1},{25,9},{2,18},{10... | collective-permute-start | bytes 393224 | tf_op jit(solution)/shard_map/ppermute | solution.py:36
  34.3 2.5 %collective-permute-done.16.got_ref = f32[256,128]{1,0:T(8,128)S(1)} collective-permute-done((f32[256,128]{1,0:T(8,128)S(1)}, f32[256,128]{1,0:T(8,128)S(1)}, u32[]{:S(2)}, u32[]{:S(2)}) %collective-permute-start.16) | collective-permute-done | bytes 131104 | tf_op jit(solution)/shard_map/ppermute | solution.py:36
  36.8 1.0 %collective-permute-done.15.refs_7_ = f32[128,256]{1,0:T(8,128)S(1)} collective-permute-done((f32[128,256]{1,0:T(8,128)S(1)}, f32[128,256]{1,0:T(8,128)S(1)}, u32[]{:S(2)}, u32[]{:S(2)}) %collective-permute-start.15) | collective-permute-done | bytes 131104 | tf_op jit(solution)/shard_map/ppermute | solution.py:55
  38.1 1.3 %collective-permute-done.17.refs_9_ = f32[256,128]{1,0:T(8,128)S(1)} collective-permute-done((f32[256,128]{1,0:T(8,128)S(1)}, f32[256,128]{1,0:T(8,128)S(1)}, u32[]{:S(2)}, u32[]{:S(2)}) %collective-permute-start.17) | collective-permute-done | bytes 131104 | tf_op jit(solution)/shard_map/ppermute | solution.py:36
  39.4 1.4 %shard_map.50 = (f32[256,128]{1,0:T(8,128)S(1)}, f32[256,128]{1,0:T(8,128)S(1)}) custom-call(f32[128,256]{1,0:T(8,128)S(1)} %copy-done.1, f32[128,256]{1,0:T(8,128)S(1)} %get-tuple-element.38.refs_1_, f32[128,256]{1,0:T(8,128)S(1)} %collective-permute-done.10.refs_2_, f32[128,256]{1,0:T(8,128)S(1)} %get-tuple-element.36.refs_3_, ...), custom_call_target="tpu_custom_call" | custom-call | tf_op jit(solution)/shard_map/pallas_call | solution.py:269
  41.1 1.2 %collective-permute-done.18.got_ref = f32[256,128]{1,0:T(8,128)S(1)} collective-permute-done((f32[256,128]{1,0:T(8,128)S(1)}, f32[256,128]{1,0:T(8,128)S(1)}, u32[]{:S(2)}, u32[]{:S(2)}) %collective-permute-start.18) | collective-permute-done | bytes 131104 | tf_op jit(solution)/shard_map/ppermute | solution.py:36
  43.0 5.0 %collective-permute-done.19.refs_10_ = f32[256,128]{1,0:T(8,128)S(1)} collective-permute-done((f32[256,128]{1,0:T(8,128)S(1)}, f32[256,128]{1,0:T(8,128)S(1)}, u32[]{:S(2)}, u32[]{:S(2)}) %collective-permute-start.19) | collective-permute-done | bytes 131104 | tf_op jit(solution)/shard_map/ppermute | solution.py:36
  48.0 1.0 %shard_map.52 = (f32[256,128]{1,0:T(8,128)S(1)}, f32[256,128]{1,0:T(8,128)S(1)}, f32[32,64]{1,0:T(8,128)S(1)}) custom-call(f32[136,256]{1,0:T(8,128)S(1)} %copy-done, f32[136,256]{1,0:T(8,128)S(1)} %collective-permute-done.refs_1_, f32[136,256]{1,0:T(8,128)S(1)} %collective-permute-done.1.refs_2_, f32[136,256]{1,0:T(8,128)S(1)} %collective-permute-done.2.refs_3_, ...), custom_call_target="tpu_custom_call" | custom-call | tf_op jit(solution)/shard_map/pallas_call | solution.py:269
  49.1 1.3 %collective-permute-done.20.refs_10_ = f32[256,128]{1,0:T(8,128)S(1)} collective-permute-done((f32[256,128]{1,0:T(8,128)S(1)}, f32[256,128]{1,0:T(8,128)S(1)}, u32[]{:S(2)}, u32[]{:S(2)}) %collective-permute-start.20) | collective-permute-done | bytes 131104 | tf_op jit(solution)/shard_map/ppermute | solution.py:36
  50.5 1.2 %shard_map.53 = f32[3,32,64]{2,1,0:T(8,128)} custom-call(f32[136,256]{1,0:T(8,128)S(1)} %copy-done, f32[136,256]{1,0:T(8,128)S(1)} %collective-permute-done.refs_1_, f32[136,256]{1,0:T(8,128)S(1)} %collective-permute-done.1.refs_2_, f32[136,256]{1,0:T(8,128)S(1)} %collective-permute-done.2.refs_3_, f32[136,256]{1,0:T(8,128)S(1)} %collective-permute-done.3.refs_4_, ...), custom_call_target="tpu_custom_call" | custom-call | tf_op jit(solution)/shard_map/pallas_call | solution.py:269
  (34 shorter events, 9.2 us)
Async XLA Ops:
  1.8 3.2 %collective-permute-start.8 = (f32[128,256]{1,0:T(8,128)}, f32[128,256]{1,0:T(8,128)S(1)}, u32[]{:S(2)}, u32[]{:S(2)}) collective-permute-start(f32[128,256]{1,0:T(8,128)} %get-tuple-element.23.refs_0_), channel_id=1, source_target_pairs={{0,8},{8,0},{16,24},{24,16},{1,9},{9,1},{17,25},{25,17},{2,10},{10... | collective-permute-start | bytes 393224 | tf_op jit(solution)/shard_map/ppermute | solution.py:36
  2.4 5.2 %copy-start = (f32[136,256]{1,0:T(8,128)S(1)}, f32[136,256]{1,0:T(8,128)}, u32[]{:S(2)}) copy-start(f32[136,256]{1,0:T(8,128)} %get-tuple-element.19.refs_0_) | copy-start | bytes 417796
  2.4 7.1 %collective-permute-start = (f32[136,256]{1,0:T(8,128)}, f32[136,256]{1,0:T(8,128)S(1)}, u32[]{:S(2)}, u32[]{:S(2)}) collective-permute-start(f32[136,256]{1,0:T(8,128)} %get-tuple-element.19.refs_0_), channel_id=1, source_target_pairs={{0,2},{2,4},{4,6},{6,7},{7,5},{5,3},{3,1},{1,0},{8,10},{10,12},{12... | collective-permute-start | bytes 417800 | tf_op jit(solution)/shard_map/ppermute | solution.py:55
  5.9 6.7 %collective-permute-start.9 = (f32[256,256]{1,0:T(8,128)S(1)}, f32[256,256]{1,0:T(8,128)S(1)}, u32[]{:S(2)}, u32[]{:S(2)}) collective-permute-start(f32[256,256]{1,0:T(8,128)S(1)} %pad_maximum_fusion), channel_id=1, source_target_pairs={{0,2},{2,4},{4,6},{6,7},{7,5},{5,3},{3,1},{1,0},{8,9},{10,8},{12,1... | collective-permute-start | bytes 786440 | tf_op jit(solution)/shard_map/ppermute | solution.py:55
  7.6 7.0 %collective-permute-start.1 = (f32[136,256]{1,0:T(8,128)S(1)}, f32[136,256]{1,0:T(8,128)S(1)}, u32[]{:S(2)}, u32[]{:S(2)}) collective-permute-start(f32[136,256]{1,0:T(8,128)S(1)} %copy-done), channel_id=1, source_target_pairs={{0,1},{2,0},{4,2},{6,4},{7,6},{5,7},{3,5},{1,3},{8,9},{10,8},{12,1... | collective-permute-start | bytes 417800 | tf_op jit(solution)/shard_map/ppermute | solution.py:55
  9.5 5.8 %collective-permute-start.2 = (f32[136,256]{1,0:T(8,128)S(1)}, f32[136,256]{1,0:T(8,128)S(1)}, u32[]{:S(2)}, u32[]{:S(2)}) collective-permute-start(f32[136,256]{1,0:T(8,128)S(1)} %collective-permute-done.refs_1_), channel_id=1, source_target_pairs={{0,2},{2,4},{4,6},{6,7},{7,5},{5,3},{3,1},{1,0},{8,10},{10,12},{12... | collective-permute-start | bytes 417800 | tf_op jit(solution)/shard_map/ppermute | solution.py:55
  12.6 11.3 %collective-permute-start.11 = (f32[256,256]{1,0:T(8,128)S(1)}, f32[256,256]{1,0:T(8,128)S(1)}, u32[]{:S(2)}, u32[]{:S(2)}) collective-permute-start(f32[256,256]{1,0:T(8,128)S(1)} %collective-permute-done.9), channel_id=1, source_target_pairs={{0,2},{2,4},{4,6},{6,7},{7,5},{5,3},{3,1},{1,0},{8,9},{10,8},{12,1... | collective-permute-start | bytes 786440 | tf_op jit(solution)/shard_map/ppermute | solution.py:55
  14.5 5.8 %collective-permute-start.3 = (f32[136,256]{1,0:T(8,128)S(1)}, f32[136,256]{1,0:T(8,128)S(1)}, u32[]{:S(2)}, u32[]{:S(2)}) collective-permute-start(f32[136,256]{1,0:T(8,128)S(1)} %collective-permute-done.1.refs_2_), channel_id=1, source_target_pairs={{0,1},{2,0},{4,2},{6,4},{7,6},{5,7},{3,5},{1,3},{8,9},{10,8},{12,1... | collective-permute-start | bytes 417800 | tf_op jit(solution)/shard_map/ppermute | solution.py:55
  15.3 6.6 %collective-permute-start.4 = (f32[136,256]{1,0:T(8,128)S(1)}, f32[136,256]{1,0:T(8,128)S(1)}, u32[]{:S(2)}, u32[]{:S(2)}) collective-permute-start(f32[136,256]{1,0:T(8,128)S(1)} %collective-permute-done.2.refs_3_), channel_id=1, source_target_pairs={{0,2},{2,4},{4,6},{6,7},{7,5},{5,3},{3,1},{1,0},{8,10},{10,12},{12... | collective-permute-start | bytes 417800 | tf_op jit(solution)/shard_map/ppermute | solution.py:55
  20.4 6.3 %collective-permute-start.5 = (f32[136,256]{1,0:T(8,128)S(1)}, f32[136,256]{1,0:T(8,128)S(1)}, u32[]{:S(2)}, u32[]{:S(2)}) collective-permute-start(f32[136,256]{1,0:T(8,128)S(1)} %collective-permute-done.3.refs_4_), channel_id=1, source_target_pairs={{0,1},{2,0},{4,2},{6,4},{7,6},{5,7},{3,5},{1,3},{8,9},{10,8},{12,1... | collective-permute-start | bytes 417800 | tf_op jit(solution)/shard_map/ppermute | solution.py:55
  22.0 6.2 %collective-permute-start.6 = (f32[136,256]{1,0:T(8,128)S(1)}, f32[136,256]{1,0:T(8,128)S(1)}, u32[]{:S(2)}, u32[]{:S(2)}) collective-permute-start(f32[136,256]{1,0:T(8,128)S(1)} %collective-permute-done.4.refs_5_), channel_id=1, source_target_pairs={{0,2},{2,4},{4,6},{6,7},{7,5},{5,3},{3,1},{1,0},{8,10},{10,12},{12... | collective-permute-start | bytes 417800 | tf_op jit(solution)/shard_map/ppermute | solution.py:55
  23.9 8.9 %collective-permute-start.13 = (f32[256,256]{1,0:T(8,128)S(1)}, f32[256,256]{1,0:T(8,128)S(1)}, u32[]{:S(2)}, u32[]{:S(2)}) collective-permute-start(f32[256,256]{1,0:T(8,128)S(1)} %collective-permute-done.11), channel_id=1, source_target_pairs={{0,2},{2,4},{4,6},{6,7},{7,5},{5,3},{3,1},{1,0},{8,9},{10,8},{12,1... | collective-permute-start | bytes 786440 | tf_op jit(solution)/shard_map/ppermute | solution.py:55
  29.0 1.4 %collective-permute-start.7 = (f32[256,128]{1,0:T(8,128)S(1)}, f32[256,128]{1,0:T(8,128)S(1)}, u32[]{:S(2)}, u32[]{:S(2)}) collective-permute-start(f32[256,128]{1,0:T(8,128)S(1)} %get-tuple-element.21.refs_8_), channel_id=1, source_target_pairs={{0,8},{8,0},{16,24},{24,16},{1,9},{9,1},{17,25},{25,17},{2,10},{10... | collective-permute-start | bytes 393224 | tf_op jit(solution)/shard_map/ppermute | solution.py:36
  29.1 9.0 %collective-permute-start.10 = (f32[128,256]{1,0:T(8,128)S(1)}, f32[128,256]{1,0:T(8,128)S(1)}, u32[]{:S(2)}, u32[]{:S(2)}) collective-permute-start(f32[128,256]{1,0:T(8,128)S(1)} %get-tuple-element.37), channel_id=1, source_target_pairs={{0,8},{8,0},{16,24},{24,16},{1,9},{9,1},{17,25},{25,17},{2,10},{10... | collective-permute-start | bytes 393224 | tf_op jit(solution)/shard_map/ppermute | solution.py:36
  31.2 5.6 %collective-permute-start.16 = (f32[256,128]{1,0:T(8,128)S(1)}, f32[256,128]{1,0:T(8,128)S(1)}, u32[]{:S(2)}, u32[]{:S(2)}) collective-permute-start(f32[256,128]{1,0:T(8,128)S(1)} %get-tuple-element.24.mine_ref), channel_id=1, source_target_pairs={{0,16},{8,24},{16,0},{24,8},{1,17},{9,25},{17,1},{25,9},{2,18},{10... | collective-permute-start | bytes 393224 | tf_op jit(solution)/shard_map/ppermute | solution.py:36
  32.8 5.0 %collective-permute-start.15 = (f32[128,256]{1,0:T(8,128)S(1)}, f32[128,256]{1,0:T(8,128)S(1)}, u32[]{:S(2)}, u32[]{:S(2)}) collective-permute-start(f32[128,256]{1,0:T(8,128)S(1)} %get-tuple-element.34.refs_5_), channel_id=1, source_target_pairs={{0,2},{2,4},{4,6},{6,7},{7,5},{5,3},{3,1},{1,0},{8,9},{10,8},{12,1... | collective-permute-start | bytes 393224 | tf_op jit(solution)/shard_map/ppermute | solution.py:55
  33.6 4.5 %collective-permute-start.12 = (f32[128,256]{1,0:T(8,128)S(1)}, f32[128,256]{1,0:T(8,128)S(1)}, u32[]{:S(2)}, u32[]{:S(2)}) collective-permute-start(f32[128,256]{1,0:T(8,128)S(1)} %get-tuple-element.35), channel_id=1, source_target_pairs={{0,8},{8,0},{16,24},{24,16},{1,9},{9,1},{17,25},{25,17},{2,10},{10... | collective-permute-start | bytes 393224 | tf_op jit(solution)/shard_map/ppermute | solution.py:36
  34.3 5.2 %copy-start.1 = (f32[128,256]{1,0:T(8,128)S(1)}, f32[128,256]{1,0:T(8,128)}, u32[]{:S(2)}) copy-start(f32[128,256]{1,0:T(8,128)} %get-tuple-element.23.refs_0_) | copy-start | bytes 393220
  34.3 3.9 %collective-permute-start.14 = (f32[128,256]{1,0:T(8,128)S(1)}, f32[128,256]{1,0:T(8,128)S(1)}, u32[]{:S(2)}, u32[]{:S(2)}) collective-permute-start(f32[128,256]{1,0:T(8,128)S(1)} %get-tuple-element.33), channel_id=1, source_target_pairs={{0,8},{8,0},{16,24},{24,16},{1,9},{9,1},{17,25},{25,17},{2,10},{10... | collective-permute-start | bytes 393224 | tf_op jit(solution)/shard_map/ppermute | solution.py:36
  38.0 1.4 %collective-permute-start.17 = (f32[256,128]{1,0:T(8,128)S(1)}, f32[256,128]{1,0:T(8,128)S(1)}, u32[]{:S(2)}, u32[]{:S(2)}) collective-permute-start(f32[256,128]{1,0:T(8,128)S(1)} %shard_map.49.refs_8_), channel_id=1, source_target_pairs={{0,8},{8,0},{16,24},{24,16},{1,9},{9,1},{17,25},{25,17},{2,10},{10... | collective-permute-start | bytes 393224 | tf_op jit(solution)/shard_map/ppermute | solution.py:36
  40.9 1.4 %collective-permute-start.18 = (f32[256,128]{1,0:T(8,128)S(1)}, f32[256,128]{1,0:T(8,128)S(1)}, u32[]{:S(2)}, u32[]{:S(2)}) collective-permute-start(f32[256,128]{1,0:T(8,128)S(1)} %get-tuple-element.27), channel_id=1, source_target_pairs={{0,8},{8,0},{16,24},{24,16},{1,9},{9,1},{17,25},{25,17},{2,10},{10... | collective-permute-start | bytes 393224 | tf_op jit(solution)/shard_map/ppermute | solution.py:36
  42.4 5.6 %collective-permute-start.19 = (f32[256,128]{1,0:T(8,128)S(1)}, f32[256,128]{1,0:T(8,128)S(1)}, u32[]{:S(2)}, u32[]{:S(2)}) collective-permute-start(f32[256,128]{1,0:T(8,128)S(1)} %get-tuple-element.29), channel_id=1, source_target_pairs={{0,16},{8,24},{16,0},{24,8},{1,17},{9,25},{17,1},{25,9},{2,18},{10... | collective-permute-start | bytes 393224 | tf_op jit(solution)/shard_map/ppermute | solution.py:36
  49.0 1.4 %collective-permute-start.20 = (f32[256,128]{1,0:T(8,128)S(1)}, f32[256,128]{1,0:T(8,128)S(1)}, u32[]{:S(2)}, u32[]{:S(2)}) collective-permute-start(f32[256,128]{1,0:T(8,128)S(1)} %get-tuple-element.31), channel_id=1, source_target_pairs={{0,8},{8,0},{16,24},{24,16},{1,9},{9,1},{17,25},{25,17},{2,10},{10... | collective-permute-start | bytes 393224 | tf_op jit(solution)/shard_map/ppermute | solution.py:36

commit v6 on v5

--- a/solution.py
+++ b/solution.py
@@ -16,19 +16,30 @@
 
 
 def product(a, b, dims):
-    def term(x, y):
-        return lax.dot_general(x, y, (dims, ((), ())), preferred_element_type=jnp.float32)
-
     (a_high, a_low), (b_high, b_low) = a, b
-    return term(a_high, b_high) + (term(a_high, b_low) + term(a_low, b_high))
-
-
-def dot(a, b):
-    return product(split(a), split(b), ((1,), (0,)))
-
-
-def dot_t(a, b):
-    return product(split(a), split(b), ((0,), (0,)))
+    return term(a_high, b_high, dims) + (term(a_high, b_low, dims) + term(a_low, b_high, dims))
+
+
+def term(x, y, dims):
+    return lax.dot_general(x, y, (dims, ((), ())), preferred_element_type=jnp.float32)
+
+
+def dot_small(a, b):
+    (a_high, a_low), (b_high, b_low) = split(a), split(b)
+    return term(
+        jnp.concatenate([a_high, a_high, a_low], axis=1),
+        jnp.concatenate([b_high, b_low, b_high], axis=0),
+        ((1,), (0,)),
+    )
+
+
+def dot_t_small(a, b):
+    (a_high, a_low), (b_high, b_low) = split(a), split(b)
+    return term(
+        jnp.concatenate([a_high, a_high, a_low], axis=0),
+        jnp.concatenate([b_high, b_low, b_high], axis=0),
+        ((0,), (0,)),
+    )
 
 
 def swap(block, axis, mask):
@@ -59,21 +70,27 @@
     return [0] + [x for r in range(1, count // 2) for x in (r, -r)] + [count // 2]
 
 
-def gather_rows(block):
+def gather_rows(block, AFTER={}):
     height = block.shape[0]
     moving = jnp.concatenate([block, swap(block, "cube", 1)], axis=0)
     out = [block]
-    for _ in range(1, lax.axis_size("blk") // 2):
+    for r in range(1, lax.axis_size("blk") // 2):
+        if r in AFTER:
+            moving = tie(moving, AFTER[r])
         moving = ring_step(moving, 1, -1)
         out += [moving[:height], swap(moving[height:], "cube", 1)]
+    if 4 in AFTER:
+        moving = tie(moving, AFTER[4])
     return out + [ring_step(moving[:height], 1, -1)]
 
 
-def gather_both_ways(block):
+def gather_both_ways(block, JOINT=()):
     out = [block]
     up = down = block
-    for _ in range(1, lax.axis_size("blk") // 2):
+    for r in range(1, lax.axis_size("blk") // 2):
         up, down = ring_step(up, 1, 1), ring_step(down, -1, -1)
+        if r in JOINT:
+            up, down = lax.optimization_barrier((up, down))
         out += [up, down]
     return out + [ring_step(up, 1, 1)]
 
@@ -102,12 +119,8 @@
         )
 
     def extend(self, piece, level):
-        rows = self.rows
-        first = (self.levels - 1) * self.cols + level * 2 * rows
-        return jnp.concatenate(
-            [piece[self.top : self.top + rows, first + h * rows : first + (h + 1) * rows] for h in (0, 1)],
-            axis=0,
-        )
+        first = (self.levels - 1) * self.cols + level * 2 * self.rows
+        return piece[self.top : self.top + self.rows, first : first + 2 * self.rows]
 
     def diag(self, pieces, level, diag_ref, place_of, first=None):
         first = (2**level - 1) * self.rows if first is None else first
@@ -138,7 +151,13 @@
             names = maps_ref[l, 0, 0, h : h + 1, :]
             onehot = jnp.where(row_ids == names, 1.0, 0.0).astype(jnp.float32)
             parts.append(
-                jnp.dot(onehot, panel, precision=lax.Precision.HIGHEST, preferred_element_type=jnp.float32)
+                lax.dot_general(
+                    panel,
+                    onehot,
+                    (((0,), (1,)), ((), ())),
+                    precision=lax.Precision.HIGHEST,
+                    preferred_element_type=jnp.float32,
+                )
             )
     out_ref[pk.top : pk.top + rows, :] = jnp.concatenate(parts, axis=1)
     last = rhs_ref[pk.levels - 1, 0, 0]
@@ -165,9 +184,15 @@
     rows, cols = pk.rows, pk.cols
     for m, piece in enumerate(pieces):
         place = block_of(pk, m)
-        e = dot(pk.extend(piece, level), y_ref[place, :])
+        e = dot_t_small(pk.extend(piece, level), y_ref[place, :])
         send_ref[place, :cols] = pk.rhs(piece, level + 1) - e[:rows]
         send_ref[place, cols:] = e[rows:]
+
+
+def split_kernel(pk, level, place_of, first, *refs):
+    pieces, (high_ref, low_ref, diag_ref) = refs[: pk.n_blk], refs[pk.n_blk :]
+    pk.diag(pieces, level, diag_ref, place_of, first)
+    high_ref[...], low_ref[...] = split(diag_ref[...])
 
 
 def first_kernel(pk, *refs):
@@ -175,19 +200,18 @@
     pk.diag(pieces, 0, diag_ref, block_of)
     for m, piece in enumerate(pieces):
         z_ref[block_of(pk, m), :] = pk.rhs(piece, 0)
-    y_ref[...] = dot_t(diag_ref[...], z_ref[...])
+    y_ref[...] = product(split(diag_ref[...]), split(z_ref[...]), ((0,), (0,)))
     extend_out(pk, 0, pieces, y_ref, send_ref)
 
 
 def middle_kernel(pk, *refs):
-    pieces, (mine_ref, got_ref, send_ref, y_ref, diag_ref) = refs[: pk.n_blk], refs[pk.n_blk :]
+    pieces, (high_ref, low_ref, mine_ref, got_ref, send_ref, y_ref) = refs[: pk.n_blk], refs[pk.n_blk :]
     cols = pk.cols
     own = mine_ref[:, :cols] - got_ref[:, cols:]
     other = got_ref[:, :cols] - mine_ref[:, cols:]
     upper = lax.axis_index("cube") % 2 == 1
     z = jnp.concatenate([jnp.where(upper, other, own), jnp.where(upper, own, other)], axis=0)
-    pk.diag(pieces, 1, diag_ref, block_of)
-    y_ref[...] = dot_t(diag_ref[...], z)
+    y_ref[...] = product((high_ref[...], low_ref[...]), split(z), ((0,), (0,)))
     extend_out(pk, 1, pieces, y_ref, send_ref)
 
 
@@ -197,20 +221,18 @@
     out_ref[:, cols:] = got_ref[:, :cols] - mine_ref[:, cols:]
 
 
-def top_kernel(pk, *refs):
-    pieces, (mine_ref, got_ref, keep_ref, send_ref, diag_ref, vec_ref) = refs[: pk.n_blk], refs[pk.n_blk :]
+def top_kernel(pk, high_ref, low_ref, mine_ref, got_ref, keep_ref, send_ref, vec_ref):
     node, cols = pk.width, pk.cols
     cube = lax.axis_index("cube")
 
     def part(k):
         return pl.ds(pl.multiple_of((cube ^ k) * node, node), node)
 
-    pk.diag(pieces, 2, diag_ref, shared_block_of, 0)
     vec_ref[part(0), :] = mine_ref[:, :cols]
     vec_ref[part(2), :] = mine_ref[:, cols:]
     vec_ref[part(1), :] = got_ref[:, :cols]
     vec_ref[part(3), :] = got_ref[:, cols:]
-    diag = split(diag_ref[...])
+    diag = (high_ref[...], low_ref[...])
     y = product(diag, split(vec_ref[...]), ((0,), (0,)))
     vec_ref[...] = product(diag, split(y), ((1,), (0,)))
     keep_ref[:, :cols] = vec_ref[part(0), :]
@@ -233,18 +255,17 @@
         place = block_of(pk, m)
         pair = mine_ref[place, :] + got_ref[place, :]
         both = jnp.concatenate([pair[:, :cols], pair[:, cols:]], axis=0)
-        w_ref[place, :] = y_ref[place, :] - dot_t(pk.extend(piece, level), both)
+        w_ref[place, :] = y_ref[place, :] - dot_small(pk.extend(piece, level), both)
 
 
 def down_kernel(pk, *refs):
     pieces, refs = refs[: pk.n_blk], refs[pk.n_blk :]
-    y_ref, mine_ref, got_ref, keep_ref, send_ref, top_ref, w_ref, diag_ref = refs
+    high_ref, low_ref, y_ref, mine_ref, got_ref, keep_ref, send_ref, top_ref, w_ref = refs
     node, cols = pk.width, pk.cols
     own_rows = block_of(pk, 0)
     top_ref[...] = mine_ref[own_rows, :cols] + got_ref[own_rows, :cols]
-    pk.diag(pieces, 1, diag_ref, block_of)
     reduce_rows(pk, 1, pieces, y_ref, mine_ref, got_ref, w_ref)
-    x = dot(diag_ref[...], w_ref[...])
+    x = product((high_ref[...], low_ref[...]), split(w_ref[...]), ((1,), (0,)))
     upper = lax.axis_index("cube") % 2 == 1
     own = jnp.where(upper, x[node:], x[:node])
     other = jnp.where(upper, x[:node], x[node:])
@@ -261,16 +282,15 @@
     out_ref[2] = top_ref[...]
     out_ref[1] = mine_ref[own_rows, :cols] + got_ref[own_rows, :cols]
     reduce_rows(pk, 0, pieces, y_ref, mine_ref, got_ref, w_ref)
-    out_ref[0] = dot(pieces[0][: pk.rows, :], w_ref[...])
-
-
-def call(kernel, pk, args, outs, scratch=(), place=pltpu.VMEM, room=24):
-    vmem = pl.BlockSpec(memory_space=pltpu.VMEM)
+    out_ref[0] = product(split(pieces[0][: pk.rows, :]), split(w_ref[...]), ((1,), (0,)))
+
+
+def call(kernel, pk, args, outs, scratch=(), place=pltpu.VMEM, room=24, kind=jnp.float32):
     return pl.pallas_call(
         functools.partial(kernel, pk),
-        out_shape=[jax.ShapeDtypeStruct(s, jnp.float32) for s in outs],
+        out_shape=[jax.ShapeDtypeStruct(s, kind) for s in outs],
         in_specs=[pl.BlockSpec(memory_space=place)] * len(args),
-        out_specs=[vmem] * len(outs),
+        out_specs=[pl.BlockSpec(memory_space=pltpu.VMEM)] * len(outs),
         scratch_shapes=scratch,
         compiler_params=pltpu.CompilerParams(vmem_limit_bytes=room * 2**20),
     )(*args)
@@ -286,6 +306,17 @@
 
     def work(*shapes):
         return [pltpu.VMEM(s, jnp.float32) for s in shapes]
+
+    def split_diag(pieces, level, place_of, first):
+        shape = (2**level * node, node)
+        return call(
+            lambda pk, *refs: split_kernel(pk, level, place_of, first, *refs),
+            pk,
+            pieces,
+            [shape, shape],
+            work(shape),
+            kind=jnp.bfloat16,
+        )
 
     inputs = [right_side, panels, extend_map, diag_inverse]
     packed, top = call(
@@ -293,25 +324,26 @@
         pk,
         inputs,
         [(pk.height, node), (diag_inverse.shape[0] - pk.top, node)],
-        [pltpu.VMEM(a.shape, a.dtype) for a in inputs[:3]] + [pltpu.SemaphoreType.DMA((5,))],
+        [pltpu.VMEM(a.shape, a.dtype) for a in inputs[:3]]
+        + [pltpu.SemaphoreType.DMA((5,))],
         pltpu.HBM,
-        60,
-    )
-    first = gather_both_ways(packed)
-    last = gather_rows(top)
+        room=60,
+    )
+    first = gather_both_ways(packed, ())
+    last = gather_rows(top, {})
     send, y0 = call(first_kernel, pk, first, [two, one], work((node, node), one))
     got = swap(send, "cube", 1)
-    send, y1 = call(middle_kernel, pk, [*first, send, got], [two, one], work((2 * node, node)))
+    diag1 = split_diag(first, 1, block_of, None)
+    send, y1 = call(middle_kernel, pk, [*first, *diag1, send, got], [two, one])
     got = tie(swap(send, "cube", 2), last[7])
     (held,) = call(meet_kernel, pk, [send, got], [two])
     got = swap(held, "cube", 1)
-    keep, send = call(
-        top_kernel, pk, [*last, held, got], [two, two], work((4 * node, node), (4 * node, cols))
-    )
+    diag2 = split_diag(last, 2, shared_block_of, 0)
+    keep, send = call(top_kernel, pk, [*diag2, held, got], [two, two], work((4 * node, cols)))
     held, send = call(turn_kernel, pk, [keep, swap(send, "cube", 1)], [two, two])
     got = swap(send, "cube", 2)
     keep, send, top = call(
-        down_kernel, pk, [*first, y1, held, got], [two, two, (rows, cols)], work(one, (2 * node, node))
+        down_kernel, pk, [*first, *diag1, y1, held, got], [two, two, (rows, cols)], work(one)
     )
     got = swap(send, "cube", 1)
     (out,) = call(last_kernel, pk, [*first, y0, keep, got, top], [(3, rows, cols)], work(one))

time: 51.8 us -> 51.4 us (level)
  waiting for transfers between devices: 23.5 us -> 22.9 us
    ppermute x10, waiting for transfers between devices: 12.1 us -> 11.5 us  [swap(): return lax.ppermute(block, axis, [(i, i ^ mask) for i in range(count)])]
    pallas_call x8 -> x10, Pallas kernels: 7.43 us -> 7.53 us  [call(): pl.pallas_call(functools.partial(kernel, pk), out_shape=[jax.ShapeDtypeSt...]
  transfers between devices with their start and end apart: 21 -> 21, of which waited for: 14 -> 14; matrix products, arithmetic and copies ran while one was open for 2% -> 2% of each run, Pallas kernels for 3% -> 4%
where the time goes in v6:
time: 51.4 us; the launch traced here: 51.3 us
  waiting for transfers between devices  22.9 us (45%)
  starting transfers between devices  19.7 us (38%)
  Pallas kernels  7.53 us (15%)
  other arithmetic  0.92 us (2%)
    ppermute x11, starting transfers between devices, ring_step(): return lax.ppermute(block, ('cube', 'blk'), route)  15.3 us
    ppermute x10, waiting for transfers between devices, swap(): return lax.ppermute(block, axis, [(i, i ^ mask) for i in range(count)])  11.5 us
    ppermute x11, waiting for transfers between devices, ring_step(): return lax.ppermute(block, ('cube', 'blk'), route)  11.4 us
    pallas_call x10, Pallas kernels, call(): pl.pallas_call(functools.partial(kernel, pk), out_shape=[jax.ShapeDtypeSt...  7.53 us
    ppermute x10, starting transfers between devices, swap(): return lax.ppermute(block, axis, [(i, i ^ mask) for i in range(count)])  4.38 us
  transfers between devices with their start and end apart: 21, of which 14 were waited for; matrix products, arithmetic and copies ran while one was open for 2% of the time, Pallas kernels for 4%

profile of v6, /device:TPU:0, one launch (start us, length us, event | category | flops | bytes accessed | tf_op | source)
XLA Modules:
  0.0 51.3 jit_solution(812237126417936571)
XLA Ops:
  0.0 1.9 %shard_map.46 = (f32[136,256]{1,0:T(8,128)}, f32[128,256]{1,0:T(8,128)}) custom-call(f32[3,1,1,32,64]{4,3,2,1,0:T(8,128)} %rhs_hbm.1, f32[2,1,1,2,16,32]{5,4,3,2,1,0:T(8,128)} %panels_hbm.1, s32[2,1,1,2,16]{4,3,2,1,0:T(2,128)} %maps_hbm.1, f32[224,256]{1,0:T(8,128)} %diag_hbm.1), custom_call_target="tpu_custom_call" | custom-call | tf_op jit(solution)/shard_map/pallas_call | solution.py:289
  2.5 2.6 %collective-permute-start = (f32[136,256]{1,0:T(8,128)}, f32[136,256]{1,0:T(8,128)S(1)}, u32[]{:S(2)}, u32[]{:S(2)}) collective-permute-start(f32[136,256]{1,0:T(8,128)} %get-tuple-element.23.refs_0_), channel_id=1, source_target_pairs={{0,2},{2,4},{4,6},{6,7},{7,5},{5,3},{3,1},{1,0},{8,10},{10,12},{12... | collective-permute-start | bytes 417800 | tf_op jit(solution)/shard_map/ppermute | solution.py:66
  5.1 0.9 %pad_maximum_fusion = f32[256,256]{1,0:T(8,128)S(1)} fusion(f32[128,256]{1,0:T(8,128)S(1)} %collective-permute-done.8, f32[128,256]{1,0:T(8,128)} %get-tuple-element.29.refs_0_), kind=kLoop, calls=%fused_computation | loop fusion | flops 65536 | bytes 524288 | tf_op jit(solution)/shard_map/concatenate | solution.py:75
  6.0 1.6 %collective-permute-start.9 = (f32[256,256]{1,0:T(8,128)S(1)}, f32[256,256]{1,0:T(8,128)S(1)}, u32[]{:S(2)}, u32[]{:S(2)}) collective-permute-start(f32[256,256]{1,0:T(8,128)S(1)} %pad_maximum_fusion), channel_id=1, source_target_pairs={{0,2},{2,4},{4,6},{6,7},{7,5},{5,3},{3,1},{1,0},{8,9},{10,8},{12,1... | collective-permute-start | bytes 786440 | tf_op jit(solution)/shard_map/ppermute | solution.py:66
  8.1 1.5 %collective-permute-done.refs_1_ = f32[136,256]{1,0:T(8,128)S(1)} collective-permute-done((f32[136,256]{1,0:T(8,128)}, f32[136,256]{1,0:T(8,128)S(1)}, u32[]{:S(2)}, u32[]{:S(2)}) %collective-permute-start) | collective-permute-done | bytes 139296 | tf_op jit(solution)/shard_map/ppermute | solution.py:66
  9.6 1.7 %collective-permute-start.2 = (f32[136,256]{1,0:T(8,128)S(1)}, f32[136,256]{1,0:T(8,128)S(1)}, u32[]{:S(2)}, u32[]{:S(2)}) collective-permute-start(f32[136,256]{1,0:T(8,128)S(1)} %collective-permute-done.refs_1_), channel_id=1, source_target_pairs={{0,2},{2,4},{4,6},{6,7},{7,5},{5,3},{3,1},{1,0},{8,10},{10,12},{12... | collective-permute-start | bytes 417800 | tf_op jit(solution)/shard_map/ppermute | solution.py:66
  11.3 1.4 %collective-permute-done.9 = f32[256,256]{1,0:T(8,128)S(1)} collective-permute-done((f32[256,256]{1,0:T(8,128)S(1)}, f32[256,256]{1,0:T(8,128)S(1)}, u32[]{:S(2)}, u32[]{:S(2)}) %collective-permute-start.9) | collective-permute-done | bytes 262176 | tf_op jit(solution)/shard_map/ppermute | solution.py:66
  12.7 1.9 %collective-permute-start.11 = (f32[256,256]{1,0:T(8,128)S(1)}, f32[256,256]{1,0:T(8,128)S(1)}, u32[]{:S(2)}, u32[]{:S(2)}) collective-permute-start(f32[256,256]{1,0:T(8,128)S(1)} %collective-permute-done.9), channel_id=1, source_target_pairs={{0,2},{2,4},{4,6},{6,7},{7,5},{5,3},{3,1},{1,0},{8,9},{10,8},{12,1... | collective-permute-start | bytes 786440 | tf_op jit(solution)/shard_map/ppermute | solution.py:66
  15.4 1.7 %collective-permute-start.4 = (f32[136,256]{1,0:T(8,128)S(1)}, f32[136,256]{1,0:T(8,128)S(1)}, u32[]{:S(2)}, u32[]{:S(2)}) collective-permute-start(f32[136,256]{1,0:T(8,128)S(1)} %collective-permute-done.2.refs_3_), channel_id=1, source_target_pairs={{0,2},{2,4},{4,6},{6,7},{7,5},{5,3},{3,1},{1,0},{8,10},{10,12},{12... | collective-permute-start | bytes 417800 | tf_op jit(solution)/shard_map/ppermute | solution.py:66
  17.1 3.4 %collective-permute-done.3.refs_4_ = f32[136,256]{1,0:T(8,128)S(1)} collective-permute-done((f32[136,256]{1,0:T(8,128)S(1)}, f32[136,256]{1,0:T(8,128)S(1)}, u32[]{:S(2)}, u32[]{:S(2)}) %collective-permute-start.3) | collective-permute-done | bytes 139296 | tf_op jit(solution)/shard_map/ppermute | solution.py:66
  20.5 0.8 %collective-permute-start.5 = (f32[136,256]{1,0:T(8,128)S(1)}, f32[136,256]{1,0:T(8,128)S(1)}, u32[]{:S(2)}, u32[]{:S(2)}) collective-permute-start(f32[136,256]{1,0:T(8,128)S(1)} %collective-permute-done.3.refs_4_), channel_id=1, source_target_pairs={{0,1},{2,0},{4,2},{6,4},{7,6},{5,7},{3,5},{1,3},{8,9},{10,8},{12,1... | collective-permute-start | bytes 417800 | tf_op jit(solution)/shard_map/ppermute | solution.py:66
  22.1 1.9 %collective-permute-start.6 = (f32[136,256]{1,0:T(8,128)S(1)}, f32[136,256]{1,0:T(8,128)S(1)}, u32[]{:S(2)}, u32[]{:S(2)}) collective-permute-start(f32[136,256]{1,0:T(8,128)S(1)} %collective-permute-done.4.refs_5_), channel_id=1, source_target_pairs={{0,2},{2,4},{4,6},{6,7},{7,5},{5,3},{3,1},{1,0},{8,10},{10,12},{12... | collective-permute-start | bytes 417800 | tf_op jit(solution)/shard_map/ppermute | solution.py:66
  24.0 1.6 %collective-permute-start.13 = (f32[256,256]{1,0:T(8,128)S(1)}, f32[256,256]{1,0:T(8,128)S(1)}, u32[]{:S(2)}, u32[]{:S(2)}) collective-permute-start(f32[256,256]{1,0:T(8,128)S(1)} %collective-permute-done.11), channel_id=1, source_target_pairs={{0,2},{2,4},{4,6},{6,7},{7,5},{5,3},{3,1},{1,0},{8,9},{10,8},{12,1... | collective-permute-start | bytes 786440 | tf_op jit(solution)/shard_map/ppermute | solution.py:66
  25.6 1.2 %collective-permute-done.5.refs_6_ = f32[136,256]{1,0:T(8,128)S(1)} collective-permute-done((f32[136,256]{1,0:T(8,128)S(1)}, f32[136,256]{1,0:T(8,128)S(1)}, u32[]{:S(2)}, u32[]{:S(2)}) %collective-permute-start.5) | collective-permute-done | bytes 139296 | tf_op jit(solution)/shard_map/ppermute | solution.py:66
  26.8 1.5 %collective-permute-done.6.refs_7_ = f32[136,256]{1,0:T(8,128)S(1)} collective-permute-done((f32[136,256]{1,0:T(8,128)S(1)}, f32[136,256]{1,0:T(8,128)S(1)}, u32[]{:S(2)}, u32[]{:S(2)}) %collective-permute-start.6) | collective-permute-done | bytes 139296 | tf_op jit(solution)/shard_map/ppermute | solution.py:66
  31.2 1.6 %collective-permute-start.16 = (f32[256,128]{1,0:T(8,128)S(1)}, f32[256,128]{1,0:T(8,128)S(1)}, u32[]{:S(2)}, u32[]{:S(2)}) collective-permute-start(f32[256,128]{1,0:T(8,128)S(1)} %get-tuple-element.32.mine_ref), channel_id=1, source_target_pairs={{0,16},{8,24},{16,0},{24,8},{1,17},{9,25},{17,1},{25,9},{2,18},{10... | collective-permute-start | bytes 393224 | tf_op jit(solution)/shard_map/ppermute | solution.py:47
  34.3 2.5 %collective-permute-done.16.got_ref = f32[256,128]{1,0:T(8,128)S(1)} collective-permute-done((f32[256,128]{1,0:T(8,128)S(1)}, f32[256,128]{1,0:T(8,128)S(1)}, u32[]{:S(2)}, u32[]{:S(2)}) %collective-permute-start.16) | collective-permute-done | bytes 131104 | tf_op jit(solution)/shard_map/ppermute | solution.py:47
  36.8 1.0 %collective-permute-done.15.refs_7_ = f32[128,256]{1,0:T(8,128)S(1)} collective-permute-done((f32[128,256]{1,0:T(8,128)S(1)}, f32[128,256]{1,0:T(8,128)S(1)}, u32[]{:S(2)}, u32[]{:S(2)}) %collective-permute-start.15) | collective-permute-done | bytes 131104 | tf_op jit(solution)/shard_map/ppermute | solution.py:66
  38.5 0.9 %collective-permute-done.17.got_ref = f32[256,128]{1,0:T(8,128)S(1)} collective-permute-done((f32[256,128]{1,0:T(8,128)S(1)}, f32[256,128]{1,0:T(8,128)S(1)}, u32[]{:S(2)}, u32[]{:S(2)}) %collective-permute-start.17) | collective-permute-done | bytes 131104 | tf_op jit(solution)/shard_map/ppermute | solution.py:47
  39.4 1.4 %shard_map.52 = (f32[256,128]{1,0:T(8,128)S(1)}, f32[256,128]{1,0:T(8,128)S(1)}) custom-call(bf16[1024,256]{1,0:T(8,128)(2,1)S(1)} %get-tuple-element.30.high_ref, bf16[1024,256]{1,0:T(8,128)(2,1)S(1)} %get-tuple-element.31.low_ref, f32[256,128]{1,0:T(8,128)S(1)} %shard_map.51.mine_ref, f32[256,128]{1,0:T(8,128)S(1)} %collective-permute-done.17.got_ref), custom_call_target="tpu_custom_call" | custom-call | tf_op jit(solution)/shard_map/pallas_call | solution.py:289
  41.0 1.2 %collective-permute-done.18.got_ref = f32[256,128]{1,0:T(8,128)S(1)} collective-permute-done((f32[256,128]{1,0:T(8,128)S(1)}, f32[256,128]{1,0:T(8,128)S(1)}, u32[]{:S(2)}, u32[]{:S(2)}) %collective-permute-start.18) | collective-permute-done | bytes 131104 | tf_op jit(solution)/shard_map/ppermute | solution.py:47
  42.9 5.0 %collective-permute-done.19.refs_12_ = f32[256,128]{1,0:T(8,128)S(1)} collective-permute-done((f32[256,128]{1,0:T(8,128)S(1)}, f32[256,128]{1,0:T(8,128)S(1)}, u32[]{:S(2)}, u32[]{:S(2)}) %collective-permute-start.19) | collective-permute-done | bytes 131104 | tf_op jit(solution)/shard_map/ppermute | solution.py:47
  48.8 1.3 %collective-permute-done.20.refs_10_ = f32[256,128]{1,0:T(8,128)S(1)} collective-permute-done((f32[256,128]{1,0:T(8,128)S(1)}, f32[256,128]{1,0:T(8,128)S(1)}, u32[]{:S(2)}, u32[]{:S(2)}) %collective-permute-start.20) | collective-permute-done | bytes 131104 | tf_op jit(solution)/shard_map/ppermute | solution.py:47
  50.1 1.1 %shard_map.55 = f32[3,32,64]{2,1,0:T(8,128)} custom-call(f32[136,256]{1,0:T(8,128)S(1)} %copy-done, f32[136,256]{1,0:T(8,128)S(1)} %collective-permute-done.refs_1_, f32[136,256]{1,0:T(8,128)S(1)} %collective-permute-done.1.refs_2_, f32[136,256]{1,0:T(8,128)S(1)} %collective-permute-done.2.refs_3_, f32[136,256]{1,0:T(8,128)S(1)} %collective-permute-done.3.refs_4_, ...), custom_call_target="tpu_custom_call" | custom-call | tf_op jit(solution)/shard_map/pallas_call | solution.py:289
  (36 shorter events, 9.3 us)
Async XLA Ops:
  1.9 3.2 %collective-permute-start.8 = (f32[128,256]{1,0:T(8,128)}, f32[128,256]{1,0:T(8,128)S(1)}, u32[]{:S(2)}, u32[]{:S(2)}) collective-permute-start(f32[128,256]{1,0:T(8,128)} %get-tuple-element.29.refs_0_), channel_id=1, source_target_pairs={{0,8},{8,0},{16,24},{24,16},{1,9},{9,1},{17,25},{25,17},{2,10},{10... | collective-permute-start | bytes 393224 | tf_op jit(solution)/shard_map/ppermute | solution.py:47
  2.4 5.2 %copy-start = (f32[136,256]{1,0:T(8,128)S(1)}, f32[136,256]{1,0:T(8,128)}, u32[]{:S(2)}) copy-start(f32[136,256]{1,0:T(8,128)} %get-tuple-element.23.refs_0_) | copy-start | bytes 417796
  2.5 7.1 %collective-permute-start = (f32[136,256]{1,0:T(8,128)}, f32[136,256]{1,0:T(8,128)S(1)}, u32[]{:S(2)}, u32[]{:S(2)}) collective-permute-start(f32[136,256]{1,0:T(8,128)} %get-tuple-element.23.refs_0_), channel_id=1, source_target_pairs={{0,2},{2,4},{4,6},{6,7},{7,5},{5,3},{3,1},{1,0},{8,10},{10,12},{12... | collective-permute-start | bytes 417800 | tf_op jit(solution)/shard_map/ppermute | solution.py:66
  6.0 6.7 %collective-permute-start.9 = (f32[256,256]{1,0:T(8,128)S(1)}, f32[256,256]{1,0:T(8,128)S(1)}, u32[]{:S(2)}, u32[]{:S(2)}) collective-permute-start(f32[256,256]{1,0:T(8,128)S(1)} %pad_maximum_fusion), channel_id=1, source_target_pairs={{0,2},{2,4},{4,6},{6,7},{7,5},{5,3},{3,1},{1,0},{8,9},{10,8},{12,1... | collective-permute-start | bytes 786440 | tf_op jit(solution)/shard_map/ppermute | solution.py:66
  7.7 7.0 %collective-permute-start.1 = (f32[136,256]{1,0:T(8,128)S(1)}, f32[136,256]{1,0:T(8,128)S(1)}, u32[]{:S(2)}, u32[]{:S(2)}) collective-permute-start(f32[136,256]{1,0:T(8,128)S(1)} %copy-done), channel_id=1, source_target_pairs={{0,1},{2,0},{4,2},{6,4},{7,6},{5,7},{3,5},{1,3},{8,9},{10,8},{12,1... | collective-permute-start | bytes 417800 | tf_op jit(solution)/shard_map/ppermute | solution.py:66
  9.6 5.8 %collective-permute-start.2 = (f32[136,256]{1,0:T(8,128)S(1)}, f32[136,256]{1,0:T(8,128)S(1)}, u32[]{:S(2)}, u32[]{:S(2)}) collective-permute-start(f32[136,256]{1,0:T(8,128)S(1)} %collective-permute-done.refs_1_), channel_id=1, source_target_pairs={{0,2},{2,4},{4,6},{6,7},{7,5},{5,3},{3,1},{1,0},{8,10},{10,12},{12... | collective-permute-start | bytes 417800 | tf_op jit(solution)/shard_map/ppermute | solution.py:66
  12.7 11.3 %collective-permute-start.11 = (f32[256,256]{1,0:T(8,128)S(1)}, f32[256,256]{1,0:T(8,128)S(1)}, u32[]{:S(2)}, u32[]{:S(2)}) collective-permute-start(f32[256,256]{1,0:T(8,128)S(1)} %collective-permute-done.9), channel_id=1, source_target_pairs={{0,2},{2,4},{4,6},{6,7},{7,5},{5,3},{3,1},{1,0},{8,9},{10,8},{12,1... | collective-permute-start | bytes 786440 | tf_op jit(solution)/shard_map/ppermute | solution.py:66
  14.6 5.8 %collective-permute-start.3 = (f32[136,256]{1,0:T(8,128)S(1)}, f32[136,256]{1,0:T(8,128)S(1)}, u32[]{:S(2)}, u32[]{:S(2)}) collective-permute-start(f32[136,256]{1,0:T(8,128)S(1)} %collective-permute-done.1.refs_2_), channel_id=1, source_target_pairs={{0,1},{2,0},{4,2},{6,4},{7,6},{5,7},{3,5},{1,3},{8,9},{10,8},{12,1... | collective-permute-start | bytes 417800 | tf_op jit(solution)/shard_map/ppermute | solution.py:66
  15.4 6.6 %collective-permute-start.4 = (f32[136,256]{1,0:T(8,128)S(1)}, f32[136,256]{1,0:T(8,128)S(1)}, u32[]{:S(2)}, u32[]{:S(2)}) collective-permute-start(f32[136,256]{1,0:T(8,128)S(1)} %collective-permute-done.2.refs_3_), channel_id=1, source_target_pairs={{0,2},{2,4},{4,6},{6,7},{7,5},{5,3},{3,1},{1,0},{8,10},{10,12},{12... | collective-permute-start | bytes 417800 | tf_op jit(solution)/shard_map/ppermute | solution.py:66
  20.5 6.3 %collective-permute-start.5 = (f32[136,256]{1,0:T(8,128)S(1)}, f32[136,256]{1,0:T(8,128)S(1)}, u32[]{:S(2)}, u32[]{:S(2)}) collective-permute-start(f32[136,256]{1,0:T(8,128)S(1)} %collective-permute-done.3.refs_4_), channel_id=1, source_target_pairs={{0,1},{2,0},{4,2},{6,4},{7,6},{5,7},{3,5},{1,3},{8,9},{10,8},{12,1... | collective-permute-start | bytes 417800 | tf_op jit(solution)/shard_map/ppermute | solution.py:66
  22.1 6.2 %collective-permute-start.6 = (f32[136,256]{1,0:T(8,128)S(1)}, f32[136,256]{1,0:T(8,128)S(1)}, u32[]{:S(2)}, u32[]{:S(2)}) collective-permute-start(f32[136,256]{1,0:T(8,128)S(1)} %collective-permute-done.4.refs_5_), channel_id=1, source_target_pairs={{0,2},{2,4},{4,6},{6,7},{7,5},{5,3},{3,1},{1,0},{8,10},{10,12},{12... | collective-permute-start | bytes 417800 | tf_op jit(solution)/shard_map/ppermute | solution.py:66
  24.0 8.8 %collective-permute-start.13 = (f32[256,256]{1,0:T(8,128)S(1)}, f32[256,256]{1,0:T(8,128)S(1)}, u32[]{:S(2)}, u32[]{:S(2)}) collective-permute-start(f32[256,256]{1,0:T(8,128)S(1)} %collective-permute-done.11), channel_id=1, source_target_pairs={{0,2},{2,4},{4,6},{6,7},{7,5},{5,3},{3,1},{1,0},{8,9},{10,8},{12,1... | collective-permute-start | bytes 786440 | tf_op jit(solution)/shard_map/ppermute | solution.py:66
  29.0 1.4 %collective-permute-start.7 = (f32[256,128]{1,0:T(8,128)S(1)}, f32[256,128]{1,0:T(8,128)S(1)}, u32[]{:S(2)}, u32[]{:S(2)}) collective-permute-start(f32[256,128]{1,0:T(8,128)S(1)} %get-tuple-element.27.refs_10_), channel_id=1, source_target_pairs={{0,8},{8,0},{16,24},{24,16},{1,9},{9,1},{17,25},{25,17},{2,10},{10... | collective-permute-start | bytes 393224 | tf_op jit(solution)/shard_map/ppermute | solution.py:47
  29.1 8.9 %collective-permute-start.10 = (f32[128,256]{1,0:T(8,128)S(1)}, f32[128,256]{1,0:T(8,128)S(1)}, u32[]{:S(2)}, u32[]{:S(2)}) collective-permute-start(f32[128,256]{1,0:T(8,128)S(1)} %get-tuple-element.45), channel_id=1, source_target_pairs={{0,8},{8,0},{16,24},{24,16},{1,9},{9,1},{17,25},{25,17},{2,10},{10... | collective-permute-start | bytes 393224 | tf_op jit(solution)/shard_map/ppermute | solution.py:47
  31.2 5.6 %collective-permute-start.16 = (f32[256,128]{1,0:T(8,128)S(1)}, f32[256,128]{1,0:T(8,128)S(1)}, u32[]{:S(2)}, u32[]{:S(2)}) collective-permute-start(f32[256,128]{1,0:T(8,128)S(1)} %get-tuple-element.32.mine_ref), channel_id=1, source_target_pairs={{0,16},{8,24},{16,0},{24,8},{1,17},{9,25},{17,1},{25,9},{2,18},{10... | collective-permute-start | bytes 393224 | tf_op jit(solution)/shard_map/ppermute | solution.py:47
  32.8 5.0 %collective-permute-start.15 = (f32[128,256]{1,0:T(8,128)S(1)}, f32[128,256]{1,0:T(8,128)S(1)}, u32[]{:S(2)}, u32[]{:S(2)}) collective-permute-start(f32[128,256]{1,0:T(8,128)S(1)} %get-tuple-element.42.refs_5_), channel_id=1, source_target_pairs={{0,2},{2,4},{4,6},{6,7},{7,5},{5,3},{3,1},{1,0},{8,9},{10,8},{12,1... | collective-permute-start | bytes 393224 | tf_op jit(solution)/shard_map/ppermute | solution.py:66
  33.6 4.5 %collective-permute-start.12 = (f32[128,256]{1,0:T(8,128)S(1)}, f32[128,256]{1,0:T(8,128)S(1)}, u32[]{:S(2)}, u32[]{:S(2)}) collective-permute-start(f32[128,256]{1,0:T(8,128)S(1)} %get-tuple-element.43), channel_id=1, source_target_pairs={{0,8},{8,0},{16,24},{24,16},{1,9},{9,1},{17,25},{25,17},{2,10},{10... | collective-permute-start | bytes 393224 | tf_op jit(solution)/shard_map/ppermute | solution.py:47
  34.3 3.9 %copy-start.1 = (f32[128,256]{1,0:T(8,128)S(1)}, f32[128,256]{1,0:T(8,128)}, u32[]{:S(2)}) copy-start(f32[128,256]{1,0:T(8,128)} %get-tuple-element.29.refs_0_) | copy-start | bytes 393220
  34.3 3.8 %collective-permute-start.14 = (f32[128,256]{1,0:T(8,128)S(1)}, f32[128,256]{1,0:T(8,128)S(1)}, u32[]{:S(2)}, u32[]{:S(2)}) collective-permute-start(f32[128,256]{1,0:T(8,128)S(1)} %get-tuple-element.41), channel_id=1, source_target_pairs={{0,8},{8,0},{16,24},{24,16},{1,9},{9,1},{17,25},{25,17},{2,10},{10... | collective-permute-start | bytes 393224 | tf_op jit(solution)/shard_map/ppermute | solution.py:47
  38.0 1.4 %collective-permute-start.17 = (f32[256,128]{1,0:T(8,128)S(1)}, f32[256,128]{1,0:T(8,128)S(1)}, u32[]{:S(2)}, u32[]{:S(2)}) collective-permute-start(f32[256,128]{1,0:T(8,128)S(1)} %shard_map.51.mine_ref), channel_id=1, source_target_pairs={{0,8},{8,0},{16,24},{24,16},{1,9},{9,1},{17,25},{25,17},{2,10},{10... | collective-permute-start | bytes 393224 | tf_op jit(solution)/shard_map/ppermute | solution.py:47
  40.8 1.4 %collective-permute-start.18 = (f32[256,128]{1,0:T(8,128)S(1)}, f32[256,128]{1,0:T(8,128)S(1)}, u32[]{:S(2)}, u32[]{:S(2)}) collective-permute-start(f32[256,128]{1,0:T(8,128)S(1)} %get-tuple-element.35), channel_id=1, source_target_pairs={{0,8},{8,0},{16,24},{24,16},{1,9},{9,1},{17,25},{25,17},{2,10},{10... | collective-permute-start | bytes 393224 | tf_op jit(solution)/shard_map/ppermute | solution.py:47
  42.3 5.6 %collective-permute-start.19 = (f32[256,128]{1,0:T(8,128)S(1)}, f32[256,128]{1,0:T(8,128)S(1)}, u32[]{:S(2)}, u32[]{:S(2)}) collective-permute-start(f32[256,128]{1,0:T(8,128)S(1)} %get-tuple-element.37), channel_id=1, source_target_pairs={{0,16},{8,24},{16,0},{24,8},{1,17},{9,25},{17,1},{25,9},{2,18},{10... | collective-permute-start | bytes 393224 | tf_op jit(solution)/shard_map/ppermute | solution.py:47
  48.7 1.4 %collective-permute-start.20 = (f32[256,128]{1,0:T(8,128)S(1)}, f32[256,128]{1,0:T(8,128)S(1)}, u32[]{:S(2)}, u32[]{:S(2)}) collective-permute-start(f32[256,128]{1,0:T(8,128)S(1)} %get-tuple-element.39), channel_id=1, source_target_pairs={{0,8},{8,0},{16,24},{24,16},{1,9},{9,1},{17,25},{25,17},{2,10},{10... | collective-permute-start | bytes 393224 | tf_op jit(solution)/shard_map/ppermute | solution.py:47

commit v7 on v6

--- a/solution.py
+++ b/solution.py
@@ -70,27 +70,24 @@
     return [0] + [x for r in range(1, count // 2) for x in (r, -r)] + [count // 2]
 
 
-def gather_rows(block, AFTER={}):
+def gather_rows(block):
     height = block.shape[0]
-    moving = jnp.concatenate([block, swap(block, "cube", 1)], axis=0)
-    out = [block]
-    for r in range(1, lax.axis_size("blk") // 2):
-        if r in AFTER:
-            moving = tie(moving, AFTER[r])
+    even = lax.axis_index("cube") % 2 == 0
+    up, down = ring_step(block, 1, 1), ring_step(block, -1, -1)
+    out = [block, up, down]
+    handed = swap(jnp.where(even, down, up), "cube", 1)
+    moving = jnp.concatenate([jnp.where(even, up, down), handed], axis=0)
+    for _ in range(2, lax.axis_size("blk") // 2):
         moving = ring_step(moving, 1, -1)
         out += [moving[:height], swap(moving[height:], "cube", 1)]
-    if 4 in AFTER:
-        moving = tie(moving, AFTER[4])
     return out + [ring_step(moving[:height], 1, -1)]
 
 
-def gather_both_ways(block, JOINT=()):
+def gather_both_ways(block):
     out = [block]
     up = down = block
-    for r in range(1, lax.axis_size("blk") // 2):
+    for _ in range(1, lax.axis_size("blk") // 2):
         up, down = ring_step(up, 1, 1), ring_step(down, -1, -1)
-        if r in JOINT:
-            up, down = lax.optimization_barrier((up, down))
         out += [up, down]
     return out + [ring_step(up, 1, 1)]
 
@@ -177,7 +174,8 @@
 
 
 def shared_block_of(pk, m, p=0):
-    return block_of(pk, m, p, 1 - 2 * (lax.axis_index("cube") % 2))
+    shared = 3 <= m < pk.n_blk - 1
+    return block_of(pk, m, p, 1 - 2 * (lax.axis_index("cube") % 2) if shared else 1)
 
 
 def extend_out(pk, level, pieces, y_ref, send_ref):
@@ -296,10 +294,6 @@
     )(*args)
 
 
-def tie(value, other):
-    return lax.optimization_barrier((value, other))[0]
-
-
 def gathered(pk, right_side, diag_inverse, panels, extend_map):
     rows, cols, node = pk.rows, pk.cols, pk.width
     one, two = (node, cols), (node, 2 * cols)
@@ -329,13 +323,13 @@
         pltpu.HBM,
         room=60,
     )
-    first = gather_both_ways(packed, ())
-    last = gather_rows(top, {})
+    first = gather_both_ways(packed)
+    last = gather_rows(top)
     send, y0 = call(first_kernel, pk, first, [two, one], work((node, node), one))
     got = swap(send, "cube", 1)
     diag1 = split_diag(first, 1, block_of, None)
     send, y1 = call(middle_kernel, pk, [*first, *diag1, send, got], [two, one])
-    got = tie(swap(send, "cube", 2), last[7])
+    got = swap(send, "cube", 2)
     (held,) = call(meet_kernel, pk, [send, got], [two])
     got = swap(held, "cube", 1)
     diag2 = split_diag(last, 2, shared_block_of, 0)

time: 51.4 us -> 50.7 us (0.986)
  starting transfers between devices: 19.7 us -> 21.6 us
  waiting for transfers between devices: 22.9 us -> 21.2 us
  other arithmetic: 0.92 us -> 0.04 us
    ppermute x11 -> x12, starting transfers between devices: 15.3 us -> 17.4 us  [ring_step(): return lax.ppermute(block, ('cube', 'blk'), route)]
    ppermute x10 -> x9, waiting for transfers between devices: 11.5 us -> 9.62 us  [swap(): return lax.ppermute(block, axis, [(i, i ^ mask) for i in range(count)])]
    concatenate x1, other arithmetic: 0.92 us -> 0.02 us  [gather_rows(): moving = jnp.concatenate([jnp.where(even, up, down), handed], axis=0)]
    ppermute x11 -> x12, waiting for transfers between devices: 11.4 us -> 11.5 us  [ring_step(): return lax.ppermute(block, ('cube', 'blk'), route)]
    ppermute x10 -> x9, starting transfers between devices: 4.38 us -> 4.26 us  [swap(): return lax.ppermute(block, axis, [(i, i ^ mask) for i in range(count)])]
  transfers between devices with their start and end apart: 21 -> 21, of which waited for: 14 -> 12; matrix products, arithmetic and copies ran while one was open for 2% -> 0% of each run, Pallas kernels for 4% -> 4%
where the time goes in v7:
time: 50.7 us; the launch traced here: 50.6 us
  starting transfers between devices  21.6 us (43%)
  waiting for transfers between devices  21.2 us (42%)
  Pallas kernels  7.54 us (15%)
    ppermute x12, starting transfers between devices, ring_step(): return lax.ppermute(block, ('cube', 'blk'), route)  17.4 us
    ppermute x12, waiting for transfers between devices, ring_step(): return lax.ppermute(block, ('cube', 'blk'), route)  11.5 us
    ppermute x9, waiting for transfers between devices, swap(): return lax.ppermute(block, axis, [(i, i ^ mask) for i in range(count)])  9.62 us
    pallas_call x10, Pallas kernels, call(): pl.pallas_call(functools.partial(kernel, pk), out_shape=[jax.ShapeDtypeSt...  7.54 us
    ppermute x9, starting transfers between devices, swap(): return lax.ppermute(block, axis, [(i, i ^ mask) for i in range(count)])  4.26 us
  transfers between devices with their start and end apart: 21, of which 12 were waited for; matrix products, arithmetic and copies ran while one was open for 0% of the time, Pallas kernels for 4%

profile of v7, /device:TPU:0, one launch (start us, length us, event | category | flops | bytes accessed | tf_op | source)
XLA Modules:
  0.0 50.6 jit_solution(250338769923878041)
XLA Ops:
  0.0 1.9 %shard_map.46 = (f32[136,256]{1,0:T(8,128)}, f32[128,256]{1,0:T(8,128)}) custom-call(f32[3,1,1,32,64]{4,3,2,1,0:T(8,128)} %rhs_hbm.1, f32[2,1,1,2,16,32]{5,4,3,2,1,0:T(8,128)} %panels_hbm.1, s32[2,1,1,2,16]{4,3,2,1,0:T(2,128)} %maps_hbm.1, f32[224,256]{1,0:T(8,128)} %diag_hbm.1), custom_call_target="tpu_custom_call" | custom-call | tf_op jit(solution)/shard_map/pallas_call | solution.py:287
  1.9 3.1 %collective-permute-start.8 = (f32[128,256]{1,0:T(8,128)}, f32[128,256]{1,0:T(8,128)S(1)}, u32[]{:S(2)}, u32[]{:S(2)}) collective-permute-start(f32[128,256]{1,0:T(8,128)} %get-tuple-element.28.refs_0_), channel_id=1, source_target_pairs={{0,2},{2,4},{4,6},{6,7},{7,5},{5,3},{3,1},{1,0},{8,10},{10,12},{12... | collective-permute-start | bytes 393224 | tf_op jit(solution)/shard_map/ppermute | solution.py:66
  5.0 2.0 %collective-permute-start = (f32[136,256]{1,0:T(8,128)}, f32[136,256]{1,0:T(8,128)S(1)}, u32[]{:S(2)}, u32[]{:S(2)}) collective-permute-start(f32[136,256]{1,0:T(8,128)} %get-tuple-element.22.refs_0_), channel_id=1, source_target_pairs={{0,2},{2,4},{4,6},{6,7},{7,5},{5,3},{3,1},{1,0},{8,10},{10,12},{12... | collective-permute-start | bytes 417800 | tf_op jit(solution)/shard_map/ppermute | solution.py:66
  7.0 2.4 %collective-permute-done.8.refs_1_ = f32[128,256]{1,0:T(8,128)S(1)} collective-permute-done((f32[128,256]{1,0:T(8,128)}, f32[128,256]{1,0:T(8,128)S(1)}, u32[]{:S(2)}, u32[]{:S(2)}) %collective-permute-start.8) | collective-permute-done | bytes 131104 | tf_op jit(solution)/shard_map/ppermute | solution.py:66
  10.3 1.4 %collective-permute-start.1 = (f32[136,256]{1,0:T(8,128)S(1)}, f32[136,256]{1,0:T(8,128)S(1)}, u32[]{:S(2)}, u32[]{:S(2)}) collective-permute-start(f32[136,256]{1,0:T(8,128)S(1)} %copy-done), channel_id=1, source_target_pairs={{0,1},{2,0},{4,2},{6,4},{7,6},{5,7},{3,5},{1,3},{8,9},{10,8},{12,1... | collective-permute-start | bytes 417800 | tf_op jit(solution)/shard_map/ppermute | solution.py:66
  11.7 1.7 %collective-permute-start.2 = (f32[136,256]{1,0:T(8,128)S(1)}, f32[136,256]{1,0:T(8,128)S(1)}, u32[]{:S(2)}, u32[]{:S(2)}) collective-permute-start(f32[136,256]{1,0:T(8,128)S(1)} %collective-permute-done.refs_1_), channel_id=1, source_target_pairs={{0,2},{2,4},{4,6},{6,7},{7,5},{5,3},{3,1},{1,0},{8,10},{10,12},{12... | collective-permute-start | bytes 417800 | tf_op jit(solution)/shard_map/ppermute | solution.py:66
  13.5 1.6 %collective-permute-start.11 = (f32[256,256]{1,0:T(8,128)S(1)}, f32[256,256]{1,0:T(8,128)S(1)}, u32[]{:S(2)}, u32[]{:S(2)}) collective-permute-start(f32[256,256]{1,0:T(8,128)S(1)} %pad_maximum_fusion), channel_id=1, source_target_pairs={{0,2},{2,4},{4,6},{6,7},{7,5},{5,3},{3,1},{1,0},{8,9},{10,8},{12,1... | collective-permute-start | bytes 786440 | tf_op jit(solution)/shard_map/ppermute | solution.py:66
  15.1 1.7 %collective-permute-done.1.refs_2_ = f32[136,256]{1,0:T(8,128)S(1)} collective-permute-done((f32[136,256]{1,0:T(8,128)S(1)}, f32[136,256]{1,0:T(8,128)S(1)}, u32[]{:S(2)}, u32[]{:S(2)}) %collective-permute-start.1) | collective-permute-done | bytes 139296 | tf_op jit(solution)/shard_map/ppermute | solution.py:66
  16.8 1.4 %collective-permute-start.3 = (f32[136,256]{1,0:T(8,128)S(1)}, f32[136,256]{1,0:T(8,128)S(1)}, u32[]{:S(2)}, u32[]{:S(2)}) collective-permute-start(f32[136,256]{1,0:T(8,128)S(1)} %collective-permute-done.1.refs_2_), channel_id=1, source_target_pairs={{0,1},{2,0},{4,2},{6,4},{7,6},{5,7},{3,5},{1,3},{8,9},{10,8},{12,1... | collective-permute-start | bytes 417800 | tf_op jit(solution)/shard_map/ppermute | solution.py:66
  18.9 3.3 %collective-permute-done.3.refs_4_ = f32[136,256]{1,0:T(8,128)S(1)} collective-permute-done((f32[136,256]{1,0:T(8,128)S(1)}, f32[136,256]{1,0:T(8,128)S(1)}, u32[]{:S(2)}, u32[]{:S(2)}) %collective-permute-start.3) | collective-permute-done | bytes 139296 | tf_op jit(solution)/shard_map/ppermute | solution.py:66
  22.2 1.4 %collective-permute-start.5 = (f32[136,256]{1,0:T(8,128)S(1)}, f32[136,256]{1,0:T(8,128)S(1)}, u32[]{:S(2)}, u32[]{:S(2)}) collective-permute-start(f32[136,256]{1,0:T(8,128)S(1)} %collective-permute-done.3.refs_4_), channel_id=1, source_target_pairs={{0,1},{2,0},{4,2},{6,4},{7,6},{5,7},{3,5},{1,3},{8,9},{10,8},{12,1... | collective-permute-start | bytes 417800 | tf_op jit(solution)/shard_map/ppermute | solution.py:66
  23.5 0.9 %collective-permute-start.6 = (f32[136,256]{1,0:T(8,128)S(1)}, f32[136,256]{1,0:T(8,128)S(1)}, u32[]{:S(2)}, u32[]{:S(2)}) collective-permute-start(f32[136,256]{1,0:T(8,128)S(1)} %collective-permute-done.4.refs_5_), channel_id=1, source_target_pairs={{0,2},{2,4},{4,6},{6,7},{7,5},{5,3},{3,1},{1,0},{8,10},{10,12},{12... | collective-permute-start | bytes 417800 | tf_op jit(solution)/shard_map/ppermute | solution.py:66
  24.5 1.6 %collective-permute-start.13 = (f32[256,256]{1,0:T(8,128)S(1)}, f32[256,256]{1,0:T(8,128)S(1)}, u32[]{:S(2)}, u32[]{:S(2)}) collective-permute-start(f32[256,256]{1,0:T(8,128)S(1)} %collective-permute-done.11), channel_id=1, source_target_pairs={{0,2},{2,4},{4,6},{6,7},{7,5},{5,3},{3,1},{1,0},{8,9},{10,8},{12,1... | collective-permute-start | bytes 786440 | tf_op jit(solution)/shard_map/ppermute | solution.py:66
  26.0 2.6 %collective-permute-done.5.refs_6_ = f32[136,256]{1,0:T(8,128)S(1)} collective-permute-done((f32[136,256]{1,0:T(8,128)S(1)}, f32[136,256]{1,0:T(8,128)S(1)}, u32[]{:S(2)}, u32[]{:S(2)}) %collective-permute-start.5) | collective-permute-done | bytes 139296 | tf_op jit(solution)/shard_map/ppermute | solution.py:66
  31.5 1.6 %collective-permute-start.16 = (f32[256,128]{1,0:T(8,128)S(1)}, f32[256,128]{1,0:T(8,128)S(1)}, u32[]{:S(2)}, u32[]{:S(2)}) collective-permute-start(f32[256,128]{1,0:T(8,128)S(1)} %get-tuple-element.31.mine_ref), channel_id=1, source_target_pairs={{0,16},{8,24},{16,0},{24,8},{1,17},{9,25},{17,1},{25,9},{2,18},{10... | collective-permute-start | bytes 393224 | tf_op jit(solution)/shard_map/ppermute | solution.py:47
  33.2 1.6 %collective-permute-start.15 = (f32[128,256]{1,0:T(8,128)S(1)}, f32[128,256]{1,0:T(8,128)S(1)}, u32[]{:S(2)}, u32[]{:S(2)}) collective-permute-start(f32[128,256]{1,0:T(8,128)S(1)} %get-tuple-element.40.refs_5_), channel_id=1, source_target_pairs={{0,2},{2,4},{4,6},{6,7},{7,5},{5,3},{3,1},{1,0},{8,9},{10,8},{12,1... | collective-permute-start | bytes 393224 | tf_op jit(solution)/shard_map/ppermute | solution.py:66
  34.8 2.3 %collective-permute-done.16.got_ref = f32[256,128]{1,0:T(8,128)S(1)} collective-permute-done((f32[256,128]{1,0:T(8,128)S(1)}, f32[256,128]{1,0:T(8,128)S(1)}, u32[]{:S(2)}, u32[]{:S(2)}) %collective-permute-start.16) | collective-permute-done | bytes 131104 | tf_op jit(solution)/shard_map/ppermute | solution.py:47
  37.4 0.8 %collective-permute-done.15.refs_7_ = f32[128,256]{1,0:T(8,128)S(1)} collective-permute-done((f32[128,256]{1,0:T(8,128)S(1)}, f32[128,256]{1,0:T(8,128)S(1)}, u32[]{:S(2)}, u32[]{:S(2)}) %collective-permute-start.15) | collective-permute-done | bytes 131104 | tf_op jit(solution)/shard_map/ppermute | solution.py:66
  38.7 1.4 %shard_map.52 = (f32[256,128]{1,0:T(8,128)S(1)}, f32[256,128]{1,0:T(8,128)S(1)}) custom-call(bf16[1024,256]{1,0:T(8,128)(2,1)S(1)} %get-tuple-element.29.high_ref, bf16[1024,256]{1,0:T(8,128)(2,1)S(1)} %get-tuple-element.30.low_ref, f32[256,128]{1,0:T(8,128)S(1)} %shard_map.51.mine_ref, f32[256,128]{1,0:T(8,128)S(1)} %collective-permute-done.17.got_ref), custom_call_target="tpu_custom_call" | custom-call | tf_op jit(solution)/shard_map/pallas_call | solution.py:287
  40.4 1.2 %collective-permute-done.18.got_ref = f32[256,128]{1,0:T(8,128)S(1)} collective-permute-done((f32[256,128]{1,0:T(8,128)S(1)}, f32[256,128]{1,0:T(8,128)S(1)}, u32[]{:S(2)}, u32[]{:S(2)}) %collective-permute-start.18) | collective-permute-done | bytes 131104 | tf_op jit(solution)/shard_map/ppermute | solution.py:47
  41.7 1.6 %collective-permute-start.19 = (f32[256,128]{1,0:T(8,128)S(1)}, f32[256,128]{1,0:T(8,128)S(1)}, u32[]{:S(2)}, u32[]{:S(2)}) collective-permute-start(f32[256,128]{1,0:T(8,128)S(1)} %get-tuple-element.35), channel_id=1, source_target_pairs={{0,16},{8,24},{16,0},{24,8},{1,17},{9,25},{17,1},{25,9},{2,18},{10... | collective-permute-start | bytes 393224 | tf_op jit(solution)/shard_map/ppermute | solution.py:47
  43.2 4.0 %collective-permute-done.19.refs_12_ = f32[256,128]{1,0:T(8,128)S(1)} collective-permute-done((f32[256,128]{1,0:T(8,128)S(1)}, f32[256,128]{1,0:T(8,128)S(1)}, u32[]{:S(2)}, u32[]{:S(2)}) %collective-permute-start.19) | collective-permute-done | bytes 131104 | tf_op jit(solution)/shard_map/ppermute | solution.py:47
  48.1 1.3 %collective-permute-done.20.refs_10_ = f32[256,128]{1,0:T(8,128)S(1)} collective-permute-done((f32[256,128]{1,0:T(8,128)S(1)}, f32[256,128]{1,0:T(8,128)S(1)}, u32[]{:S(2)}, u32[]{:S(2)}) %collective-permute-start.20) | collective-permute-done | bytes 131104 | tf_op jit(solution)/shard_map/ppermute | solution.py:47
  49.5 1.1 %shard_map.55 = f32[3,32,64]{2,1,0:T(8,128)} custom-call(f32[136,256]{1,0:T(8,128)S(1)} %copy-done, f32[136,256]{1,0:T(8,128)S(1)} %collective-permute-done.refs_1_, f32[136,256]{1,0:T(8,128)S(1)} %collective-permute-done.1.refs_2_, f32[136,256]{1,0:T(8,128)S(1)} %collective-permute-done.2.refs_3_, f32[136,256]{1,0:T(8,128)S(1)} %collective-permute-done.3.refs_4_, ...), custom_call_target="tpu_custom_call" | custom-call | tf_op jit(solution)/shard_map/pallas_call | solution.py:287
  (36 shorter events, 6.4 us)
Async XLA Ops:
  1.9 7.6 %collective-permute-start.8 = (f32[128,256]{1,0:T(8,128)}, f32[128,256]{1,0:T(8,128)S(1)}, u32[]{:S(2)}, u32[]{:S(2)}) collective-permute-start(f32[128,256]{1,0:T(8,128)} %get-tuple-element.28.refs_0_), channel_id=1, source_target_pairs={{0,2},{2,4},{4,6},{6,7},{7,5},{5,3},{3,1},{1,0},{8,10},{10,12},{12... | collective-permute-start | bytes 393224 | tf_op jit(solution)/shard_map/ppermute | solution.py:66
  5.0 5.2 %collective-permute-start.9 = (f32[128,256]{1,0:T(8,128)}, f32[128,256]{1,0:T(8,128)S(1)}, u32[]{:S(2)}, u32[]{:S(2)}) collective-permute-start(f32[128,256]{1,0:T(8,128)} %get-tuple-element.28.refs_0_), channel_id=1, source_target_pairs={{0,1},{2,0},{4,2},{6,4},{7,6},{5,7},{3,5},{1,3},{8,9},{10,8},{12,1... | collective-permute-start | bytes 393224 | tf_op jit(solution)/shard_map/ppermute | solution.py:66
  5.0 6.7 %collective-permute-start = (f32[136,256]{1,0:T(8,128)}, f32[136,256]{1,0:T(8,128)S(1)}, u32[]{:S(2)}, u32[]{:S(2)}) collective-permute-start(f32[136,256]{1,0:T(8,128)} %get-tuple-element.22.refs_0_), channel_id=1, source_target_pairs={{0,2},{2,4},{4,6},{6,7},{7,5},{5,3},{3,1},{1,0},{8,10},{10,12},{12... | collective-permute-start | bytes 417800 | tf_op jit(solution)/shard_map/ppermute | solution.py:66
  7.0 3.3 %copy-start = (f32[136,256]{1,0:T(8,128)S(1)}, f32[136,256]{1,0:T(8,128)}, u32[]{:S(2)}) copy-start(f32[136,256]{1,0:T(8,128)} %get-tuple-element.22.refs_0_) | copy-start | bytes 417796
  10.2 3.2 %collective-permute-start.10 = (f32[128,256]{1,0:T(8,128)S(1)}, f32[128,256]{1,0:T(8,128)S(1)}, u32[]{:S(2)}, u32[]{:S(2)}) collective-permute-start(f32[128,256]{1,0:T(8,128)S(1)} %get-tuple-element.44), channel_id=1, source_target_pairs={{0,8},{8,0},{16,24},{24,16},{1,9},{9,1},{17,25},{25,17},{2,10},{10... | collective-permute-start | bytes 393224 | tf_op jit(solution)/shard_map/ppermute | solution.py:47
  10.3 6.5 %collective-permute-start.1 = (f32[136,256]{1,0:T(8,128)S(1)}, f32[136,256]{1,0:T(8,128)S(1)}, u32[]{:S(2)}, u32[]{:S(2)}) collective-permute-start(f32[136,256]{1,0:T(8,128)S(1)} %copy-done), channel_id=1, source_target_pairs={{0,1},{2,0},{4,2},{6,4},{7,6},{5,7},{3,5},{1,3},{8,9},{10,8},{12,1... | collective-permute-start | bytes 417800 | tf_op jit(solution)/shard_map/ppermute | solution.py:66
  11.7 6.5 %collective-permute-start.2 = (f32[136,256]{1,0:T(8,128)S(1)}, f32[136,256]{1,0:T(8,128)S(1)}, u32[]{:S(2)}, u32[]{:S(2)}) collective-permute-start(f32[136,256]{1,0:T(8,128)S(1)} %collective-permute-done.refs_1_), channel_id=1, source_target_pairs={{0,2},{2,4},{4,6},{6,7},{7,5},{5,3},{3,1},{1,0},{8,10},{10,12},{12... | collective-permute-start | bytes 417800 | tf_op jit(solution)/shard_map/ppermute | solution.py:66
  13.5 11.0 %collective-permute-start.11 = (f32[256,256]{1,0:T(8,128)S(1)}, f32[256,256]{1,0:T(8,128)S(1)}, u32[]{:S(2)}, u32[]{:S(2)}) collective-permute-start(f32[256,256]{1,0:T(8,128)S(1)} %pad_maximum_fusion), channel_id=1, source_target_pairs={{0,2},{2,4},{4,6},{6,7},{7,5},{5,3},{3,1},{1,0},{8,9},{10,8},{12,1... | collective-permute-start | bytes 786440 | tf_op jit(solution)/shard_map/ppermute | solution.py:66
  16.8 5.3 %collective-permute-start.3 = (f32[136,256]{1,0:T(8,128)S(1)}, f32[136,256]{1,0:T(8,128)S(1)}, u32[]{:S(2)}, u32[]{:S(2)}) collective-permute-start(f32[136,256]{1,0:T(8,128)S(1)} %collective-permute-done.1.refs_2_), channel_id=1, source_target_pairs={{0,1},{2,0},{4,2},{6,4},{7,6},{5,7},{3,5},{1,3},{8,9},{10,8},{12,1... | collective-permute-start | bytes 417800 | tf_op jit(solution)/shard_map/ppermute | solution.py:66
  18.2 5.3 %collective-permute-start.4 = (f32[136,256]{1,0:T(8,128)S(1)}, f32[136,256]{1,0:T(8,128)S(1)}, u32[]{:S(2)}, u32[]{:S(2)}) collective-permute-start(f32[136,256]{1,0:T(8,128)S(1)} %collective-permute-done.2.refs_3_), channel_id=1, source_target_pairs={{0,2},{2,4},{4,6},{6,7},{7,5},{5,3},{3,1},{1,0},{8,10},{10,12},{12... | collective-permute-start | bytes 417800 | tf_op jit(solution)/shard_map/ppermute | solution.py:66
  22.2 6.4 %collective-permute-start.5 = (f32[136,256]{1,0:T(8,128)S(1)}, f32[136,256]{1,0:T(8,128)S(1)}, u32[]{:S(2)}, u32[]{:S(2)}) collective-permute-start(f32[136,256]{1,0:T(8,128)S(1)} %collective-permute-done.3.refs_4_), channel_id=1, source_target_pairs={{0,1},{2,0},{4,2},{6,4},{7,6},{5,7},{3,5},{1,3},{8,9},{10,8},{12,1... | collective-permute-start | bytes 417800 | tf_op jit(solution)/shard_map/ppermute | solution.py:66
  23.5 5.1 %collective-permute-start.6 = (f32[136,256]{1,0:T(8,128)S(1)}, f32[136,256]{1,0:T(8,128)S(1)}, u32[]{:S(2)}, u32[]{:S(2)}) collective-permute-start(f32[136,256]{1,0:T(8,128)S(1)} %collective-permute-done.4.refs_5_), channel_id=1, source_target_pairs={{0,2},{2,4},{4,6},{6,7},{7,5},{5,3},{3,1},{1,0},{8,10},{10,12},{12... | collective-permute-start | bytes 417800 | tf_op jit(solution)/shard_map/ppermute | solution.py:66
  24.5 8.6 %collective-permute-start.13 = (f32[256,256]{1,0:T(8,128)S(1)}, f32[256,256]{1,0:T(8,128)S(1)}, u32[]{:S(2)}, u32[]{:S(2)}) collective-permute-start(f32[256,256]{1,0:T(8,128)S(1)} %collective-permute-done.11), channel_id=1, source_target_pairs={{0,2},{2,4},{4,6},{6,7},{7,5},{5,3},{3,1},{1,0},{8,9},{10,8},{12,1... | collective-permute-start | bytes 786440 | tf_op jit(solution)/shard_map/ppermute | solution.py:66
  29.3 1.4 %collective-permute-start.7 = (f32[256,128]{1,0:T(8,128)S(1)}, f32[256,128]{1,0:T(8,128)S(1)}, u32[]{:S(2)}, u32[]{:S(2)}) collective-permute-start(f32[256,128]{1,0:T(8,128)S(1)} %get-tuple-element.26.refs_10_), channel_id=1, source_target_pairs={{0,8},{8,0},{16,24},{24,16},{1,9},{9,1},{17,25},{25,17},{2,10},{10... | collective-permute-start | bytes 393224 | tf_op jit(solution)/shard_map/ppermute | solution.py:47
  29.4 8.0 %collective-permute-start.12 = (f32[128,256]{1,0:T(8,128)S(1)}, f32[128,256]{1,0:T(8,128)S(1)}, u32[]{:S(2)}, u32[]{:S(2)}) collective-permute-start(f32[128,256]{1,0:T(8,128)S(1)} %get-tuple-element.41), channel_id=1, source_target_pairs={{0,8},{8,0},{16,24},{24,16},{1,9},{9,1},{17,25},{25,17},{2,10},{10... | collective-permute-start | bytes 393224 | tf_op jit(solution)/shard_map/ppermute | solution.py:47
  31.5 5.6 %collective-permute-start.16 = (f32[256,128]{1,0:T(8,128)S(1)}, f32[256,128]{1,0:T(8,128)S(1)}, u32[]{:S(2)}, u32[]{:S(2)}) collective-permute-start(f32[256,128]{1,0:T(8,128)S(1)} %get-tuple-element.31.mine_ref), channel_id=1, source_target_pairs={{0,16},{8,24},{16,0},{24,8},{1,17},{9,25},{17,1},{25,9},{2,18},{10... | collective-permute-start | bytes 393224 | tf_op jit(solution)/shard_map/ppermute | solution.py:47
  33.1 4.3 %collective-permute-start.14 = (f32[128,256]{1,0:T(8,128)S(1)}, f32[128,256]{1,0:T(8,128)S(1)}, u32[]{:S(2)}, u32[]{:S(2)}) collective-permute-start(f32[128,256]{1,0:T(8,128)S(1)} %get-tuple-element.39), channel_id=1, source_target_pairs={{0,8},{8,0},{16,24},{24,16},{1,9},{9,1},{17,25},{25,17},{2,10},{10... | collective-permute-start | bytes 393224 | tf_op jit(solution)/shard_map/ppermute | solution.py:47
  33.2 5.0 %copy-start.1 = (f32[128,256]{1,0:T(8,128)S(1)}, f32[128,256]{1,0:T(8,128)}, u32[]{:S(2)}) copy-start(f32[128,256]{1,0:T(8,128)} %get-tuple-element.28.refs_0_) | copy-start | bytes 393220
  33.2 5.0 %collective-permute-start.15 = (f32[128,256]{1,0:T(8,128)S(1)}, f32[128,256]{1,0:T(8,128)S(1)}, u32[]{:S(2)}, u32[]{:S(2)}) collective-permute-start(f32[128,256]{1,0:T(8,128)S(1)} %get-tuple-element.40.refs_5_), channel_id=1, source_target_pairs={{0,2},{2,4},{4,6},{6,7},{7,5},{5,3},{3,1},{1,0},{8,9},{10,8},{12,1... | collective-permute-start | bytes 393224 | tf_op jit(solution)/shard_map/ppermute | solution.py:66
  37.3 1.4 %collective-permute-start.17 = (f32[256,128]{1,0:T(8,128)S(1)}, f32[256,128]{1,0:T(8,128)S(1)}, u32[]{:S(2)}, u32[]{:S(2)}) collective-permute-start(f32[256,128]{1,0:T(8,128)S(1)} %shard_map.51.mine_ref), channel_id=1, source_target_pairs={{0,8},{8,0},{16,24},{24,16},{1,9},{9,1},{17,25},{25,17},{2,10},{10... | collective-permute-start | bytes 393224 | tf_op jit(solution)/shard_map/ppermute | solution.py:47
  40.1 1.4 %collective-permute-start.18 = (f32[256,128]{1,0:T(8,128)S(1)}, f32[256,128]{1,0:T(8,128)S(1)}, u32[]{:S(2)}, u32[]{:S(2)}) collective-permute-start(f32[256,128]{1,0:T(8,128)S(1)} %get-tuple-element.33), channel_id=1, source_target_pairs={{0,8},{8,0},{16,24},{24,16},{1,9},{9,1},{17,25},{25,17},{2,10},{10... | collective-permute-start | bytes 393224 | tf_op jit(solution)/shard_map/ppermute | solution.py:47
  41.7 5.6 %collective-permute-start.19 = (f32[256,128]{1,0:T(8,128)S(1)}, f32[256,128]{1,0:T(8,128)S(1)}, u32[]{:S(2)}, u32[]{:S(2)}) collective-permute-start(f32[256,128]{1,0:T(8,128)S(1)} %get-tuple-element.35), channel_id=1, source_target_pairs={{0,16},{8,24},{16,0},{24,8},{1,17},{9,25},{17,1},{25,9},{2,18},{10... | collective-permute-start | bytes 393224 | tf_op jit(solution)/shard_map/ppermute | solution.py:47
  48.1 1.4 %collective-permute-start.20 = (f32[256,128]{1,0:T(8,128)S(1)}, f32[256,128]{1,0:T(8,128)S(1)}, u32[]{:S(2)}, u32[]{:S(2)}) collective-permute-start(f32[256,128]{1,0:T(8,128)S(1)} %get-tuple-element.37), channel_id=1, source_target_pairs={{0,8},{8,0},{16,24},{24,16},{1,9},{9,1},{17,25},{25,17},{2,10},{10... | collective-permute-start | bytes 393224 | tf_op jit(solution)/shard_map/ppermute | solution.py:47

commit v8 on v7

--- a/solution.py
+++ b/solution.py
@@ -18,6 +18,12 @@
 def product(a, b, dims):
     (a_high, a_low), (b_high, b_low) = a, b
     return term(a_high, b_high, dims) + (term(a_high, b_low, dims) + term(a_low, b_high, dims))
+
+
+def stacked_product(a, b, dims):
+    high, low = split(a)
+    both = term(jnp.concatenate([high, low], axis=0), b[0], dims)
+    return both[: a.shape[0]] + both[a.shape[0] :] + term(high, b[1], dims)
 
 
 def term(x, y, dims):
@@ -89,7 +95,7 @@
     for _ in range(1, lax.axis_size("blk") // 2):
         up, down = ring_step(up, 1, 1), ring_step(down, -1, -1)
         out += [up, down]
-    return out + [ring_step(up, 1, 1)]
+    return out + [ring_step(jnp.where(lax.axis_index("cube") % 2 == 0, up, down), 1, -1)]
 
 
 class Packing:
@@ -231,8 +237,8 @@
     vec_ref[part(1), :] = got_ref[:, :cols]
     vec_ref[part(3), :] = got_ref[:, cols:]
     diag = (high_ref[...], low_ref[...])
-    y = product(diag, split(vec_ref[...]), ((0,), (0,)))
-    vec_ref[...] = product(diag, split(y), ((1,), (0,)))
+    y = stacked_product(vec_ref[...].T, diag, ((1,), (0,)))
+    vec_ref[...] = stacked_product(y, diag, ((1,), (1,))).T
     keep_ref[:, :cols] = vec_ref[part(0), :]
     keep_ref[:, cols:] = vec_ref[part(2), :]
     send_ref[:, :cols] = vec_ref[part(1), :]
@@ -283,6 +289,10 @@
     out_ref[0] = product(split(pieces[0][: pk.rows, :]), split(w_ref[...]), ((1,), (0,)))
 
 
+def tie(value, other):
+    return lax.optimization_barrier((value, other))[0]
+
+
 def call(kernel, pk, args, outs, scratch=(), place=pltpu.VMEM, room=24, kind=jnp.float32):
     return pl.pallas_call(
         functools.partial(kernel, pk),
@@ -325,6 +335,7 @@
     )
     first = gather_both_ways(packed)
     last = gather_rows(top)
+    first[-1] = tie(first[-1], last[3])
     send, y0 = call(first_kernel, pk, first, [two, one], work((node, node), one))
     got = swap(send, "cube", 1)
     diag1 = split_diag(first, 1, block_of, None)

time: 50.7 us -> 49 us (0.966)
  starting transfers between devices: 21.6 us -> 19.4 us
  waiting for transfers between devices: 21.2 us -> 21.8 us
    ppermute x12, starting transfers between devices: 17.4 us -> 15.2 us  [ring_step(): return lax.ppermute(block, ('cube', 'blk'), route)]
  transfers between devices with their start and end apart: 21 -> 21, of which waited for: 12 -> 15; matrix products, arithmetic and copies ran while one was open for 0% -> 0% of each run, Pallas kernels for 4% -> 5%
where the time goes in v8:
time: 49 us; the launch traced here: 48.9 us
  waiting for transfers between devices  21.8 us (44%)
  starting transfers between devices  19.4 us (40%)
  Pallas kernels  7.42 us (15%)
    ppermute x12, starting transfers between devices, ring_step(): return lax.ppermute(block, ('cube', 'blk'), route)  15.2 us
    ppermute x12, waiting for transfers between devices, ring_step(): return lax.ppermute(block, ('cube', 'blk'), route)  12 us
    ppermute x9, waiting for transfers between devices, swap(): return lax.ppermute(block, axis, [(i, i ^ mask) for i in range(count)])  9.74 us
    pallas_call x10, Pallas kernels, call(): pl.pallas_call(functools.partial(kernel, pk), out_shape=[jax.ShapeDtypeSt...  7.42 us
    ppermute x9, starting transfers between devices, swap(): return lax.ppermute(block, axis, [(i, i ^ mask) for i in range(count)])  4.21 us
  transfers between devices with their start and end apart: 21, of which 15 were waited for; matrix products, arithmetic and copies ran while one was open for 0% of the time, Pallas kernels for 5%

profile of v8, /device:TPU:0, one launch (start us, length us, event | category | flops | bytes accessed | tf_op | source)
XLA Modules:
  0.0 48.9 jit_solution(16345239587069229308)
XLA Ops:
  0.0 1.9 %shard_map.46 = (f32[136,256]{1,0:T(8,128)}, f32[128,256]{1,0:T(8,128)}) custom-call(f32[3,1,1,32,64]{4,3,2,1,0:T(8,128)} %rhs_hbm.1, f32[2,1,1,2,16,32]{5,4,3,2,1,0:T(8,128)} %panels_hbm.1, s32[2,1,1,2,16]{4,3,2,1,0:T(2,128)} %maps_hbm.1, f32[224,256]{1,0:T(8,128)} %diag_hbm.1), custom_call_target="tpu_custom_call" | custom-call | tf_op jit(solution)/shard_map/pallas_call | solution.py:297
  1.9 3.0 %collective-permute-start.1 = (f32[136,256]{1,0:T(8,128)}, f32[136,256]{1,0:T(8,128)S(1)}, u32[]{:S(2)}, u32[]{:S(2)}) collective-permute-start(f32[136,256]{1,0:T(8,128)} %get-tuple-element.23.refs_0_), channel_id=1, source_target_pairs={{0,1},{2,0},{4,2},{6,4},{7,6},{5,7},{3,5},{1,3},{8,9},{10,8},{12,1... | collective-permute-start | bytes 417800 | tf_op jit(solution)/shard_map/ppermute | solution.py:72
  5.1 1.9 %collective-permute-start.8 = (f32[128,256]{1,0:T(8,128)}, f32[128,256]{1,0:T(8,128)S(1)}, u32[]{:S(2)}, u32[]{:S(2)}) collective-permute-start(f32[128,256]{1,0:T(8,128)} %get-tuple-element.24.refs_0_), channel_id=1, source_target_pairs={{0,1},{2,0},{4,2},{6,4},{7,6},{5,7},{3,5},{1,3},{8,9},{10,8},{12,1... | collective-permute-start | bytes 393224 | tf_op jit(solution)/shard_map/ppermute | solution.py:72
  7.1 2.6 %collective-permute-done.1.refs_2_ = f32[136,256]{1,0:T(8,128)S(1)} collective-permute-done((f32[136,256]{1,0:T(8,128)}, f32[136,256]{1,0:T(8,128)S(1)}, u32[]{:S(2)}, u32[]{:S(2)}) %collective-permute-start.1) | collective-permute-done | bytes 139296 | tf_op jit(solution)/shard_map/ppermute | solution.py:72
  9.7 2.0 %collective-permute-start.3 = (f32[136,256]{1,0:T(8,128)S(1)}, f32[136,256]{1,0:T(8,128)S(1)}, u32[]{:S(2)}, u32[]{:S(2)}) collective-permute-start(f32[136,256]{1,0:T(8,128)S(1)} %collective-permute-done.1.refs_2_), channel_id=1, source_target_pairs={{0,1},{2,0},{4,2},{6,4},{7,6},{5,7},{3,5},{1,3},{8,9},{10,8},{12,1... | collective-permute-start | bytes 417800 | tf_op jit(solution)/shard_map/ppermute | solution.py:72
  12.5 1.8 %collective-permute-done.7.refs_1_ = f32[128,256]{1,0:T(8,128)S(1)} collective-permute-done((f32[128,256]{1,0:T(8,128)}, f32[128,256]{1,0:T(8,128)S(1)}, u32[]{:S(2)}, u32[]{:S(2)}) %collective-permute-start.7) | collective-permute-done | bytes 131104 | tf_op jit(solution)/shard_map/ppermute | solution.py:72
  14.8 2.0 %collective-permute-start.5 = (f32[136,256]{1,0:T(8,128)S(1)}, f32[136,256]{1,0:T(8,128)S(1)}, u32[]{:S(2)}, u32[]{:S(2)}) collective-permute-start(f32[136,256]{1,0:T(8,128)S(1)} %collective-permute-done.3.refs_4_), channel_id=1, source_target_pairs={{0,1},{2,0},{4,2},{6,4},{7,6},{5,7},{3,5},{1,3},{8,9},{10,8},{12,1... | collective-permute-start | bytes 417800 | tf_op jit(solution)/shard_map/ppermute | solution.py:72
  16.9 2.0 %collective-permute-start.10 = (f32[256,256]{1,0:T(8,128)S(1)}, f32[256,256]{1,0:T(8,128)S(1)}, u32[]{:S(2)}, u32[]{:S(2)}) collective-permute-start(f32[256,256]{1,0:T(8,128)S(1)} %pad_maximum_fusion), channel_id=1, source_target_pairs={{0,2},{2,4},{4,6},{6,7},{7,5},{5,3},{3,1},{1,0},{8,9},{10,8},{12,1... | collective-permute-start | bytes 786440 | tf_op jit(solution)/shard_map/ppermute | solution.py:72
  18.9 2.4 %collective-permute-done.5.refs_6_ = f32[136,256]{1,0:T(8,128)S(1)} collective-permute-done((f32[136,256]{1,0:T(8,128)S(1)}, f32[136,256]{1,0:T(8,128)S(1)}, u32[]{:S(2)}, u32[]{:S(2)}) %collective-permute-start.5) | collective-permute-done | bytes 139296 | tf_op jit(solution)/shard_map/ppermute | solution.py:72
  21.9 1.6 %collective-permute-start.6 = (f32[136,256]{1,0:T(8,128)S(1)}, f32[136,256]{1,0:T(8,128)S(1)}, u32[]{:S(2)}, u32[]{:S(2)}) collective-permute-start(f32[136,256]{1,0:T(8,128)S(1)} %broadcast_select_fusion), channel_id=1, source_target_pairs={{0,2},{2,4},{4,6},{6,7},{7,5},{5,3},{3,1},{1,0},{8,9},{10,8},{12,1... | collective-permute-start | bytes 417800 | tf_op jit(solution)/shard_map/ppermute | solution.py:72
  23.5 1.2 %collective-permute-done.10 = f32[256,256]{1,0:T(8,128)S(1)} collective-permute-done((f32[256,256]{1,0:T(8,128)S(1)}, f32[256,256]{1,0:T(8,128)S(1)}, u32[]{:S(2)}, u32[]{:S(2)}) %collective-permute-start.10) | collective-permute-done | bytes 262176 | tf_op jit(solution)/shard_map/ppermute | solution.py:72
  25.3 1.6 %collective-permute-done.6.refs_7_ = f32[136,256]{1,0:T(8,128)S(1)} collective-permute-done((f32[136,256]{1,0:T(8,128)S(1)}, f32[136,256]{1,0:T(8,128)S(1)}, u32[]{:S(2)}, u32[]{:S(2)}) %collective-permute-start.6) | collective-permute-done | bytes 139296 | tf_op jit(solution)/shard_map/ppermute | solution.py:72
  29.1 0.8 %shard_map.49 = (f32[256,128]{1,0:T(8,128)S(1)}, f32[256,64]{1,0:T(8,128)S(1)}) custom-call(f32[136,256]{1,0:T(8,128)S(1)} %copy-done, f32[136,256]{1,0:T(8,128)S(1)} %collective-permute-done.refs_1_, f32[136,256]{1,0:T(8,128)S(1)} %collective-permute-done.1.refs_2_, f32[136,256]{1,0:T(8,128)S(1)} %collective-permute-done.2.refs_3_, ...), custom_call_target="tpu_custom_call" | custom-call | tf_op jit(solution)/shard_map/pallas_call | solution.py:297
  29.9 1.6 %collective-permute-start.16 = (f32[256,128]{1,0:T(8,128)S(1)}, f32[256,128]{1,0:T(8,128)S(1)}, u32[]{:S(2)}, u32[]{:S(2)}) collective-permute-start(f32[256,128]{1,0:T(8,128)S(1)} %get-tuple-element.33.mine_ref), channel_id=1, source_target_pairs={{0,16},{8,24},{16,0},{24,8},{1,17},{9,25},{17,1},{25,9},{2,18},{10... | collective-permute-start | bytes 393224 | tf_op jit(solution)/shard_map/ppermute | solution.py:53
  31.6 1.6 %collective-permute-start.15 = (f32[128,256]{1,0:T(8,128)S(1)}, f32[128,256]{1,0:T(8,128)S(1)}, u32[]{:S(2)}, u32[]{:S(2)}) collective-permute-start(f32[128,256]{1,0:T(8,128)S(1)} %get-tuple-element.42.refs_5_), channel_id=1, source_target_pairs={{0,2},{2,4},{4,6},{6,7},{7,5},{5,3},{3,1},{1,0},{8,9},{10,8},{12,1... | collective-permute-start | bytes 393224 | tf_op jit(solution)/shard_map/ppermute | solution.py:72
  33.1 2.4 %collective-permute-done.16.got_ref = f32[256,128]{1,0:T(8,128)S(1)} collective-permute-done((f32[256,128]{1,0:T(8,128)S(1)}, f32[256,128]{1,0:T(8,128)S(1)}, u32[]{:S(2)}, u32[]{:S(2)}) %collective-permute-start.16) | collective-permute-done | bytes 131104 | tf_op jit(solution)/shard_map/ppermute | solution.py:53
  35.8 0.8 %collective-permute-done.15.refs_7_ = f32[128,256]{1,0:T(8,128)S(1)} collective-permute-done((f32[128,256]{1,0:T(8,128)S(1)}, f32[128,256]{1,0:T(8,128)S(1)}, u32[]{:S(2)}, u32[]{:S(2)}) %collective-permute-start.15) | collective-permute-done | bytes 131104 | tf_op jit(solution)/shard_map/ppermute | solution.py:72
  37.1 1.3 %shard_map.52 = (f32[256,128]{1,0:T(8,128)S(1)}, f32[256,128]{1,0:T(8,128)S(1)}) custom-call(bf16[1024,256]{1,0:T(8,128)(2,1)S(1)} %get-tuple-element.31.high_ref, bf16[1024,256]{1,0:T(8,128)(2,1)S(1)} %get-tuple-element.32.low_ref, f32[256,128]{1,0:T(8,128)S(1)} %shard_map.51.mine_ref, f32[256,128]{1,0:T(8,128)S(1)} %collective-permute-done.17.got_ref), custom_call_target="tpu_custom_call" | custom-call | tf_op jit(solution)/shard_map/pallas_call | solution.py:297
  38.6 1.2 %collective-permute-done.18.got_ref = f32[256,128]{1,0:T(8,128)S(1)} collective-permute-done((f32[256,128]{1,0:T(8,128)S(1)}, f32[256,128]{1,0:T(8,128)S(1)}, u32[]{:S(2)}, u32[]{:S(2)}) %collective-permute-start.18) | collective-permute-done | bytes 131104 | tf_op jit(solution)/shard_map/ppermute | solution.py:53
  39.9 1.6 %collective-permute-start.19 = (f32[256,128]{1,0:T(8,128)S(1)}, f32[256,128]{1,0:T(8,128)S(1)}, u32[]{:S(2)}, u32[]{:S(2)}) collective-permute-start(f32[256,128]{1,0:T(8,128)S(1)} %get-tuple-element.37), channel_id=1, source_target_pairs={{0,16},{8,24},{16,0},{24,8},{1,17},{9,25},{17,1},{25,9},{2,18},{10... | collective-permute-start | bytes 393224 | tf_op jit(solution)/shard_map/ppermute | solution.py:53
  41.5 4.0 %collective-permute-done.19.refs_12_ = f32[256,128]{1,0:T(8,128)S(1)} collective-permute-done((f32[256,128]{1,0:T(8,128)S(1)}, f32[256,128]{1,0:T(8,128)S(1)}, u32[]{:S(2)}, u32[]{:S(2)}) %collective-permute-start.19) | collective-permute-done | bytes 131104 | tf_op jit(solution)/shard_map/ppermute | solution.py:53
  45.6 0.8 %shard_map.54 = (f32[256,128]{1,0:T(8,128)S(1)}, f32[256,128]{1,0:T(8,128)S(1)}, f32[32,64]{1,0:T(8,128)S(1)}) custom-call(f32[136,256]{1,0:T(8,128)S(1)} %copy-done, f32[136,256]{1,0:T(8,128)S(1)} %collective-permute-done.refs_1_, f32[136,256]{1,0:T(8,128)S(1)} %collective-permute-done.1.refs_2_, f32[136,256]{1,0:T(8,128)S(1)} %collective-permute-done.2.refs_3_, ...), custom_call_target="tpu_custom_call" | custom-call | tf_op jit(solution)/shard_map/pallas_call | solution.py:297
  46.4 1.3 %collective-permute-done.20.refs_10_ = f32[256,128]{1,0:T(8,128)S(1)} collective-permute-done((f32[256,128]{1,0:T(8,128)S(1)}, f32[256,128]{1,0:T(8,128)S(1)}, u32[]{:S(2)}, u32[]{:S(2)}) %collective-permute-start.20) | collective-permute-done | bytes 131104 | tf_op jit(solution)/shard_map/ppermute | solution.py:53
  47.7 1.1 %shard_map.55 = f32[3,32,64]{2,1,0:T(8,128)} custom-call(f32[136,256]{1,0:T(8,128)S(1)} %copy-done, f32[136,256]{1,0:T(8,128)S(1)} %collective-permute-done.refs_1_, f32[136,256]{1,0:T(8,128)S(1)} %collective-permute-done.1.refs_2_, f32[136,256]{1,0:T(8,128)S(1)} %collective-permute-done.2.refs_3_, f32[136,256]{1,0:T(8,128)S(1)} %collective-permute-done.3.refs_4_, ...), custom_call_target="tpu_custom_call" | custom-call | tf_op jit(solution)/shard_map/pallas_call | solution.py:297
  (37 shorter events, 6.3 us)
Async XLA Ops:
  1.9 7.8 %collective-permute-start.1 = (f32[136,256]{1,0:T(8,128)}, f32[136,256]{1,0:T(8,128)S(1)}, u32[]{:S(2)}, u32[]{:S(2)}) collective-permute-start(f32[136,256]{1,0:T(8,128)} %get-tuple-element.23.refs_0_), channel_id=1, source_target_pairs={{0,1},{2,0},{4,2},{6,4},{7,6},{5,7},{3,5},{1,3},{8,9},{10,8},{12,1... | collective-permute-start | bytes 417800 | tf_op jit(solution)/shard_map/ppermute | solution.py:72
  5.0 6.8 %collective-permute-start = (f32[136,256]{1,0:T(8,128)}, f32[136,256]{1,0:T(8,128)S(1)}, u32[]{:S(2)}, u32[]{:S(2)}) collective-permute-start(f32[136,256]{1,0:T(8,128)} %get-tuple-element.23.refs_0_), channel_id=1, source_target_pairs={{0,2},{2,4},{4,6},{6,7},{7,5},{5,3},{3,1},{1,0},{8,10},{10,12},{12... | collective-permute-start | bytes 417800 | tf_op jit(solution)/shard_map/ppermute | solution.py:72
  5.1 7.5 %collective-permute-start.8 = (f32[128,256]{1,0:T(8,128)}, f32[128,256]{1,0:T(8,128)S(1)}, u32[]{:S(2)}, u32[]{:S(2)}) collective-permute-start(f32[128,256]{1,0:T(8,128)} %get-tuple-element.24.refs_0_), channel_id=1, source_target_pairs={{0,1},{2,0},{4,2},{6,4},{7,6},{5,7},{3,5},{1,3},{8,9},{10,8},{12,1... | collective-permute-start | bytes 393224 | tf_op jit(solution)/shard_map/ppermute | solution.py:72
  7.0 7.3 %collective-permute-start.7 = (f32[128,256]{1,0:T(8,128)}, f32[128,256]{1,0:T(8,128)S(1)}, u32[]{:S(2)}, u32[]{:S(2)}) collective-permute-start(f32[128,256]{1,0:T(8,128)} %get-tuple-element.24.refs_0_), channel_id=1, source_target_pairs={{0,2},{2,4},{4,6},{6,7},{7,5},{5,3},{3,1},{1,0},{8,10},{10,12},{12... | collective-permute-start | bytes 393224 | tf_op jit(solution)/shard_map/ppermute | solution.py:72
  9.7 5.1 %collective-permute-start.3 = (f32[136,256]{1,0:T(8,128)S(1)}, f32[136,256]{1,0:T(8,128)S(1)}, u32[]{:S(2)}, u32[]{:S(2)}) collective-permute-start(f32[136,256]{1,0:T(8,128)S(1)} %collective-permute-done.1.refs_2_), channel_id=1, source_target_pairs={{0,1},{2,0},{4,2},{6,4},{7,6},{5,7},{3,5},{1,3},{8,9},{10,8},{12,1... | collective-permute-start | bytes 417800 | tf_op jit(solution)/shard_map/ppermute | solution.py:72
  11.7 5.1 %collective-permute-start.2 = (f32[136,256]{1,0:T(8,128)S(1)}, f32[136,256]{1,0:T(8,128)S(1)}, u32[]{:S(2)}, u32[]{:S(2)}) collective-permute-start(f32[136,256]{1,0:T(8,128)S(1)} %collective-permute-done.refs_1_), channel_id=1, source_target_pairs={{0,2},{2,4},{4,6},{6,7},{7,5},{5,3},{3,1},{1,0},{8,10},{10,12},{12... | collective-permute-start | bytes 417800 | tf_op jit(solution)/shard_map/ppermute | solution.py:72
  14.3 2.6 %collective-permute-start.9 = (f32[128,256]{1,0:T(8,128)S(1)}, f32[128,256]{1,0:T(8,128)S(1)}, u32[]{:S(2)}, u32[]{:S(2)}) collective-permute-start(f32[128,256]{1,0:T(8,128)S(1)} %get-tuple-element.46), channel_id=1, source_target_pairs={{0,8},{8,0},{16,24},{24,16},{1,9},{9,1},{17,25},{25,17},{2,10},{10... | collective-permute-start | bytes 393224 | tf_op jit(solution)/shard_map/ppermute | solution.py:53
  14.8 6.5 %collective-permute-start.5 = (f32[136,256]{1,0:T(8,128)S(1)}, f32[136,256]{1,0:T(8,128)S(1)}, u32[]{:S(2)}, u32[]{:S(2)}) collective-permute-start(f32[136,256]{1,0:T(8,128)S(1)} %collective-permute-done.3.refs_4_), channel_id=1, source_target_pairs={{0,1},{2,0},{4,2},{6,4},{7,6},{5,7},{3,5},{1,3},{8,9},{10,8},{12,1... | collective-permute-start | bytes 417800 | tf_op jit(solution)/shard_map/ppermute | solution.py:72
  16.8 5.1 %collective-permute-start.4 = (f32[136,256]{1,0:T(8,128)S(1)}, f32[136,256]{1,0:T(8,128)S(1)}, u32[]{:S(2)}, u32[]{:S(2)}) collective-permute-start(f32[136,256]{1,0:T(8,128)S(1)} %collective-permute-done.2.refs_3_), channel_id=1, source_target_pairs={{0,2},{2,4},{4,6},{6,7},{7,5},{5,3},{3,1},{1,0},{8,10},{10,12},{12... | collective-permute-start | bytes 417800 | tf_op jit(solution)/shard_map/ppermute | solution.py:72
  16.9 7.7 %collective-permute-start.10 = (f32[256,256]{1,0:T(8,128)S(1)}, f32[256,256]{1,0:T(8,128)S(1)}, u32[]{:S(2)}, u32[]{:S(2)}) collective-permute-start(f32[256,256]{1,0:T(8,128)S(1)} %pad_maximum_fusion), channel_id=1, source_target_pairs={{0,2},{2,4},{4,6},{6,7},{7,5},{5,3},{3,1},{1,0},{8,9},{10,8},{12,1... | collective-permute-start | bytes 786440 | tf_op jit(solution)/shard_map/ppermute | solution.py:72
  21.9 5.1 %copy-start = (f32[136,256]{1,0:T(8,128)S(1)}, f32[136,256]{1,0:T(8,128)}, u32[]{:S(2)}) copy-start(f32[136,256]{1,0:T(8,128)} %get-tuple-element.23.refs_0_) | copy-start | bytes 417796
  21.9 5.1 %collective-permute-start.6 = (f32[136,256]{1,0:T(8,128)S(1)}, f32[136,256]{1,0:T(8,128)S(1)}, u32[]{:S(2)}, u32[]{:S(2)}) collective-permute-start(f32[136,256]{1,0:T(8,128)S(1)} %broadcast_select_fusion), channel_id=1, source_target_pairs={{0,2},{2,4},{4,6},{6,7},{7,5},{5,3},{3,1},{1,0},{8,9},{10,8},{12,1... | collective-permute-start | bytes 417800 | tf_op jit(solution)/shard_map/ppermute | solution.py:72
  24.6 6.8 %collective-permute-start.13 = (f32[256,256]{1,0:T(8,128)S(1)}, f32[256,256]{1,0:T(8,128)S(1)}, u32[]{:S(2)}, u32[]{:S(2)}) collective-permute-start(f32[256,256]{1,0:T(8,128)S(1)} %collective-permute-done.10), channel_id=1, source_target_pairs={{0,2},{2,4},{4,6},{6,7},{7,5},{5,3},{3,1},{1,0},{8,9},{10,8},{12,1... | collective-permute-start | bytes 786440 | tf_op jit(solution)/shard_map/ppermute | solution.py:72
  27.7 1.4 %collective-permute-start.11 = (f32[256,128]{1,0:T(8,128)S(1)}, f32[256,128]{1,0:T(8,128)S(1)}, u32[]{:S(2)}, u32[]{:S(2)}) collective-permute-start(f32[256,128]{1,0:T(8,128)S(1)} %get-tuple-element.29.refs_10_), channel_id=1, source_target_pairs={{0,8},{8,0},{16,24},{24,16},{1,9},{9,1},{17,25},{25,17},{2,10},{10... | collective-permute-start | bytes 393224 | tf_op jit(solution)/shard_map/ppermute | solution.py:53
  27.8 8.0 %collective-permute-start.12 = (f32[128,256]{1,0:T(8,128)S(1)}, f32[128,256]{1,0:T(8,128)S(1)}, u32[]{:S(2)}, u32[]{:S(2)}) collective-permute-start(f32[128,256]{1,0:T(8,128)S(1)} %get-tuple-element.43), channel_id=1, source_target_pairs={{0,8},{8,0},{16,24},{24,16},{1,9},{9,1},{17,25},{25,17},{2,10},{10... | collective-permute-start | bytes 393224 | tf_op jit(solution)/shard_map/ppermute | solution.py:53
  29.9 5.6 %collective-permute-start.16 = (f32[256,128]{1,0:T(8,128)S(1)}, f32[256,128]{1,0:T(8,128)S(1)}, u32[]{:S(2)}, u32[]{:S(2)}) collective-permute-start(f32[256,128]{1,0:T(8,128)S(1)} %get-tuple-element.33.mine_ref), channel_id=1, source_target_pairs={{0,16},{8,24},{16,0},{24,8},{1,17},{9,25},{17,1},{25,9},{2,18},{10... | collective-permute-start | bytes 393224 | tf_op jit(solution)/shard_map/ppermute | solution.py:53
  31.5 4.3 %collective-permute-start.14 = (f32[128,256]{1,0:T(8,128)S(1)}, f32[128,256]{1,0:T(8,128)S(1)}, u32[]{:S(2)}, u32[]{:S(2)}) collective-permute-start(f32[128,256]{1,0:T(8,128)S(1)} %get-tuple-element.41), channel_id=1, source_target_pairs={{0,8},{8,0},{16,24},{24,16},{1,9},{9,1},{17,25},{25,17},{2,10},{10... | collective-permute-start | bytes 393224 | tf_op jit(solution)/shard_map/ppermute | solution.py:53
  31.6 5.0 %copy-start.1 = (f32[128,256]{1,0:T(8,128)S(1)}, f32[128,256]{1,0:T(8,128)}, u32[]{:S(2)}) copy-start(f32[128,256]{1,0:T(8,128)} %get-tuple-element.24.refs_0_) | copy-start | bytes 393220
  31.6 5.0 %collective-permute-start.15 = (f32[128,256]{1,0:T(8,128)S(1)}, f32[128,256]{1,0:T(8,128)S(1)}, u32[]{:S(2)}, u32[]{:S(2)}) collective-permute-start(f32[128,256]{1,0:T(8,128)S(1)} %get-tuple-element.42.refs_5_), channel_id=1, source_target_pairs={{0,2},{2,4},{4,6},{6,7},{7,5},{5,3},{3,1},{1,0},{8,9},{10,8},{12,1... | collective-permute-start | bytes 393224 | tf_op jit(solution)/shard_map/ppermute | solution.py:72
  35.7 1.4 %collective-permute-start.17 = (f32[256,128]{1,0:T(8,128)S(1)}, f32[256,128]{1,0:T(8,128)S(1)}, u32[]{:S(2)}, u32[]{:S(2)}) collective-permute-start(f32[256,128]{1,0:T(8,128)S(1)} %shard_map.51.mine_ref), channel_id=1, source_target_pairs={{0,8},{8,0},{16,24},{24,16},{1,9},{9,1},{17,25},{25,17},{2,10},{10... | collective-permute-start | bytes 393224 | tf_op jit(solution)/shard_map/ppermute | solution.py:53
  38.4 1.4 %collective-permute-start.18 = (f32[256,128]{1,0:T(8,128)S(1)}, f32[256,128]{1,0:T(8,128)S(1)}, u32[]{:S(2)}, u32[]{:S(2)}) collective-permute-start(f32[256,128]{1,0:T(8,128)S(1)} %get-tuple-element.35), channel_id=1, source_target_pairs={{0,8},{8,0},{16,24},{24,16},{1,9},{9,1},{17,25},{25,17},{2,10},{10... | collective-permute-start | bytes 393224 | tf_op jit(solution)/shard_map/ppermute | solution.py:53
  39.9 5.6 %collective-permute-start.19 = (f32[256,128]{1,0:T(8,128)S(1)}, f32[256,128]{1,0:T(8,128)S(1)}, u32[]{:S(2)}, u32[]{:S(2)}) collective-permute-start(f32[256,128]{1,0:T(8,128)S(1)} %get-tuple-element.37), channel_id=1, source_target_pairs={{0,16},{8,24},{16,0},{24,8},{1,17},{9,25},{17,1},{25,9},{2,18},{10... | collective-permute-start | bytes 393224 | tf_op jit(solution)/shard_map/ppermute | solution.py:53
  46.3 1.4 %collective-permute-start.20 = (f32[256,128]{1,0:T(8,128)S(1)}, f32[256,128]{1,0:T(8,128)S(1)}, u32[]{:S(2)}, u32[]{:S(2)}) collective-permute-start(f32[256,128]{1,0:T(8,128)S(1)} %get-tuple-element.39), channel_id=1, source_target_pairs={{0,8},{8,0},{16,24},{24,16},{1,9},{9,1},{17,25},{25,17},{2,10},{10... | collective-permute-start | bytes 393224 | tf_op jit(solution)/shard_map/ppermute | solution.py:53

commit v9 on v8

--- a/solution.py
+++ b/solution.py
@@ -204,7 +204,7 @@
     pk.diag(pieces, 0, diag_ref, block_of)
     for m, piece in enumerate(pieces):
         z_ref[block_of(pk, m), :] = pk.rhs(piece, 0)
-    y_ref[...] = product(split(diag_ref[...]), split(z_ref[...]), ((0,), (0,)))
+    y_ref[...] = stacked_product(z_ref[...].T, split(diag_ref[...]), ((1,), (0,))).T
     extend_out(pk, 0, pieces, y_ref, send_ref)
 
 
@@ -215,7 +215,7 @@
     other = got_ref[:, :cols] - mine_ref[:, cols:]
     upper = lax.axis_index("cube") % 2 == 1
     z = jnp.concatenate([jnp.where(upper, other, own), jnp.where(upper, own, other)], axis=0)
-    y_ref[...] = product((high_ref[...], low_ref[...]), split(z), ((0,), (0,)))
+    y_ref[...] = stacked_product(z.T, (high_ref[...], low_ref[...]), ((1,), (0,))).T
     extend_out(pk, 1, pieces, y_ref, send_ref)
 
 
@@ -269,7 +269,7 @@
     own_rows = block_of(pk, 0)
     top_ref[...] = mine_ref[own_rows, :cols] + got_ref[own_rows, :cols]
     reduce_rows(pk, 1, pieces, y_ref, mine_ref, got_ref, w_ref)
-    x = product((high_ref[...], low_ref[...]), split(w_ref[...]), ((1,), (0,)))
+    x = stacked_product(w_ref[...].T, (high_ref[...], low_ref[...]), ((1,), (1,))).T
     upper = lax.axis_index("cube") % 2 == 1
     own = jnp.where(upper, x[node:], x[:node])
     other = jnp.where(upper, x[:node], x[node:])

time: 49 us -> 49.1 us (level)
  no operation moved by 1% of the time
where the time goes in v9:
time: 49.1 us; the launch traced here: 49 us
  waiting for transfers between devices  21.8 us (44%)
  starting transfers between devices  19.4 us (40%)
  Pallas kernels  7.55 us (15%)
    ppermute x12, starting transfers between devices, ring_step(): return lax.ppermute(block, ('cube', 'blk'), route)  15.2 us
    ppermute x12, waiting for transfers between devices, ring_step(): return lax.ppermute(block, ('cube', 'blk'), route)  12 us
    ppermute x9, waiting for transfers between devices, swap(): return lax.ppermute(block, axis, [(i, i ^ mask) for i in range(count)])  9.75 us
    pallas_call x10, Pallas kernels, call(): pl.pallas_call(functools.partial(kernel, pk), out_shape=[jax.ShapeDtypeSt...  7.55 us
    ppermute x9, starting transfers between devices, swap(): return lax.ppermute(block, axis, [(i, i ^ mask) for i in range(count)])  4.19 us
  transfers between devices with their start and end apart: 21, of which 15 were waited for; matrix products, arithmetic and copies ran while one was open for 0% of the time, Pallas kernels for 5%

profile of v9, /device:TPU:0, one launch (start us, length us, event | category | flops | bytes accessed | tf_op | source)
XLA Modules:
  0.0 49.0 jit_solution(13587761376139628722)
XLA Ops:
  0.0 1.9 %shard_map.46 = (f32[136,256]{1,0:T(8,128)}, f32[128,256]{1,0:T(8,128)}) custom-call(f32[3,1,1,32,64]{4,3,2,1,0:T(8,128)} %rhs_hbm.1, f32[2,1,1,2,16,32]{5,4,3,2,1,0:T(8,128)} %panels_hbm.1, s32[2,1,1,2,16]{4,3,2,1,0:T(2,128)} %maps_hbm.1, f32[224,256]{1,0:T(8,128)} %diag_hbm.1), custom_call_target="tpu_custom_call" | custom-call | tf_op jit(solution)/shard_map/pallas_call | solution.py:297
  1.9 3.0 %collective-permute-start.1 = (f32[136,256]{1,0:T(8,128)}, f32[136,256]{1,0:T(8,128)S(1)}, u32[]{:S(2)}, u32[]{:S(2)}) collective-permute-start(f32[136,256]{1,0:T(8,128)} %get-tuple-element.23.refs_0_), channel_id=1, source_target_pairs={{0,1},{2,0},{4,2},{6,4},{7,6},{5,7},{3,5},{1,3},{8,9},{10,8},{12,1... | collective-permute-start | bytes 417800 | tf_op jit(solution)/shard_map/ppermute | solution.py:72
  5.1 1.9 %collective-permute-start.8 = (f32[128,256]{1,0:T(8,128)}, f32[128,256]{1,0:T(8,128)S(1)}, u32[]{:S(2)}, u32[]{:S(2)}) collective-permute-start(f32[128,256]{1,0:T(8,128)} %get-tuple-element.24.refs_0_), channel_id=1, source_target_pairs={{0,1},{2,0},{4,2},{6,4},{7,6},{5,7},{3,5},{1,3},{8,9},{10,8},{12,1... | collective-permute-start | bytes 393224 | tf_op jit(solution)/shard_map/ppermute | solution.py:72
  7.1 2.6 %collective-permute-done.1.refs_2_ = f32[136,256]{1,0:T(8,128)S(1)} collective-permute-done((f32[136,256]{1,0:T(8,128)}, f32[136,256]{1,0:T(8,128)S(1)}, u32[]{:S(2)}, u32[]{:S(2)}) %collective-permute-start.1) | collective-permute-done | bytes 139296 | tf_op jit(solution)/shard_map/ppermute | solution.py:72
  9.7 2.0 %collective-permute-start.3 = (f32[136,256]{1,0:T(8,128)S(1)}, f32[136,256]{1,0:T(8,128)S(1)}, u32[]{:S(2)}, u32[]{:S(2)}) collective-permute-start(f32[136,256]{1,0:T(8,128)S(1)} %collective-permute-done.1.refs_2_), channel_id=1, source_target_pairs={{0,1},{2,0},{4,2},{6,4},{7,6},{5,7},{3,5},{1,3},{8,9},{10,8},{12,1... | collective-permute-start | bytes 417800 | tf_op jit(solution)/shard_map/ppermute | solution.py:72
  12.5 1.8 %collective-permute-done.7.refs_1_ = f32[128,256]{1,0:T(8,128)S(1)} collective-permute-done((f32[128,256]{1,0:T(8,128)}, f32[128,256]{1,0:T(8,128)S(1)}, u32[]{:S(2)}, u32[]{:S(2)}) %collective-permute-start.7) | collective-permute-done | bytes 131104 | tf_op jit(solution)/shard_map/ppermute | solution.py:72
  14.8 2.0 %collective-permute-start.5 = (f32[136,256]{1,0:T(8,128)S(1)}, f32[136,256]{1,0:T(8,128)S(1)}, u32[]{:S(2)}, u32[]{:S(2)}) collective-permute-start(f32[136,256]{1,0:T(8,128)S(1)} %collective-permute-done.3.refs_4_), channel_id=1, source_target_pairs={{0,1},{2,0},{4,2},{6,4},{7,6},{5,7},{3,5},{1,3},{8,9},{10,8},{12,1... | collective-permute-start | bytes 417800 | tf_op jit(solution)/shard_map/ppermute | solution.py:72
  16.9 2.0 %collective-permute-start.10 = (f32[256,256]{1,0:T(8,128)S(1)}, f32[256,256]{1,0:T(8,128)S(1)}, u32[]{:S(2)}, u32[]{:S(2)}) collective-permute-start(f32[256,256]{1,0:T(8,128)S(1)} %pad_maximum_fusion), channel_id=1, source_target_pairs={{0,2},{2,4},{4,6},{6,7},{7,5},{5,3},{3,1},{1,0},{8,9},{10,8},{12,1... | collective-permute-start | bytes 786440 | tf_op jit(solution)/shard_map/ppermute | solution.py:72
  18.9 2.4 %collective-permute-done.5.refs_6_ = f32[136,256]{1,0:T(8,128)S(1)} collective-permute-done((f32[136,256]{1,0:T(8,128)S(1)}, f32[136,256]{1,0:T(8,128)S(1)}, u32[]{:S(2)}, u32[]{:S(2)}) %collective-permute-start.5) | collective-permute-done | bytes 139296 | tf_op jit(solution)/shard_map/ppermute | solution.py:72
  21.9 1.6 %collective-permute-start.6 = (f32[136,256]{1,0:T(8,128)S(1)}, f32[136,256]{1,0:T(8,128)S(1)}, u32[]{:S(2)}, u32[]{:S(2)}) collective-permute-start(f32[136,256]{1,0:T(8,128)S(1)} %broadcast_select_fusion), channel_id=1, source_target_pairs={{0,2},{2,4},{4,6},{6,7},{7,5},{5,3},{3,1},{1,0},{8,9},{10,8},{12,1... | collective-permute-start | bytes 417800 | tf_op jit(solution)/shard_map/ppermute | solution.py:72
  23.5 1.2 %collective-permute-done.10 = f32[256,256]{1,0:T(8,128)S(1)} collective-permute-done((f32[256,256]{1,0:T(8,128)S(1)}, f32[256,256]{1,0:T(8,128)S(1)}, u32[]{:S(2)}, u32[]{:S(2)}) %collective-permute-start.10) | collective-permute-done | bytes 262176 | tf_op jit(solution)/shard_map/ppermute | solution.py:72
  25.3 1.6 %collective-permute-done.6.refs_7_ = f32[136,256]{1,0:T(8,128)S(1)} collective-permute-done((f32[136,256]{1,0:T(8,128)S(1)}, f32[136,256]{1,0:T(8,128)S(1)}, u32[]{:S(2)}, u32[]{:S(2)}) %collective-permute-start.6) | collective-permute-done | bytes 139296 | tf_op jit(solution)/shard_map/ppermute | solution.py:72
  29.1 0.8 %shard_map.49 = (f32[256,128]{1,0:T(8,128)S(1)}, f32[256,64]{1,0:T(8,128)S(1)}) custom-call(f32[136,256]{1,0:T(8,128)S(1)} %copy-done, f32[136,256]{1,0:T(8,128)S(1)} %collective-permute-done.refs_1_, f32[136,256]{1,0:T(8,128)S(1)} %collective-permute-done.1.refs_2_, f32[136,256]{1,0:T(8,128)S(1)} %collective-permute-done.2.refs_3_, ...), custom_call_target="tpu_custom_call" | custom-call | tf_op jit(solution)/shard_map/pallas_call | solution.py:297
  29.9 1.6 %collective-permute-start.16 = (f32[256,128]{1,0:T(8,128)S(1)}, f32[256,128]{1,0:T(8,128)S(1)}, u32[]{:S(2)}, u32[]{:S(2)}) collective-permute-start(f32[256,128]{1,0:T(8,128)S(1)} %get-tuple-element.33.mine_ref), channel_id=1, source_target_pairs={{0,16},{8,24},{16,0},{24,8},{1,17},{9,25},{17,1},{25,9},{2,18},{10... | collective-permute-start | bytes 393224 | tf_op jit(solution)/shard_map/ppermute | solution.py:53
  31.6 1.6 %collective-permute-start.15 = (f32[128,256]{1,0:T(8,128)S(1)}, f32[128,256]{1,0:T(8,128)S(1)}, u32[]{:S(2)}, u32[]{:S(2)}) collective-permute-start(f32[128,256]{1,0:T(8,128)S(1)} %get-tuple-element.42.refs_5_), channel_id=1, source_target_pairs={{0,2},{2,4},{4,6},{6,7},{7,5},{5,3},{3,1},{1,0},{8,9},{10,8},{12,1... | collective-permute-start | bytes 393224 | tf_op jit(solution)/shard_map/ppermute | solution.py:72
  33.2 2.4 %collective-permute-done.16.got_ref = f32[256,128]{1,0:T(8,128)S(1)} collective-permute-done((f32[256,128]{1,0:T(8,128)S(1)}, f32[256,128]{1,0:T(8,128)S(1)}, u32[]{:S(2)}, u32[]{:S(2)}) %collective-permute-start.16) | collective-permute-done | bytes 131104 | tf_op jit(solution)/shard_map/ppermute | solution.py:53
  35.8 0.8 %collective-permute-done.15.refs_7_ = f32[128,256]{1,0:T(8,128)S(1)} collective-permute-done((f32[128,256]{1,0:T(8,128)S(1)}, f32[128,256]{1,0:T(8,128)S(1)}, u32[]{:S(2)}, u32[]{:S(2)}) %collective-permute-start.15) | collective-permute-done | bytes 131104 | tf_op jit(solution)/shard_map/ppermute | solution.py:72
  37.2 1.3 %shard_map.52 = (f32[256,128]{1,0:T(8,128)S(1)}, f32[256,128]{1,0:T(8,128)S(1)}) custom-call(bf16[1024,256]{1,0:T(8,128)(2,1)S(1)} %get-tuple-element.31.high_ref, bf16[1024,256]{1,0:T(8,128)(2,1)S(1)} %get-tuple-element.32.low_ref, f32[256,128]{1,0:T(8,128)S(1)} %shard_map.51.mine_ref, f32[256,128]{1,0:T(8,128)S(1)} %collective-permute-done.17.got_ref), custom_call_target="tpu_custom_call" | custom-call | tf_op jit(solution)/shard_map/pallas_call | solution.py:297
  38.7 1.2 %collective-permute-done.18.got_ref = f32[256,128]{1,0:T(8,128)S(1)} collective-permute-done((f32[256,128]{1,0:T(8,128)S(1)}, f32[256,128]{1,0:T(8,128)S(1)}, u32[]{:S(2)}, u32[]{:S(2)}) %collective-permute-start.18) | collective-permute-done | bytes 131104 | tf_op jit(solution)/shard_map/ppermute | solution.py:53
  40.0 1.6 %collective-permute-start.19 = (f32[256,128]{1,0:T(8,128)S(1)}, f32[256,128]{1,0:T(8,128)S(1)}, u32[]{:S(2)}, u32[]{:S(2)}) collective-permute-start(f32[256,128]{1,0:T(8,128)S(1)} %get-tuple-element.37), channel_id=1, source_target_pairs={{0,16},{8,24},{16,0},{24,8},{1,17},{9,25},{17,1},{25,9},{2,18},{10... | collective-permute-start | bytes 393224 | tf_op jit(solution)/shard_map/ppermute | solution.py:53
  41.6 4.0 %collective-permute-done.19.refs_12_ = f32[256,128]{1,0:T(8,128)S(1)} collective-permute-done((f32[256,128]{1,0:T(8,128)S(1)}, f32[256,128]{1,0:T(8,128)S(1)}, u32[]{:S(2)}, u32[]{:S(2)}) %collective-permute-start.19) | collective-permute-done | bytes 131104 | tf_op jit(solution)/shard_map/ppermute | solution.py:53
  45.6 0.8 %shard_map.54 = (f32[256,128]{1,0:T(8,128)S(1)}, f32[256,128]{1,0:T(8,128)S(1)}, f32[32,64]{1,0:T(8,128)S(1)}) custom-call(f32[136,256]{1,0:T(8,128)S(1)} %copy-done, f32[136,256]{1,0:T(8,128)S(1)} %collective-permute-done.refs_1_, f32[136,256]{1,0:T(8,128)S(1)} %collective-permute-done.1.refs_2_, f32[136,256]{1,0:T(8,128)S(1)} %collective-permute-done.2.refs_3_, ...), custom_call_target="tpu_custom_call" | custom-call | tf_op jit(solution)/shard_map/pallas_call | solution.py:297
  46.5 1.3 %collective-permute-done.20.refs_10_ = f32[256,128]{1,0:T(8,128)S(1)} collective-permute-done((f32[256,128]{1,0:T(8,128)S(1)}, f32[256,128]{1,0:T(8,128)S(1)}, u32[]{:S(2)}, u32[]{:S(2)}) %collective-permute-start.20) | collective-permute-done | bytes 131104 | tf_op jit(solution)/shard_map/ppermute | solution.py:53
  47.9 1.1 %shard_map.55 = f32[3,32,64]{2,1,0:T(8,128)} custom-call(f32[136,256]{1,0:T(8,128)S(1)} %copy-done, f32[136,256]{1,0:T(8,128)S(1)} %collective-permute-done.refs_1_, f32[136,256]{1,0:T(8,128)S(1)} %collective-permute-done.1.refs_2_, f32[136,256]{1,0:T(8,128)S(1)} %collective-permute-done.2.refs_3_, f32[136,256]{1,0:T(8,128)S(1)} %collective-permute-done.3.refs_4_, ...), custom_call_target="tpu_custom_call" | custom-call | tf_op jit(solution)/shard_map/pallas_call | solution.py:297
  (37 shorter events, 6.3 us)
Async XLA Ops:
  1.9 7.8 %collective-permute-start.1 = (f32[136,256]{1,0:T(8,128)}, f32[136,256]{1,0:T(8,128)S(1)}, u32[]{:S(2)}, u32[]{:S(2)}) collective-permute-start(f32[136,256]{1,0:T(8,128)} %get-tuple-element.23.refs_0_), channel_id=1, source_target_pairs={{0,1},{2,0},{4,2},{6,4},{7,6},{5,7},{3,5},{1,3},{8,9},{10,8},{12,1... | collective-permute-start | bytes 417800 | tf_op jit(solution)/shard_map/ppermute | solution.py:72
  5.0 6.8 %collective-permute-start = (f32[136,256]{1,0:T(8,128)}, f32[136,256]{1,0:T(8,128)S(1)}, u32[]{:S(2)}, u32[]{:S(2)}) collective-permute-start(f32[136,256]{1,0:T(8,128)} %get-tuple-element.23.refs_0_), channel_id=1, source_target_pairs={{0,2},{2,4},{4,6},{6,7},{7,5},{5,3},{3,1},{1,0},{8,10},{10,12},{12... | collective-permute-start | bytes 417800 | tf_op jit(solution)/shard_map/ppermute | solution.py:72
  5.1 7.5 %collective-permute-start.8 = (f32[128,256]{1,0:T(8,128)}, f32[128,256]{1,0:T(8,128)S(1)}, u32[]{:S(2)}, u32[]{:S(2)}) collective-permute-start(f32[128,256]{1,0:T(8,128)} %get-tuple-element.24.refs_0_), channel_id=1, source_target_pairs={{0,1},{2,0},{4,2},{6,4},{7,6},{5,7},{3,5},{1,3},{8,9},{10,8},{12,1... | collective-permute-start | bytes 393224 | tf_op jit(solution)/shard_map/ppermute | solution.py:72
  7.0 7.3 %collective-permute-start.7 = (f32[128,256]{1,0:T(8,128)}, f32[128,256]{1,0:T(8,128)S(1)}, u32[]{:S(2)}, u32[]{:S(2)}) collective-permute-start(f32[128,256]{1,0:T(8,128)} %get-tuple-element.24.refs_0_), channel_id=1, source_target_pairs={{0,2},{2,4},{4,6},{6,7},{7,5},{5,3},{3,1},{1,0},{8,10},{10,12},{12... | collective-permute-start | bytes 393224 | tf_op jit(solution)/shard_map/ppermute | solution.py:72
  9.7 5.1 %collective-permute-start.3 = (f32[136,256]{1,0:T(8,128)S(1)}, f32[136,256]{1,0:T(8,128)S(1)}, u32[]{:S(2)}, u32[]{:S(2)}) collective-permute-start(f32[136,256]{1,0:T(8,128)S(1)} %collective-permute-done.1.refs_2_), channel_id=1, source_target_pairs={{0,1},{2,0},{4,2},{6,4},{7,6},{5,7},{3,5},{1,3},{8,9},{10,8},{12,1... | collective-permute-start | bytes 417800 | tf_op jit(solution)/shard_map/ppermute | solution.py:72
  11.7 5.1 %collective-permute-start.2 = (f32[136,256]{1,0:T(8,128)S(1)}, f32[136,256]{1,0:T(8,128)S(1)}, u32[]{:S(2)}, u32[]{:S(2)}) collective-permute-start(f32[136,256]{1,0:T(8,128)S(1)} %collective-permute-done.refs_1_), channel_id=1, source_target_pairs={{0,2},{2,4},{4,6},{6,7},{7,5},{5,3},{3,1},{1,0},{8,10},{10,12},{12... | collective-permute-start | bytes 417800 | tf_op jit(solution)/shard_map/ppermute | solution.py:72
  14.3 2.6 %collective-permute-start.9 = (f32[128,256]{1,0:T(8,128)S(1)}, f32[128,256]{1,0:T(8,128)S(1)}, u32[]{:S(2)}, u32[]{:S(2)}) collective-permute-start(f32[128,256]{1,0:T(8,128)S(1)} %get-tuple-element.46), channel_id=1, source_target_pairs={{0,8},{8,0},{16,24},{24,16},{1,9},{9,1},{17,25},{25,17},{2,10},{10... | collective-permute-start | bytes 393224 | tf_op jit(solution)/shard_map/ppermute | solution.py:53
  14.8 6.5 %collective-permute-start.5 = (f32[136,256]{1,0:T(8,128)S(1)}, f32[136,256]{1,0:T(8,128)S(1)}, u32[]{:S(2)}, u32[]{:S(2)}) collective-permute-start(f32[136,256]{1,0:T(8,128)S(1)} %collective-permute-done.3.refs_4_), channel_id=1, source_target_pairs={{0,1},{2,0},{4,2},{6,4},{7,6},{5,7},{3,5},{1,3},{8,9},{10,8},{12,1... | collective-permute-start | bytes 417800 | tf_op jit(solution)/shard_map/ppermute | solution.py:72
  16.8 5.1 %collective-permute-start.4 = (f32[136,256]{1,0:T(8,128)S(1)}, f32[136,256]{1,0:T(8,128)S(1)}, u32[]{:S(2)}, u32[]{:S(2)}) collective-permute-start(f32[136,256]{1,0:T(8,128)S(1)} %collective-permute-done.2.refs_3_), channel_id=1, source_target_pairs={{0,2},{2,4},{4,6},{6,7},{7,5},{5,3},{3,1},{1,0},{8,10},{10,12},{12... | collective-permute-start | bytes 417800 | tf_op jit(solution)/shard_map/ppermute | solution.py:72
  16.9 7.7 %collective-permute-start.10 = (f32[256,256]{1,0:T(8,128)S(1)}, f32[256,256]{1,0:T(8,128)S(1)}, u32[]{:S(2)}, u32[]{:S(2)}) collective-permute-start(f32[256,256]{1,0:T(8,128)S(1)} %pad_maximum_fusion), channel_id=1, source_target_pairs={{0,2},{2,4},{4,6},{6,7},{7,5},{5,3},{3,1},{1,0},{8,9},{10,8},{12,1... | collective-permute-start | bytes 786440 | tf_op jit(solution)/shard_map/ppermute | solution.py:72
  21.9 5.1 %copy-start = (f32[136,256]{1,0:T(8,128)S(1)}, f32[136,256]{1,0:T(8,128)}, u32[]{:S(2)}) copy-start(f32[136,256]{1,0:T(8,128)} %get-tuple-element.23.refs_0_) | copy-start | bytes 417796
  21.9 5.1 %collective-permute-start.6 = (f32[136,256]{1,0:T(8,128)S(1)}, f32[136,256]{1,0:T(8,128)S(1)}, u32[]{:S(2)}, u32[]{:S(2)}) collective-permute-start(f32[136,256]{1,0:T(8,128)S(1)} %broadcast_select_fusion), channel_id=1, source_target_pairs={{0,2},{2,4},{4,6},{6,7},{7,5},{5,3},{3,1},{1,0},{8,9},{10,8},{12,1... | collective-permute-start | bytes 417800 | tf_op jit(solution)/shard_map/ppermute | solution.py:72
  24.6 6.9 %collective-permute-start.13 = (f32[256,256]{1,0:T(8,128)S(1)}, f32[256,256]{1,0:T(8,128)S(1)}, u32[]{:S(2)}, u32[]{:S(2)}) collective-permute-start(f32[256,256]{1,0:T(8,128)S(1)} %collective-permute-done.10), channel_id=1, source_target_pairs={{0,2},{2,4},{4,6},{6,7},{7,5},{5,3},{3,1},{1,0},{8,9},{10,8},{12,1... | collective-permute-start | bytes 786440 | tf_op jit(solution)/shard_map/ppermute | solution.py:72
  27.7 1.4 %collective-permute-start.11 = (f32[256,128]{1,0:T(8,128)S(1)}, f32[256,128]{1,0:T(8,128)S(1)}, u32[]{:S(2)}, u32[]{:S(2)}) collective-permute-start(f32[256,128]{1,0:T(8,128)S(1)} %get-tuple-element.29.refs_10_), channel_id=1, source_target_pairs={{0,8},{8,0},{16,24},{24,16},{1,9},{9,1},{17,25},{25,17},{2,10},{10... | collective-permute-start | bytes 393224 | tf_op jit(solution)/shard_map/ppermute | solution.py:53
  27.8 8.0 %collective-permute-start.12 = (f32[128,256]{1,0:T(8,128)S(1)}, f32[128,256]{1,0:T(8,128)S(1)}, u32[]{:S(2)}, u32[]{:S(2)}) collective-permute-start(f32[128,256]{1,0:T(8,128)S(1)} %get-tuple-element.43), channel_id=1, source_target_pairs={{0,8},{8,0},{16,24},{24,16},{1,9},{9,1},{17,25},{25,17},{2,10},{10... | collective-permute-start | bytes 393224 | tf_op jit(solution)/shard_map/ppermute | solution.py:53
  29.9 5.6 %collective-permute-start.16 = (f32[256,128]{1,0:T(8,128)S(1)}, f32[256,128]{1,0:T(8,128)S(1)}, u32[]{:S(2)}, u32[]{:S(2)}) collective-permute-start(f32[256,128]{1,0:T(8,128)S(1)} %get-tuple-element.33.mine_ref), channel_id=1, source_target_pairs={{0,16},{8,24},{16,0},{24,8},{1,17},{9,25},{17,1},{25,9},{2,18},{10... | collective-permute-start | bytes 393224 | tf_op jit(solution)/shard_map/ppermute | solution.py:53
  31.5 4.3 %collective-permute-start.14 = (f32[128,256]{1,0:T(8,128)S(1)}, f32[128,256]{1,0:T(8,128)S(1)}, u32[]{:S(2)}, u32[]{:S(2)}) collective-permute-start(f32[128,256]{1,0:T(8,128)S(1)} %get-tuple-element.41), channel_id=1, source_target_pairs={{0,8},{8,0},{16,24},{24,16},{1,9},{9,1},{17,25},{25,17},{2,10},{10... | collective-permute-start | bytes 393224 | tf_op jit(solution)/shard_map/ppermute | solution.py:53
  31.6 5.0 %copy-start.1 = (f32[128,256]{1,0:T(8,128)S(1)}, f32[128,256]{1,0:T(8,128)}, u32[]{:S(2)}) copy-start(f32[128,256]{1,0:T(8,128)} %get-tuple-element.24.refs_0_) | copy-start | bytes 393220
  31.6 5.0 %collective-permute-start.15 = (f32[128,256]{1,0:T(8,128)S(1)}, f32[128,256]{1,0:T(8,128)S(1)}, u32[]{:S(2)}, u32[]{:S(2)}) collective-permute-start(f32[128,256]{1,0:T(8,128)S(1)} %get-tuple-element.42.refs_5_), channel_id=1, source_target_pairs={{0,2},{2,4},{4,6},{6,7},{7,5},{5,3},{3,1},{1,0},{8,9},{10,8},{12,1... | collective-permute-start | bytes 393224 | tf_op jit(solution)/shard_map/ppermute | solution.py:72
  35.7 1.4 %collective-permute-start.17 = (f32[256,128]{1,0:T(8,128)S(1)}, f32[256,128]{1,0:T(8,128)S(1)}, u32[]{:S(2)}, u32[]{:S(2)}) collective-permute-start(f32[256,128]{1,0:T(8,128)S(1)} %shard_map.51.mine_ref), channel_id=1, source_target_pairs={{0,8},{8,0},{16,24},{24,16},{1,9},{9,1},{17,25},{25,17},{2,10},{10... | collective-permute-start | bytes 393224 | tf_op jit(solution)/shard_map/ppermute | solution.py:53
  38.5 1.4 %collective-permute-start.18 = (f32[256,128]{1,0:T(8,128)S(1)}, f32[256,128]{1,0:T(8,128)S(1)}, u32[]{:S(2)}, u32[]{:S(2)}) collective-permute-start(f32[256,128]{1,0:T(8,128)S(1)} %get-tuple-element.35), channel_id=1, source_target_pairs={{0,8},{8,0},{16,24},{24,16},{1,9},{9,1},{17,25},{25,17},{2,10},{10... | collective-permute-start | bytes 393224 | tf_op jit(solution)/shard_map/ppermute | solution.py:53
  40.0 5.6 %collective-permute-start.19 = (f32[256,128]{1,0:T(8,128)S(1)}, f32[256,128]{1,0:T(8,128)S(1)}, u32[]{:S(2)}, u32[]{:S(2)}) collective-permute-start(f32[256,128]{1,0:T(8,128)S(1)} %get-tuple-element.37), channel_id=1, source_target_pairs={{0,16},{8,24},{16,0},{24,8},{1,17},{9,25},{17,1},{25,9},{2,18},{10... | collective-permute-start | bytes 393224 | tf_op jit(solution)/shard_map/ppermute | solution.py:53
  46.4 1.4 %collective-permute-start.20 = (f32[256,128]{1,0:T(8,128)S(1)}, f32[256,128]{1,0:T(8,128)S(1)}, u32[]{:S(2)}, u32[]{:S(2)}) collective-permute-start(f32[256,128]{1,0:T(8,128)S(1)} %get-tuple-element.39), channel_id=1, source_target_pairs={{0,8},{8,0},{16,24},{24,16},{1,9},{9,1},{17,25},{25,17},{2,10},{10... | collective-permute-start | bytes 393224 | tf_op jit(solution)/shard_map/ppermute | solution.py:53

commit v10 on v9

--- a/solution.py
+++ b/solution.py
@@ -335,12 +335,11 @@
     )
     first = gather_both_ways(packed)
     last = gather_rows(top)
-    first[-1] = tie(first[-1], last[3])
     send, y0 = call(first_kernel, pk, first, [two, one], work((node, node), one))
-    got = swap(send, "cube", 1)
+    got = tie(swap(send, "cube", 1), last[3])
     diag1 = split_diag(first, 1, block_of, None)
     send, y1 = call(middle_kernel, pk, [*first, *diag1, send, got], [two, one])
-    got = swap(send, "cube", 2)
+    got = tie(swap(send, "cube", 2), last[5])
     (held,) = call(meet_kernel, pk, [send, got], [two])
     got = swap(held, "cube", 1)
     diag2 = split_diag(last, 2, shared_block_of, 0)

time: 49.1 us -> 49.1 us (level)
  no operation moved by 1% of the time
where the time goes in v10:
time: 49.1 us; the launch traced here: 49 us
  waiting for transfers between devices  21.7 us (44%)
  starting transfers between devices  19.5 us (40%)
  Pallas kernels  7.55 us (15%)
    ppermute x12, starting transfers between devices, ring_step(): return lax.ppermute(block, ('cube', 'blk'), route)  15.2 us
    ppermute x12, waiting for transfers between devices, ring_step(): return lax.ppermute(block, ('cube', 'blk'), route)  12 us
    ppermute x9, waiting for transfers between devices, swap(): return lax.ppermute(block, axis, [(i, i ^ mask) for i in range(count)])  9.66 us
    pallas_call x10, Pallas kernels, call(): pl.pallas_call(functools.partial(kernel, pk), out_shape=[jax.ShapeDtypeSt...  7.55 us
    ppermute x9, starting transfers between devices, swap(): return lax.ppermute(block, axis, [(i, i ^ mask) for i in range(count)])  4.25 us
  transfers between devices with their start and end apart: 21, of which 15 were waited for; matrix products, arithmetic and copies ran while one was open for 0% of the time, Pallas kernels for 5%

profile of v10, /device:TPU:0, one launch (start us, length us, event | category | flops | bytes accessed | tf_op | source)
XLA Modules:
  0.0 49.0 jit_solution(5132792884763478396)
XLA Ops:
  0.0 1.9 %shard_map.46 = (f32[136,256]{1,0:T(8,128)}, f32[128,256]{1,0:T(8,128)}) custom-call(f32[3,1,1,32,64]{4,3,2,1,0:T(8,128)} %rhs_hbm.1, f32[2,1,1,2,16,32]{5,4,3,2,1,0:T(8,128)} %panels_hbm.1, s32[2,1,1,2,16]{4,3,2,1,0:T(2,128)} %maps_hbm.1, f32[224,256]{1,0:T(8,128)} %diag_hbm.1), custom_call_target="tpu_custom_call" | custom-call | tf_op jit(solution)/shard_map/pallas_call | solution.py:297
  1.9 3.0 %collective-permute-start.1 = (f32[136,256]{1,0:T(8,128)}, f32[136,256]{1,0:T(8,128)S(1)}, u32[]{:S(2)}, u32[]{:S(2)}) collective-permute-start(f32[136,256]{1,0:T(8,128)} %get-tuple-element.24.refs_0_), channel_id=1, source_target_pairs={{0,1},{2,0},{4,2},{6,4},{7,6},{5,7},{3,5},{1,3},{8,9},{10,8},{12,1... | collective-permute-start | bytes 417800 | tf_op jit(solution)/shard_map/ppermute | solution.py:72
  5.1 1.9 %collective-permute-start.9 = (f32[128,256]{1,0:T(8,128)}, f32[128,256]{1,0:T(8,128)S(1)}, u32[]{:S(2)}, u32[]{:S(2)}) collective-permute-start(f32[128,256]{1,0:T(8,128)} %get-tuple-element.29.refs_0_), channel_id=1, source_target_pairs={{0,1},{2,0},{4,2},{6,4},{7,6},{5,7},{3,5},{1,3},{8,9},{10,8},{12,1... | collective-permute-start | bytes 393224 | tf_op jit(solution)/shard_map/ppermute | solution.py:72
  7.1 2.6 %collective-permute-done.1.refs_2_ = f32[136,256]{1,0:T(8,128)S(1)} collective-permute-done((f32[136,256]{1,0:T(8,128)}, f32[136,256]{1,0:T(8,128)S(1)}, u32[]{:S(2)}, u32[]{:S(2)}) %collective-permute-start.1) | collective-permute-done | bytes 139296 | tf_op jit(solution)/shard_map/ppermute | solution.py:72
  9.7 2.0 %collective-permute-start.3 = (f32[136,256]{1,0:T(8,128)S(1)}, f32[136,256]{1,0:T(8,128)S(1)}, u32[]{:S(2)}, u32[]{:S(2)}) collective-permute-start(f32[136,256]{1,0:T(8,128)S(1)} %collective-permute-done.1.refs_2_), channel_id=1, source_target_pairs={{0,1},{2,0},{4,2},{6,4},{7,6},{5,7},{3,5},{1,3},{8,9},{10,8},{12,1... | collective-permute-start | bytes 417800 | tf_op jit(solution)/shard_map/ppermute | solution.py:72
  12.5 1.8 %collective-permute-done.8.refs_1_ = f32[128,256]{1,0:T(8,128)S(1)} collective-permute-done((f32[128,256]{1,0:T(8,128)}, f32[128,256]{1,0:T(8,128)S(1)}, u32[]{:S(2)}, u32[]{:S(2)}) %collective-permute-start.8) | collective-permute-done | bytes 131104 | tf_op jit(solution)/shard_map/ppermute | solution.py:72
  14.8 2.0 %collective-permute-start.5 = (f32[136,256]{1,0:T(8,128)S(1)}, f32[136,256]{1,0:T(8,128)S(1)}, u32[]{:S(2)}, u32[]{:S(2)}) collective-permute-start(f32[136,256]{1,0:T(8,128)S(1)} %collective-permute-done.3.refs_4_), channel_id=1, source_target_pairs={{0,1},{2,0},{4,2},{6,4},{7,6},{5,7},{3,5},{1,3},{8,9},{10,8},{12,1... | collective-permute-start | bytes 417800 | tf_op jit(solution)/shard_map/ppermute | solution.py:72
  16.9 2.0 %collective-permute-start.11 = (f32[256,256]{1,0:T(8,128)S(1)}, f32[256,256]{1,0:T(8,128)S(1)}, u32[]{:S(2)}, u32[]{:S(2)}) collective-permute-start(f32[256,256]{1,0:T(8,128)S(1)} %pad_maximum_fusion), channel_id=1, source_target_pairs={{0,2},{2,4},{4,6},{6,7},{7,5},{5,3},{3,1},{1,0},{8,9},{10,8},{12,1... | collective-permute-start | bytes 786440 | tf_op jit(solution)/shard_map/ppermute | solution.py:72
  19.0 2.4 %collective-permute-done.5.refs_6_ = f32[136,256]{1,0:T(8,128)S(1)} collective-permute-done((f32[136,256]{1,0:T(8,128)S(1)}, f32[136,256]{1,0:T(8,128)S(1)}, u32[]{:S(2)}, u32[]{:S(2)}) %collective-permute-start.5) | collective-permute-done | bytes 139296 | tf_op jit(solution)/shard_map/ppermute | solution.py:72
  21.9 1.6 %collective-permute-start.6 = (f32[136,256]{1,0:T(8,128)S(1)}, f32[136,256]{1,0:T(8,128)S(1)}, u32[]{:S(2)}, u32[]{:S(2)}) collective-permute-start(f32[136,256]{1,0:T(8,128)S(1)} %broadcast_select_fusion), channel_id=1, source_target_pairs={{0,2},{2,4},{4,6},{6,7},{7,5},{5,3},{3,1},{1,0},{8,9},{10,8},{12,1... | collective-permute-start | bytes 417800 | tf_op jit(solution)/shard_map/ppermute | solution.py:72
  23.5 1.2 %collective-permute-done.11 = f32[256,256]{1,0:T(8,128)S(1)} collective-permute-done((f32[256,256]{1,0:T(8,128)S(1)}, f32[256,256]{1,0:T(8,128)S(1)}, u32[]{:S(2)}, u32[]{:S(2)}) %collective-permute-start.11) | collective-permute-done | bytes 262176 | tf_op jit(solution)/shard_map/ppermute | solution.py:72
  25.3 1.6 %collective-permute-done.6.refs_7_ = f32[136,256]{1,0:T(8,128)S(1)} collective-permute-done((f32[136,256]{1,0:T(8,128)S(1)}, f32[136,256]{1,0:T(8,128)S(1)}, u32[]{:S(2)}, u32[]{:S(2)}) %collective-permute-start.6) | collective-permute-done | bytes 139296 | tf_op jit(solution)/shard_map/ppermute | solution.py:72
  29.1 0.8 %shard_map.49 = (f32[256,128]{1,0:T(8,128)S(1)}, f32[256,64]{1,0:T(8,128)S(1)}) custom-call(f32[136,256]{1,0:T(8,128)S(1)} %copy-done, f32[136,256]{1,0:T(8,128)S(1)} %collective-permute-done.refs_1_, f32[136,256]{1,0:T(8,128)S(1)} %collective-permute-done.1.refs_2_, f32[136,256]{1,0:T(8,128)S(1)} %collective-permute-done.2.refs_3_, ...), custom_call_target="tpu_custom_call" | custom-call | tf_op jit(solution)/shard_map/pallas_call | solution.py:297
  29.9 1.6 %collective-permute-start.16 = (f32[256,128]{1,0:T(8,128)S(1)}, f32[256,128]{1,0:T(8,128)S(1)}, u32[]{:S(2)}, u32[]{:S(2)}) collective-permute-start(f32[256,128]{1,0:T(8,128)S(1)} %get-tuple-element.34.mine_ref), channel_id=1, source_target_pairs={{0,16},{8,24},{16,0},{24,8},{1,17},{9,25},{17,1},{25,9},{2,18},{10... | collective-permute-start | bytes 393224 | tf_op jit(solution)/shard_map/ppermute | solution.py:53
  31.6 1.6 %collective-permute-start.15 = (f32[128,256]{1,0:T(8,128)S(1)}, f32[128,256]{1,0:T(8,128)S(1)}, u32[]{:S(2)}, u32[]{:S(2)}) collective-permute-start(f32[128,256]{1,0:T(8,128)S(1)} %get-tuple-element.44.refs_5_), channel_id=1, source_target_pairs={{0,2},{2,4},{4,6},{6,7},{7,5},{5,3},{3,1},{1,0},{8,9},{10,8},{12,1... | collective-permute-start | bytes 393224 | tf_op jit(solution)/shard_map/ppermute | solution.py:72
  33.2 2.4 %collective-permute-done.16.got_ref = f32[256,128]{1,0:T(8,128)S(1)} collective-permute-done((f32[256,128]{1,0:T(8,128)S(1)}, f32[256,128]{1,0:T(8,128)S(1)}, u32[]{:S(2)}, u32[]{:S(2)}) %collective-permute-start.16) | collective-permute-done | bytes 131104 | tf_op jit(solution)/shard_map/ppermute | solution.py:53
  35.8 0.8 %collective-permute-done.15.refs_7_ = f32[128,256]{1,0:T(8,128)S(1)} collective-permute-done((f32[128,256]{1,0:T(8,128)S(1)}, f32[128,256]{1,0:T(8,128)S(1)}, u32[]{:S(2)}, u32[]{:S(2)}) %collective-permute-start.15) | collective-permute-done | bytes 131104 | tf_op jit(solution)/shard_map/ppermute | solution.py:72
  37.1 1.3 %shard_map.52 = (f32[256,128]{1,0:T(8,128)S(1)}, f32[256,128]{1,0:T(8,128)S(1)}) custom-call(bf16[1024,256]{1,0:T(8,128)(2,1)S(1)} %get-tuple-element.32.high_ref, bf16[1024,256]{1,0:T(8,128)(2,1)S(1)} %get-tuple-element.33.low_ref, f32[256,128]{1,0:T(8,128)S(1)} %shard_map.51.mine_ref, f32[256,128]{1,0:T(8,128)S(1)} %collective-permute-done.17.got_ref), custom_call_target="tpu_custom_call" | custom-call | tf_op jit(solution)/shard_map/pallas_call | solution.py:297
  38.7 1.2 %collective-permute-done.18.got_ref = f32[256,128]{1,0:T(8,128)S(1)} collective-permute-done((f32[256,128]{1,0:T(8,128)S(1)}, f32[256,128]{1,0:T(8,128)S(1)}, u32[]{:S(2)}, u32[]{:S(2)}) %collective-permute-start.18) | collective-permute-done | bytes 131104 | tf_op jit(solution)/shard_map/ppermute | solution.py:53
  40.0 1.6 %collective-permute-start.19 = (f32[256,128]{1,0:T(8,128)S(1)}, f32[256,128]{1,0:T(8,128)S(1)}, u32[]{:S(2)}, u32[]{:S(2)}) collective-permute-start(f32[256,128]{1,0:T(8,128)S(1)} %get-tuple-element.39), channel_id=1, source_target_pairs={{0,16},{8,24},{16,0},{24,8},{1,17},{9,25},{17,1},{25,9},{2,18},{10... | collective-permute-start | bytes 393224 | tf_op jit(solution)/shard_map/ppermute | solution.py:53
  41.6 4.0 %collective-permute-done.19.refs_12_ = f32[256,128]{1,0:T(8,128)S(1)} collective-permute-done((f32[256,128]{1,0:T(8,128)S(1)}, f32[256,128]{1,0:T(8,128)S(1)}, u32[]{:S(2)}, u32[]{:S(2)}) %collective-permute-start.19) | collective-permute-done | bytes 131104 | tf_op jit(solution)/shard_map/ppermute | solution.py:53
  45.6 0.8 %shard_map.54 = (f32[256,128]{1,0:T(8,128)S(1)}, f32[256,128]{1,0:T(8,128)S(1)}, f32[32,64]{1,0:T(8,128)S(1)}) custom-call(f32[136,256]{1,0:T(8,128)S(1)} %copy-done, f32[136,256]{1,0:T(8,128)S(1)} %collective-permute-done.refs_1_, f32[136,256]{1,0:T(8,128)S(1)} %collective-permute-done.1.refs_2_, f32[136,256]{1,0:T(8,128)S(1)} %collective-permute-done.2.refs_3_, ...), custom_call_target="tpu_custom_call" | custom-call | tf_op jit(solution)/shard_map/pallas_call | solution.py:297
  46.5 1.3 %collective-permute-done.20.refs_10_ = f32[256,128]{1,0:T(8,128)S(1)} collective-permute-done((f32[256,128]{1,0:T(8,128)S(1)}, f32[256,128]{1,0:T(8,128)S(1)}, u32[]{:S(2)}, u32[]{:S(2)}) %collective-permute-start.20) | collective-permute-done | bytes 131104 | tf_op jit(solution)/shard_map/ppermute | solution.py:53
  47.8 1.1 %shard_map.55 = f32[3,32,64]{2,1,0:T(8,128)} custom-call(f32[136,256]{1,0:T(8,128)S(1)} %copy-done, f32[136,256]{1,0:T(8,128)S(1)} %collective-permute-done.refs_1_, f32[136,256]{1,0:T(8,128)S(1)} %collective-permute-done.1.refs_2_, f32[136,256]{1,0:T(8,128)S(1)} %collective-permute-done.2.refs_3_, f32[136,256]{1,0:T(8,128)S(1)} %collective-permute-done.3.refs_4_, ...), custom_call_target="tpu_custom_call" | custom-call | tf_op jit(solution)/shard_map/pallas_call | solution.py:297
  (37 shorter events, 6.3 us)
Async XLA Ops:
  1.9 7.8 %collective-permute-start.1 = (f32[136,256]{1,0:T(8,128)}, f32[136,256]{1,0:T(8,128)S(1)}, u32[]{:S(2)}, u32[]{:S(2)}) collective-permute-start(f32[136,256]{1,0:T(8,128)} %get-tuple-element.24.refs_0_), channel_id=1, source_target_pairs={{0,1},{2,0},{4,2},{6,4},{7,6},{5,7},{3,5},{1,3},{8,9},{10,8},{12,1... | collective-permute-start | bytes 417800 | tf_op jit(solution)/shard_map/ppermute | solution.py:72
  5.0 6.8 %collective-permute-start = (f32[136,256]{1,0:T(8,128)}, f32[136,256]{1,0:T(8,128)S(1)}, u32[]{:S(2)}, u32[]{:S(2)}) collective-permute-start(f32[136,256]{1,0:T(8,128)} %get-tuple-element.24.refs_0_), channel_id=1, source_target_pairs={{0,2},{2,4},{4,6},{6,7},{7,5},{5,3},{3,1},{1,0},{8,10},{10,12},{12... | collective-permute-start | bytes 417800 | tf_op jit(solution)/shard_map/ppermute | solution.py:72
  5.1 7.5 %collective-permute-start.9 = (f32[128,256]{1,0:T(8,128)}, f32[128,256]{1,0:T(8,128)S(1)}, u32[]{:S(2)}, u32[]{:S(2)}) collective-permute-start(f32[128,256]{1,0:T(8,128)} %get-tuple-element.29.refs_0_), channel_id=1, source_target_pairs={{0,1},{2,0},{4,2},{6,4},{7,6},{5,7},{3,5},{1,3},{8,9},{10,8},{12,1... | collective-permute-start | bytes 393224 | tf_op jit(solution)/shard_map/ppermute | solution.py:72
  7.0 7.3 %collective-permute-start.8 = (f32[128,256]{1,0:T(8,128)}, f32[128,256]{1,0:T(8,128)S(1)}, u32[]{:S(2)}, u32[]{:S(2)}) collective-permute-start(f32[128,256]{1,0:T(8,128)} %get-tuple-element.29.refs_0_), channel_id=1, source_target_pairs={{0,2},{2,4},{4,6},{6,7},{7,5},{5,3},{3,1},{1,0},{8,10},{10,12},{12... | collective-permute-start | bytes 393224 | tf_op jit(solution)/shard_map/ppermute | solution.py:72
  9.7 5.1 %collective-permute-start.3 = (f32[136,256]{1,0:T(8,128)S(1)}, f32[136,256]{1,0:T(8,128)S(1)}, u32[]{:S(2)}, u32[]{:S(2)}) collective-permute-start(f32[136,256]{1,0:T(8,128)S(1)} %collective-permute-done.1.refs_2_), channel_id=1, source_target_pairs={{0,1},{2,0},{4,2},{6,4},{7,6},{5,7},{3,5},{1,3},{8,9},{10,8},{12,1... | collective-permute-start | bytes 417800 | tf_op jit(solution)/shard_map/ppermute | solution.py:72
  11.7 5.1 %collective-permute-start.2 = (f32[136,256]{1,0:T(8,128)S(1)}, f32[136,256]{1,0:T(8,128)S(1)}, u32[]{:S(2)}, u32[]{:S(2)}) collective-permute-start(f32[136,256]{1,0:T(8,128)S(1)} %collective-permute-done.refs_1_), channel_id=1, source_target_pairs={{0,2},{2,4},{4,6},{6,7},{7,5},{5,3},{3,1},{1,0},{8,10},{10,12},{12... | collective-permute-start | bytes 417800 | tf_op jit(solution)/shard_map/ppermute | solution.py:72
  14.3 2.6 %collective-permute-start.10 = (f32[128,256]{1,0:T(8,128)S(1)}, f32[128,256]{1,0:T(8,128)S(1)}, u32[]{:S(2)}, u32[]{:S(2)}) collective-permute-start(f32[128,256]{1,0:T(8,128)S(1)} %get-tuple-element.48), channel_id=1, source_target_pairs={{0,8},{8,0},{16,24},{24,16},{1,9},{9,1},{17,25},{25,17},{2,10},{10... | collective-permute-start | bytes 393224 | tf_op jit(solution)/shard_map/ppermute | solution.py:53
  14.8 6.5 %collective-permute-start.5 = (f32[136,256]{1,0:T(8,128)S(1)}, f32[136,256]{1,0:T(8,128)S(1)}, u32[]{:S(2)}, u32[]{:S(2)}) collective-permute-start(f32[136,256]{1,0:T(8,128)S(1)} %collective-permute-done.3.refs_4_), channel_id=1, source_target_pairs={{0,1},{2,0},{4,2},{6,4},{7,6},{5,7},{3,5},{1,3},{8,9},{10,8},{12,1... | collective-permute-start | bytes 417800 | tf_op jit(solution)/shard_map/ppermute | solution.py:72
  16.8 5.1 %collective-permute-start.4 = (f32[136,256]{1,0:T(8,128)S(1)}, f32[136,256]{1,0:T(8,128)S(1)}, u32[]{:S(2)}, u32[]{:S(2)}) collective-permute-start(f32[136,256]{1,0:T(8,128)S(1)} %collective-permute-done.2.refs_3_), channel_id=1, source_target_pairs={{0,2},{2,4},{4,6},{6,7},{7,5},{5,3},{3,1},{1,0},{8,10},{10,12},{12... | collective-permute-start | bytes 417800 | tf_op jit(solution)/shard_map/ppermute | solution.py:72
  16.9 10.0 %copy-start = (f32[136,256]{1,0:T(8,128)S(1)}, f32[136,256]{1,0:T(8,128)}, u32[]{:S(2)}) copy-start(f32[136,256]{1,0:T(8,128)} %get-tuple-element.24.refs_0_) | copy-start | bytes 417796
  16.9 7.7 %collective-permute-start.11 = (f32[256,256]{1,0:T(8,128)S(1)}, f32[256,256]{1,0:T(8,128)S(1)}, u32[]{:S(2)}, u32[]{:S(2)}) collective-permute-start(f32[256,256]{1,0:T(8,128)S(1)} %pad_maximum_fusion), channel_id=1, source_target_pairs={{0,2},{2,4},{4,6},{6,7},{7,5},{5,3},{3,1},{1,0},{8,9},{10,8},{12,1... | collective-permute-start | bytes 786440 | tf_op jit(solution)/shard_map/ppermute | solution.py:72
  21.9 5.1 %collective-permute-start.6 = (f32[136,256]{1,0:T(8,128)S(1)}, f32[136,256]{1,0:T(8,128)S(1)}, u32[]{:S(2)}, u32[]{:S(2)}) collective-permute-start(f32[136,256]{1,0:T(8,128)S(1)} %broadcast_select_fusion), channel_id=1, source_target_pairs={{0,2},{2,4},{4,6},{6,7},{7,5},{5,3},{3,1},{1,0},{8,9},{10,8},{12,1... | collective-permute-start | bytes 417800 | tf_op jit(solution)/shard_map/ppermute | solution.py:72
  24.6 6.9 %collective-permute-start.13 = (f32[256,256]{1,0:T(8,128)S(1)}, f32[256,256]{1,0:T(8,128)S(1)}, u32[]{:S(2)}, u32[]{:S(2)}) collective-permute-start(f32[256,256]{1,0:T(8,128)S(1)} %collective-permute-done.11), channel_id=1, source_target_pairs={{0,2},{2,4},{4,6},{6,7},{7,5},{5,3},{3,1},{1,0},{8,9},{10,8},{12,1... | collective-permute-start | bytes 786440 | tf_op jit(solution)/shard_map/ppermute | solution.py:72
  27.7 1.4 %collective-permute-start.7 = (f32[256,128]{1,0:T(8,128)S(1)}, f32[256,128]{1,0:T(8,128)S(1)}, u32[]{:S(2)}, u32[]{:S(2)}) collective-permute-start(f32[256,128]{1,0:T(8,128)S(1)} %get-tuple-element.28.refs_10_), channel_id=1, source_target_pairs={{0,8},{8,0},{16,24},{24,16},{1,9},{9,1},{17,25},{25,17},{2,10},{10... | collective-permute-start | bytes 393224 | tf_op jit(solution)/shard_map/ppermute | solution.py:53
  27.8 8.0 %collective-permute-start.12 = (f32[128,256]{1,0:T(8,128)S(1)}, f32[128,256]{1,0:T(8,128)S(1)}, u32[]{:S(2)}, u32[]{:S(2)}) collective-permute-start(f32[128,256]{1,0:T(8,128)S(1)} %get-tuple-element.45), channel_id=1, source_target_pairs={{0,8},{8,0},{16,24},{24,16},{1,9},{9,1},{17,25},{25,17},{2,10},{10... | collective-permute-start | bytes 393224 | tf_op jit(solution)/shard_map/ppermute | solution.py:53
  29.9 5.6 %collective-permute-start.16 = (f32[256,128]{1,0:T(8,128)S(1)}, f32[256,128]{1,0:T(8,128)S(1)}, u32[]{:S(2)}, u32[]{:S(2)}) collective-permute-start(f32[256,128]{1,0:T(8,128)S(1)} %get-tuple-element.34.mine_ref), channel_id=1, source_target_pairs={{0,16},{8,24},{16,0},{24,8},{1,17},{9,25},{17,1},{25,9},{2,18},{10... | collective-permute-start | bytes 393224 | tf_op jit(solution)/shard_map/ppermute | solution.py:53
  31.5 4.3 %collective-permute-start.14 = (f32[128,256]{1,0:T(8,128)S(1)}, f32[128,256]{1,0:T(8,128)S(1)}, u32[]{:S(2)}, u32[]{:S(2)}) collective-permute-start(f32[128,256]{1,0:T(8,128)S(1)} %get-tuple-element.43), channel_id=1, source_target_pairs={{0,8},{8,0},{16,24},{24,16},{1,9},{9,1},{17,25},{25,17},{2,10},{10... | collective-permute-start | bytes 393224 | tf_op jit(solution)/shard_map/ppermute | solution.py:53
  31.6 5.0 %copy-start.1 = (f32[128,256]{1,0:T(8,128)S(1)}, f32[128,256]{1,0:T(8,128)}, u32[]{:S(2)}) copy-start(f32[128,256]{1,0:T(8,128)} %get-tuple-element.29.refs_0_) | copy-start | bytes 393220
  31.6 5.0 %collective-permute-start.15 = (f32[128,256]{1,0:T(8,128)S(1)}, f32[128,256]{1,0:T(8,128)S(1)}, u32[]{:S(2)}, u32[]{:S(2)}) collective-permute-start(f32[128,256]{1,0:T(8,128)S(1)} %get-tuple-element.44.refs_5_), channel_id=1, source_target_pairs={{0,2},{2,4},{4,6},{6,7},{7,5},{5,3},{3,1},{1,0},{8,9},{10,8},{12,1... | collective-permute-start | bytes 393224 | tf_op jit(solution)/shard_map/ppermute | solution.py:72
  35.7 1.4 %collective-permute-start.17 = (f32[256,128]{1,0:T(8,128)S(1)}, f32[256,128]{1,0:T(8,128)S(1)}, u32[]{:S(2)}, u32[]{:S(2)}) collective-permute-start(f32[256,128]{1,0:T(8,128)S(1)} %shard_map.51.mine_ref), channel_id=1, source_target_pairs={{0,8},{8,0},{16,24},{24,16},{1,9},{9,1},{17,25},{25,17},{2,10},{10... | collective-permute-start | bytes 393224 | tf_op jit(solution)/shard_map/ppermute | solution.py:53
  38.5 1.4 %collective-permute-start.18 = (f32[256,128]{1,0:T(8,128)S(1)}, f32[256,128]{1,0:T(8,128)S(1)}, u32[]{:S(2)}, u32[]{:S(2)}) collective-permute-start(f32[256,128]{1,0:T(8,128)S(1)} %get-tuple-element.37), channel_id=1, source_target_pairs={{0,8},{8,0},{16,24},{24,16},{1,9},{9,1},{17,25},{25,17},{2,10},{10... | collective-permute-start | bytes 393224 | tf_op jit(solution)/shard_map/ppermute | solution.py:53
  40.0 5.6 %collective-permute-start.19 = (f32[256,128]{1,0:T(8,128)S(1)}, f32[256,128]{1,0:T(8,128)S(1)}, u32[]{:S(2)}, u32[]{:S(2)}) collective-permute-start(f32[256,128]{1,0:T(8,128)S(1)} %get-tuple-element.39), channel_id=1, source_target_pairs={{0,16},{8,24},{16,0},{24,8},{1,17},{9,25},{17,1},{25,9},{2,18},{10... | collective-permute-start | bytes 393224 | tf_op jit(solution)/shard_map/ppermute | solution.py:53
  46.4 1.4 %collective-permute-start.20 = (f32[256,128]{1,0:T(8,128)S(1)}, f32[256,128]{1,0:T(8,128)S(1)}, u32[]{:S(2)}, u32[]{:S(2)}) collective-permute-start(f32[256,128]{1,0:T(8,128)S(1)} %get-tuple-element.41), channel_id=1, source_target_pairs={{0,8},{8,0},{16,24},{24,16},{1,9},{9,1},{17,25},{25,17},{2,10},{10... | collective-permute-start | bytes 393224 | tf_op jit(solution)/shard_map/ppermute | solution.py:53
